TPU v7x, 32 devices: a whole 2x2x4 slice. The times are simulated.
32 devices in a mesh: row: 8 (over z, y), col: 4 (over x, core).
Axes of the slice: x: 2, y: 2, z: 4, core: 2. Of those that a mesh axis runs over, the one named last changes fastest.
Arguments:
- features: bfloat16 [2048, 512], P(('row', 'col')), may hold values from -6 to 6
- w_first: bfloat16 [512, 512], replicated, may hold values from -0.25 to 0.25
- w_second: bfloat16 [512, 512], replicated, may hold values from -0.25 to 0.25
- block_index: int32 [8, 4, 8], P('row', 'col'), may hold values from 0 to 7, as said below
- block_count: int32 [8, 4], P('row', 'col'), may hold values from 0 to 2, as said below
- block_values: bfloat16 [8, 4, 8, 128, 128], P('row', 'col'), may hold values from -0.4375 to 0.4375
- cotangent: bfloat16 [2048, 512], P(('row', 'col')), may hold values from -0.125 to 0.125
Outputs:
- out_second: bfloat16 [2048, 512], P(('row', 'col'))
- grad_first: float32 [512, 512], replicated
- grad_second: float32 [512, 512], replicated
Inputs may be any that keep to these rules, and one draw needn't show every extreme that they name: `block_index`: in each tile the 8 slots name every block position p = r * 4 + c (block row r, block column c of the tile) once, in some order; the first block_count slots are the tile's nonzero blocks and the others are unused. `block_count`: nonzero blocks of each tile; in every draw some tile has exactly 2.
All inputs are finite; a program needn't handle non-finite values.
Results may differ from a plain program's by a relative error of at most 0.0061.
Values may be sent and summed in bfloat16 or wider, within the bound.
No kernel may reach another device: no remote copies, remote signals or barrier semaphores. Data moves between devices by JAX's collectives and lax.ppermute only.
A program may use at most 64 MiB of HBM per device.

v0:
```python
import math

import jax
import jax.numpy as jnp
from jax import lax
from jax.sharding import PartitionSpec as P


def activate(v):
    return jax.nn.gelu(v, approximate=True)


def combine(tile_values, slot_index, slot_count, full_panel, flip):
    slots = slot_index.shape[0]
    block_size = tile_values.shape[-1]
    feat_width = full_panel.shape[1]
    in_blocks = full_panel.shape[0] // block_size
    if flip:
        col_blocks = slots // in_blocks
        out_blocks = col_blocks
    else:
        col_blocks = in_blocks
        out_blocks = slots // in_blocks
    group_size = math.gcd(slots, 32)
    panel_blocks = full_panel.reshape(in_blocks, block_size, feat_width)
    targets = jnp.arange(out_blocks, dtype=jnp.int32)
    offsets = jnp.arange(group_size, dtype=jnp.int32)

    def add_group(group_no, total):
        first_slot = group_no * group_size
        slot_ids = lax.dynamic_slice_in_dim(slot_index, first_slot, group_size, 0)
        group_values = lax.dynamic_slice_in_dim(tile_values, first_slot, group_size, 0)
        block_row = slot_ids // col_blocks
        block_col = slot_ids % col_blocks
        if flip:
            picked = panel_blocks[block_row]
            product = jnp.einsum(
                "sab,saf->sbf", group_values, picked, preferred_element_type=jnp.float32
            )
            target = block_col
        else:
            picked = panel_blocks[block_col]
            product = jnp.einsum(
                "sab,sbf->saf", group_values, picked, preferred_element_type=jnp.float32
            )
            target = block_row
        is_live = first_slot + offsets < slot_count
        onehot = ((target[None, :] == targets[:, None]) & is_live[None, :]).astype(jnp.float32)
        return total + jnp.einsum("os,saf->oaf", onehot, product, precision=lax.Precision.HIGHEST)

    groups = (slot_count + group_size - 1) // group_size
    total = lax.fori_loop(
        0, groups, add_group, jnp.zeros((out_blocks, block_size, feat_width), jnp.float32)
    )
    return total.reshape(out_blocks * block_size, feat_width)


def spread_rows(layer_input, tile_values, slot_index, slot_count):
    full_panel = lax.all_gather(layer_input, "row", axis=0, tiled=True)
    partial_value = combine(tile_values, slot_index, slot_count, full_panel, False)
    return lax.psum_scatter(partial_value, "col", scatter_dimension=0, tiled=True)


def spread_cols(layer_input, tile_values, slot_index, slot_count):
    full_panel = lax.all_gather(layer_input, "col", axis=0, tiled=True)
    partial_value = combine(tile_values, slot_index, slot_count, full_panel, True)
    return lax.psum_scatter(partial_value, "row", scatter_dimension=0, tiled=True)


def local(features, w_first, w_second, block_index, block_count, block_values, cotangent):
    slot_index = block_index[0, 0]
    slot_count = block_count[0, 0]
    tile_values = block_values[0, 0]
    feat_width = features.shape[1]
    first_linear = jnp.dot(features, w_first, preferred_element_type=jnp.float32).astype(
        jnp.bfloat16
    )
    joined = jnp.concatenate([first_linear, cotangent], axis=1)
    summed = spread_cols(joined, tile_values, slot_index, slot_count)
    first_sum = summed[:, :feat_width]
    back_second = summed[:, feat_width:].astype(jnp.bfloat16)
    first_value, act_back = jax.vjp(activate, first_sum)
    first_active = first_value.astype(jnp.bfloat16)
    second_linear = jnp.dot(first_active, w_second, preferred_element_type=jnp.float32).astype(
        jnp.bfloat16
    )
    out_second = spread_rows(second_linear, tile_values, slot_index, slot_count).astype(
        jnp.bfloat16
    )
    second_terms = jnp.einsum(
        "nf,ng->fg", first_active, back_second, preferred_element_type=jnp.float32
    )
    back_act = jnp.einsum("ng,fg->nf", back_second, w_second, preferred_element_type=jnp.float32)
    back_first = act_back(back_act)[0].astype(jnp.bfloat16)
    back_linear = spread_rows(back_first, tile_values, slot_index, slot_count).astype(jnp.bfloat16)
    first_terms = jnp.einsum("nf,ng->fg", features, back_linear, preferred_element_type=jnp.float32)
    grad_first, grad_second = lax.psum((first_terms, second_terms), ("row", "col"))
    return (out_second, grad_first, grad_second)


def solution(mesh):
    return jax.shard_map(
        local,
        mesh=mesh,
        in_specs=(
            P(("row", "col"), None),
            P(),
            P(),
            P("row", "col", None),
            P("row", "col"),
            P("row", "col", None, None, None),
            P(("row", "col"), None),
        ),
        out_specs=(P(("row", "col"), None), P(), P()),
        check_vma=False,
    )
```

profile of v0, /device:TPU:0, one launch (start us, length us, event | category | flops | bytes accessed | tf_op | source)
XLA Modules:
  0.0 368.6 jit_solution(17383468329062296562)
XLA Ops:
  7.2 0.0 copy-start
  7.2 0.0 copy-start.6
  7.2 0.0 copy-start.3
  7.2 0.0 reduce-scatter.4.cloned.1.call-start
  8.0 0.7 sign_bitcast_fusion
  8.6 0.7 bitcast_negate_fusion
  9.3 1.3 convolution_convert_fusion.1
  10.6 0.9 pad_maximum_fusion
  11.4 8.6 %all_gather.9 = bf16[256,1024]{1,0:T(8,128)(2,1)S(1)} all-gather(bf16[64,1024]{1,0:T(8,128)(2,1)S(1)} %pad_maximum_fusion), channel_id=1, replica_groups=mesh['row'=8,'col'=4] {'col'}, dimensions={0}, use_global_device_ids=true | all-gather | bytes 655360 | tf_op jit(solution)/shard_map/all_gather | solution.py:65
  20.0 1.9 broadcast_in_dim.2
  21.9 0.0 copy-done.6
  21.9 0.0 copy-done.3
  21.9 4.1 %copy.13 = f32[4,128,1024]{2,1,0:T(8,128)} copy(f32[4,128,1024]{2,0,1:T(4,128)} %get-tuple-element.648) | data formatting | bytes 4194304 | tf_op jit(solution)/shard_map/while | solution.py:52
  26.1 0.0 reduce-scatter.4.cloned.1.call-update
  26.1 0.0 reduce-scatter.8.cloned.1.call-start
  26.1 85.4 %reduce-scatter.4.cloned.1.call-done = f32[64,1024]{1,0:T(8,128)} async-done(((f32[512,1024]{1,0:T(8,128)}), f32[64,1024]{1,0:T(8,128)}) %reduce-scatter.4.cloned.1.call-update) | async-done | bytes 262160 | tf_op jit(solution)/shard_map/reduce_scatter | solution.py:67
  111.6 0.0 copy-done
  111.6 1.3 fusion.61
  112.8 31.6 %all_gather.11 = bf16[512,512]{1,0:T(8,128)(2,1)S(1)} all-gather(bf16[64,512]{1,0:T(8,128)(2,1)S(1)} %fusion.61), channel_id=1, replica_groups=mesh['row'=8,'col'=4] {'row'}, dimensions={0}, use_global_device_ids=true | all-gather | bytes 589824 | tf_op jit(solution)/shard_map/all_gather | solution.py:59
  144.4 0.9 broadcast.533.clone.1
  145.4 1.9 copy.15
  147.3 0.0 reduce-scatter.8.cloned.1.call-update
  147.3 0.0 reduce-scatter.6.cloned.1.call-start
  147.4 1.1 convolution_convert_fusion
  148.5 32.6 %all_gather.10 = bf16[512,512]{1,0:T(8,128)(2,1)S(1)} all-gather(bf16[64,512]{1,0:T(8,128)(2,1)S(1)} %convolution_convert_fusion), channel_id=1, replica_groups=mesh['row'=8,'col'=4] {'row'}, dimensions={0}, use_global_device_ids=true | all-gather | bytes 589824 | tf_op jit(solution)/shard_map/all_gather | solution.py:59
  181.1 0.9 broadcast.533.clone
  182.1 0.0 copy-start.5
  182.1 2.0 copy.14
  184.0 0.0 reduce-scatter.6.cloned.1.call-update
  184.1 0.0 all-reduce.3.cloned.1.call-start
  184.1 2.3 fusion.64
  186.4 0.0 reduce-scatter.8.cloned.1.call-done
  186.4 0.0 copy-done.5
  186.4 2.2 convolution_bitcast_fusion
  188.6 0.0 all-reduce.3.cloned.1.call-update
  188.6 29.9 %reduce-scatter.6.cloned.1.call-done = f32[64,512]{1,0:T(8,128)} async-done(((f32[256,512]{1,0:T(8,128)}), f32[64,512]{1,0:T(8,128)}) %reduce-scatter.6.cloned.1.call-update) | async-done | bytes 131088 | tf_op jit(solution)/shard_map/reduce_scatter | solution.py:61
  218.5 1.5 convert_element_type.25
  220.0 138.5 %all-reduce.3.cloned.1.call-done = (f32[512,512]{0,1:T(8,128)}, f32[512,512]{1,0:T(8,128)}) async-done(((f32[512,512]{0,1:T(8,128)}, f32[512,512]{1,0:T(8,128)}), (f32[512,512]{0,1:T(8,128)}, f32[512,512]{1,0:T(8,128)})) %all-reduce.3.cloned.1.call-update) | async-done | bytes 2097168 | tf_op jit(solution)/shard_map/psum | solution.py:97
  358.5 0.0 copy-start.4
  358.5 2.6 copy.16
  361.1 0.0 copy-done.4
  361.1 1.0 copy.48
  (3 shorter events, 0.0 us)
Async XLA Ops:
  7.2 104.4 %copy-start = (bf16[512,512]{1,0:T(8,128)(2,1)S(1)}, bf16[512,512]{1,0:T(8,128)(2,1)}, u32[]{:S(2)}) copy-start(bf16[512,512]{1,0:T(8,128)(2,1)} %param.15) | copy-start | bytes 1572868
  7.2 14.8 %copy-start.6 = (s32[1,1,8]{2,1,0:T(1,128)S(1)}, s32[1,1,8]{2,1,0:T(1,128)}, u32[]{:S(2)}) copy-start(s32[1,1,8]{2,1,0:T(1,128)} %param.16) | copy-start | bytes 100
  7.2 14.7 %copy-start.3 = (bf16[1,1,8,128,128]{4,3,2,1,0:T(8,128)(2,1)S(1)}, bf16[1,1,8,128,128]{4,3,2,1,0:T(8,128)(2,1)}, u32[]{:S(2)}) copy-start(bf16[1,1,8,128,128]{4,3,2,1,0:T(8,128)(2,1)} %param.18) | copy-start | bytes 786436
  7.2 104.3 %reduce-scatter.4.cloned.1.call-start = ((), (), s32[]{:S(2)}) async-start(), calls=%async_computation.3 | async-start | bytes 2359296 | tf_op jit(solution)/shard_map/reduce_scatter | solution.py:67
  26.1 160.3 %reduce-scatter.8.cloned.1.call-start = ((), (), s32[]{:S(2)}) async-start(), calls=%async_computation.5 | async-start | bytes 655360 | tf_op jit(solution)/shard_map/reduce_scatter | solution.py:61
  147.3 71.1 %reduce-scatter.6.cloned.1.call-start = ((), (), s32[]{:S(2)}) async-start(), calls=%async_computation.4 | async-start | bytes 655360 | tf_op jit(solution)/shard_map/reduce_scatter | solution.py:61
  182.1 4.3 %copy-start.5 = (bf16[64,512]{1,0:T(8,128)(2,1)S(1)}, bf16[64,512]{1,0:T(8,128)(2,1)}, u32[]{:S(2)}) copy-start(bf16[64,512]{1,0:T(8,128)(2,1)} %param.13) | copy-start | bytes 196612
  184.1 174.4 %all-reduce.3.cloned.1.call-start = ((), (), s32[]{:S(2)}) async-start(), calls=%async_computation.6 | async-start | bytes 4194304 | tf_op jit(solution)/shard_map/psum | solution.py:97
  358.5 2.6 copy-start.4
Sparse Core Ops, SparseCore 0:
  26.2 85.2 reduce-scatter.3
  147.5 27.1 reduce-scatter.7
  184.2 34.2 reduce-scatter.5
  224.4 133.9 all-reduce.2
where the time goes:
time: 370 us; the launch traced here: 369 us
  waiting for transfers between devices  254 us (69%)
  blocking collectives  72.8 us (20%)
  local copies, waits for them, and re-layouts  15.4 us (4%)
  between operations  14.5 us (4%)
  matrix products  8.13 us (2%)
  other arithmetic  3.71 us (1%)
    psum x1, waiting for transfers between devices, local(): lax.psum((first_terms, second_terms), ('row', 'col'))  138 us
    reduce_scatter x1, waiting for transfers between devices, spread_cols(): lax.psum_scatter(partial_value, 'row', scatter_dimension=0, tiled=True)  85.4 us
    all_gather x2, blocking collectives, spread_rows(): full_panel = lax.all_gather(layer_input, 'row', axis=0, tiled=True)  64.2 us
    reduce_scatter x2, waiting for transfers between devices, spread_rows(): lax.psum_scatter(partial_value, 'col', scatter_dimension=0, tiled=True)  29.9 us
    all_gather x1, blocking collectives, spread_cols(): full_panel = lax.all_gather(layer_input, 'col', axis=0, tiled=True)  8.62 us
    while x3, local copies, waits for them, and re-layouts, combine(): lax.fori_loop(0, groups, add_group, jnp.zeros((out_blocks, block_size, fe...  8.06 us
  transfers between devices with their start and end apart: 4, of which 3 were waited for; matrix products, arithmetic and copies ran while one was open for 3% of the time, Pallas kernels for 0%

commit v1 on v0

--- a/solution.py
+++ b/solution.py
@@ -1,9 +1,17 @@
+import functools
 import math
 
 import jax
 import jax.numpy as jnp
 from jax import lax
+from jax.experimental import pallas as pl
+from jax.experimental.pallas import tpu as pltpu
 from jax.sharding import PartitionSpec as P
+
+AXES = ("row", "col")
+GELU_C = 0.7978845608028654
+GELU_A = 0.044715
+REPLICATE_BYTES = 8 * 1024 * 1024
 
 
 def activate(v):
@@ -67,7 +75,7 @@
     return lax.psum_scatter(partial_value, "row", scatter_dimension=0, tiled=True)
 
 
-def local(features, w_first, w_second, block_index, block_count, block_values, cotangent):
+def tiled_local(features, w_first, w_second, block_index, block_count, block_values, cotangent):
     slot_index = block_index[0, 0]
     slot_count = block_count[0, 0]
     tile_values = block_values[0, 0]
@@ -98,9 +106,262 @@
     return (out_second, grad_first, grad_second)
 
 
+class Sizes:
+    def __init__(self, mesh, features, block_values):
+        self.n_row, self.n_col = mesh.shape["row"], mesh.shape["col"]
+        self.n_dev = self.n_row * self.n_col
+        self.rows, self.width = features.shape[0] // self.n_dev, features.shape[1]
+        self.slots, self.block = block_values.shape[2], block_values.shape[-1]
+        self.live = self.slots // 4
+        self.nodes = features.shape[0]
+        self.blk_rows = self.nodes // self.n_row // self.block
+        self.blk_cols = self.nodes // self.n_col // self.block
+        self.chunks = self.width // self.block
+        self.part = self.chunks * self.rows
+        self.at_cot = self.part
+        self.at_val = 2 * self.part
+        self.at_info = self.at_val + self.live * self.block
+        self.payload = self.at_info + 16
+        self.n_blocks = self.nodes // self.block
+
+    def replicates(self):
+        whole = self.n_dev * self.payload * self.block * 2
+        return (
+            whole <= REPLICATE_BYTES
+            and self.n_col == 4
+            and self.n_row % 2 == 0
+            and 2 * self.rows == self.block
+            and self.blk_rows == 2
+            and self.n_blocks % 2 == 0
+        )
+
+
+def pack_kernel(sz, index_ref, count_ref, feat_ref, cot_ref, val_ref, out_ref):
+    for k in range(sz.chunks):
+        lanes = pl.ds(k * sz.block, sz.block)
+        out_ref[pl.ds(k * sz.rows, sz.rows), :] = feat_ref[:, lanes]
+        out_ref[pl.ds(sz.at_cot + k * sz.rows, sz.rows), :] = cot_ref[:, lanes]
+    for s in range(sz.live):
+        out_ref[pl.ds(sz.at_val + s * sz.block, sz.block), :] = val_ref[0, 0, s]
+    lane = lax.broadcasted_iota(jnp.int32, (16, sz.block), 1)
+    info = jnp.where(lane == 0, count_ref[0, 0], 0)
+    for s in range(sz.live):
+        info = jnp.where(lane == s + 1, index_ref[0, 0, s], info)
+    out_ref[pl.ds(sz.at_info, 16), :] = info.astype(jnp.float32).astype(jnp.bfloat16)
+
+
+def pack(sz, features, block_index, block_count, block_values, cotangent):
+    vmem = pl.BlockSpec(memory_space=pltpu.VMEM)
+    smem = pl.BlockSpec(memory_space=pltpu.SMEM)
+    return pl.pallas_call(
+        functools.partial(pack_kernel, sz),
+        grid=(1,),
+        out_shape=jax.ShapeDtypeStruct((sz.payload, sz.block), jnp.bfloat16),
+        in_specs=[
+            smem,
+            smem,
+            pl.BlockSpec((sz.rows, sz.width), lambda i: (0, 0)),
+            pl.BlockSpec((sz.rows, sz.width), lambda i: (0, 0)),
+            pl.BlockSpec((1, 1, sz.live, sz.block, sz.block), lambda i: (0, 0, 0, 0, 0)),
+        ],
+        out_specs=pl.BlockSpec((sz.payload, sz.block), lambda i: (0, 0)),
+    )(block_index, block_count, features, cotangent, block_values)
+
+
+def gather_parts(sz, payload):
+    n_z = sz.n_row // 2
+
+    def send(value, to):
+        pairs = []
+        for z in range(n_z):
+            for y in range(2):
+                for x in range(2):
+                    for c in range(2):
+                        z2, y2, x2, c2 = to(z, y, x, c)
+                        src = (z * 2 + y) * 4 + x * 2 + c
+                        pairs.append((src, (z2 * 2 + y2) * 4 + x2 * 2 + c2))
+        return lax.ppermute(value, AXES, pairs)
+
+    def first_way(z, y, x, c):
+        return (z, y, 1 - x, c) if c == 0 else (z, 1 - y, x, c)
+
+    def second_way(z, y, x, c):
+        return (z, 1 - y, x, c) if c == 0 else (z, y, 1 - x, c)
+
+    def sibling(z, y, x, c):
+        return (z, y, x, 1 - c)
+
+    shifts = sorted(range(n_z), key=lambda d: min(d, n_z - d))
+    parts = []
+    for d in shifts:
+        own = payload
+        if d:
+            own = send(payload, lambda z, y, x, c: ((z + d) % n_z, y, x, c))
+        near = jnp.concatenate([own, send(own, first_way)], axis=0)
+        far = send(near, second_way)
+        parts.append((d, near, far, send(near, sibling), send(far, sibling)))
+    return parts
+
+
+def main_kernel(sz, shifts, *refs):
+    n_parts = 4 * len(shifts)
+    part_refs = refs[:n_parts]
+    w1_ref, w2_ref, out_ref, gf_ref, gs_ref = refs[n_parts : n_parts + 5]
+    buf, info_v, info_s, fct, gb, act, w1t, rows_out, sem, info_sem = refs[n_parts + 5 :]
+    n_z = sz.n_row // 2
+    block, width = sz.block, sz.width
+    row, col = lax.axis_index("row"), lax.axis_index("col")
+    z, y, x, c = row // 2, row % 2, col // 2, col % 2
+
+    copies = []
+    for n, d in enumerate(shifts):
+        for q in range(4):
+            for k in range(2):
+                core = c if q < 2 else 1 - c
+                first, second = k, q % 2
+                dx = jnp.where(core == 0, first, second)
+                dy = jnp.where(core == 0, second, first)
+                from_z = lax.rem(z + n_z - d, n_z)
+                from_y, from_x = lax.rem(y + dy, 2), lax.rem(x + dx, 2)
+                dev = (from_z * 2 + from_y) * 4 + from_x * 2 + core
+                copy = pltpu.make_async_copy(
+                    part_refs[4 * n + q].at[pl.ds(k * sz.payload, sz.payload)],
+                    buf.at[dev],
+                    sem.at[(4 * n + q) * 2 + k],
+                )
+                copy.start()
+                copies.append(copy)
+
+    w1t[...] = jnp.transpose(w1_ref[...].astype(jnp.float32)).astype(jnp.bfloat16)
+    gb[...] = jnp.zeros_like(gb)
+    for copy in copies:
+        copy.wait()
+
+    for t in range(sz.n_dev):
+        line = buf[t, pl.ds(sz.at_info, 16), :]
+        info_v[pl.ds(t * 8, 8), :] = line.astype(jnp.float32).astype(jnp.int32)[0:8]
+    info_copy = pltpu.make_async_copy(info_v, info_s, info_sem)
+    info_copy.start()
+    info_copy.wait()
+
+    def tile_blocks(t):
+        count = info_s[t * 8, 0]
+        for s in range(sz.live):
+            p = info_s[t * 8, s + 1]
+            yield s < count, p // sz.blk_cols, lax.rem(p, sz.blk_cols), s
+
+    def values(t, s):
+        return buf[t, pl.ds(sz.at_val + s * block, block), :]
+
+    def tile_row(i, carry):
+        for r in range(sz.blk_rows):
+            t0 = i * sz.n_col + 2 * r
+            for k in range(2 * sz.chunks):
+                at = pl.ds(k * sz.rows, sz.rows)
+                piece = jnp.concatenate([buf[t0, at, :], buf[t0 + 1, at, :]], axis=0)
+                fct[r, pl.ds(k * block, block), :] = jnp.transpose(piece)
+        for j in range(sz.n_col):
+            t = i * sz.n_col + j
+            for live, r, cb, s in tile_blocks(t):
+
+                @pl.when(live)
+                def _():
+                    gb[j * sz.blk_cols + cb] += jnp.dot(
+                        fct[r], values(t, s), preferred_element_type=jnp.float32
+                    )
+
+        return carry
+
+    lax.fori_loop(0, sz.n_row, tile_row, 0)
+
+    def chunk(n, carry):
+        both = jnp.concatenate(
+            [gb[2 * n].astype(jnp.bfloat16), gb[2 * n + 1].astype(jnp.bfloat16)], axis=1
+        )
+        g, b = both[:width], both[width:]
+        v = jnp.dot(w1t[...], g, preferred_element_type=jnp.float32)
+        sq = v * v
+        t = jnp.tanh(GELU_C * (v + GELU_A * sq * v))
+        half = 0.5 * (1.0 + t)
+        a = (v * half).astype(jnp.bfloat16)
+        slope = half + 0.5 * v * (1.0 - t * t) * (GELU_C * (1.0 + 3.0 * GELU_A * sq))
+        act[2 * n] = a[:, :block]
+        act[2 * n + 1] = a[:, block:]
+        back = jnp.dot(w2_ref[...], b, preferred_element_type=jnp.float32)
+        bf = (back * slope).astype(jnp.bfloat16)
+        nt = (((1,), (1,)), ((), ()))
+        gs = lax.dot_general(a, b, nt, preferred_element_type=jnp.float32)
+        gf = lax.dot_general(g, bf, nt, preferred_element_type=jnp.float32)
+
+        @pl.when(n == 0)
+        def _():
+            gs_ref[...] = gs
+            gf_ref[...] = gf
+
+        @pl.when(n > 0)
+        def _():
+            gs_ref[...] += gs
+            gf_ref[...] += gf
+
+        return carry
+
+    lax.fori_loop(0, sz.n_blocks // 2, chunk, 0)
+
+    rows_out[...] = jnp.zeros_like(rows_out)
+    for j in range(sz.n_col):
+        t = row * sz.n_col + j
+        for live, r, cb, s in tile_blocks(t):
+
+            @pl.when(live & (r == x))
+            def _():
+                rows_out[...] += lax.dot_general(
+                    act[j * sz.blk_cols + cb],
+                    values(t, s),
+                    (((1,), (1,)), ((), ())),
+                    preferred_element_type=jnp.float32,
+                )
+
+    h = jnp.transpose(rows_out[...])
+    high = h.astype(jnp.bfloat16)
+    low = (h - high.astype(jnp.float32)).astype(jnp.bfloat16)
+    out = jnp.dot(high, w2_ref[...], preferred_element_type=jnp.float32)
+    out += jnp.dot(low, w2_ref[...], preferred_element_type=jnp.float32)
+    out = jnp.where(c == 0, out[: sz.rows], out[sz.rows :])
+    out_ref[...] = out.astype(jnp.bfloat16)
+
+
+def replicated_local(sz, features, w_first, w_second, block_index, block_count, block_values, cotangent):
+    payload = pack(sz, features, block_index, block_count, block_values, cotangent)
+    parts = gather_parts(sz, payload)
+    shifts = [p[0] for p in parts]
+    arrays = [a for p in parts for a in p[1:]]
+    vmem = pl.BlockSpec(memory_space=pltpu.VMEM)
+    grad = jax.ShapeDtypeStruct((sz.width, sz.width), jnp.float32)
+    return tuple(
+        pl.pallas_call(
+            functools.partial(main_kernel, sz, shifts),
+            out_shape=(jax.ShapeDtypeStruct((sz.rows, sz.width), jnp.bfloat16), grad, grad),
+            in_specs=[pl.BlockSpec(memory_space=pl.ANY)] * len(arrays) + [vmem] * 2,
+            out_specs=(vmem, vmem, vmem),
+            scratch_shapes=[
+                pltpu.VMEM((sz.n_dev, sz.payload, sz.block), jnp.bfloat16),
+                pltpu.VMEM((sz.n_dev * 8, sz.block), jnp.int32),
+                pltpu.SMEM((sz.n_dev * 8, sz.block), jnp.int32),
+                pltpu.VMEM((sz.blk_rows, 2 * sz.width, sz.block), jnp.bfloat16),
+                pltpu.VMEM((sz.n_blocks, 2 * sz.width, sz.block), jnp.float32),
+                pltpu.VMEM((sz.n_blocks, sz.width, sz.block), jnp.bfloat16),
+                pltpu.VMEM((sz.width, sz.width), jnp.bfloat16),
+                pltpu.VMEM((sz.width, sz.block), jnp.float32),
+                pltpu.SemaphoreType.DMA((2 * len(arrays),)),
+                pltpu.SemaphoreType.DMA,
+            ],
+            compiler_params=pltpu.CompilerParams(vmem_limit_bytes=40 * 1024 * 1024),
+        )(*arrays, w_first, w_second)
+    )
+
+
 def solution(mesh):
-    return jax.shard_map(
-        local,
+    specs = dict(
         mesh=mesh,
         in_specs=(
             P(("row", "col"), None),
@@ -114,3 +375,12 @@
         out_specs=(P(("row", "col"), None), P(), P()),
         check_vma=False,
     )
+
+    def run(features, w_first, w_second, block_index, block_count, block_values, cotangent):
+        sz = Sizes(mesh, features, block_values)
+        local = functools.partial(replicated_local, sz) if sz.replicates() else tiled_local
+        return jax.shard_map(local, **specs)(
+            features, w_first, w_second, block_index, block_count, block_values, cotangent
+        )
+
+    return run

time: 370 us -> 82.4 us (0.22)
  waiting for transfers between devices: 254 us -> 29.1 us
  blocking collectives: 72.8 us -> 0 us
  Pallas kernels: 0 us -> 33.4 us
  starting transfers between devices: 0.16 us -> 17.7 us
  local copies, waits for them, and re-layouts: 15.4 us -> 0.14 us
  between operations: 14.5 us -> 1.42 us
  matrix products: 8.13 us -> 0 us
    psum x1 -> x0, waiting for transfers between devices: 138 us -> none  [local(): lax.psum((first_terms, second_terms), ('row', 'col'))]
    reduce_scatter x3 -> x0, waiting for transfers between devices: 115 us -> none  [the longest x1 85.4 us: spread_cols(): lax.psum_scatter(partial_value, 'row', scatter_dimension=0, tiled=True)]
    all_gather x3 -> x0, blocking collectives: 72.8 us -> none  [the longest x2 64.2 us: spread_rows(): full_panel = lax.all_gather(layer_input, 'row', axis=0, tiled=True)]
    pallas_call x0 -> x2, Pallas kernels: none -> 33.4 us  [the longest x1 31.8 us: replicated_local(): pl.pallas_call(functools.partial(main_kernel, sz, shifts), out_shape=(jax...]
    ppermute x0 -> x19, waiting for transfers between devices: none -> 29.1 us  [send(): return lax.ppermute(value, AXES, pairs)]
    ppermute x0 -> x19, starting transfers between devices: none -> 17.7 us  [send(): return lax.ppermute(value, AXES, pairs)]
    dot_general x5 -> x0, matrix products: 8.13 us -> none  [the longest x1 2.28 us: local(): jnp.einsum('nf,ng->fg', first_active, back_second, preferred_element_type...]
    while x3 -> x0, local copies, waits for them, and re-layouts: 8.06 us -> none  [combine(): lax.fori_loop(0, groups, add_group, jnp.zeros((out_blocks, block_size, fe...]
  transfers between devices with their start and end apart: 4 -> 19, of which waited for: 3 -> 8; matrix products, arithmetic and copies ran while one was open for 3% -> 1% of each run, Pallas kernels for 0% -> 0%
where the time goes in v1:
time: 82.4 us; the launch traced here: 82.8 us
  Pallas kernels  33.4 us (41%)
  waiting for transfers between devices  29.1 us (35%)
  starting transfers between devices  17.7 us (21%)
  between operations  1.42 us (2%)
  other arithmetic  0.98 us (1%)
    pallas_call x1, Pallas kernels, replicated_local(): pl.pallas_call(functools.partial(main_kernel, sz, shifts), out_shape=(jax...  31.8 us
    ppermute x19, waiting for transfers between devices, send(): return lax.ppermute(value, AXES, pairs)  29.1 us
    ppermute x19, starting transfers between devices, send(): return lax.ppermute(value, AXES, pairs)  17.7 us
  transfers between devices with their start and end apart: 19, of which 8 were waited for; matrix products, arithmetic and copies ran while one was open for 1% of the time, Pallas kernels for 0%

profile of v1, /device:TPU:0, one launch (start us, length us, event | category | flops | bytes accessed | tf_op | source)
XLA Modules:
  0.0 82.8 jit_solution(11283991283064341342)
XLA Ops:
  1.3 1.6 %shard_map.94 = bf16[784,128]{1,0:T(8,128)(2,1)} custom-call(s32[1,1,8]{2,1,0:T(1,128)} %index_ref.1, s32[1,1]{1,0:T(1,128)S(6)} %copy.13.count_ref, bf16[64,512]{1,0:T(8,128)(2,1)} %feat_ref.1, bf16[64,512]{1,0:T(8,128)(2,1)} %cot_ref.1, bf16[1,1,8,128,128]{4,3,2,1,0:T(8,128)(2,1)} %val_ref.1), custom_call_target="tpu_custom_call" | custom-call | tf_op jit(solution)/shard_map/pallas_call | solution.py:156
  2.9 2.9 %collective-permute-start = (bf16[784,128]{1,0:T(8,128)(2,1)}, bf16[784,128]{1,0:T(8,128)(2,1)S(1)}, u32[]{:S(2)}, u32[]{:S(2)}) collective-permute-start(bf16[784,128]{1,0:T(8,128)(2,1)} %shard_map.94), channel_id=1, source_target_pairs={{0,2},{1,5},{2,0},{3,7},{4,6},{5,1},{6,4},{7,3},{8,10},{9,13},{10,... | collective-permute-start | bytes 602120 | tf_op jit(solution)/shard_map/ppermute | solution.py:183
  5.8 2.6 %collective-permute-start.14 = (bf16[784,128]{1,0:T(8,128)(2,1)}, bf16[784,128]{1,0:T(8,128)(2,1)S(1)}, u32[]{:S(2)}, u32[]{:S(2)}) collective-permute-start(bf16[784,128]{1,0:T(8,128)(2,1)} %shard_map.94), channel_id=1, source_target_pairs={{0,16},{1,17},{2,18},{3,19},{4,20},{5,21},{6,22},{7,23},{8,24},{9,... | collective-permute-start | bytes 602120 | tf_op jit(solution)/shard_map/ppermute | solution.py:183
  8.4 1.3 %collective-permute-start.9 = (bf16[784,128]{1,0:T(8,128)(2,1)}, bf16[784,128]{1,0:T(8,128)(2,1)S(1)}, u32[]{:S(2)}, u32[]{:S(2)}) collective-permute-start(bf16[784,128]{1,0:T(8,128)(2,1)} %shard_map.94), channel_id=1, source_target_pairs={{0,24},{1,25},{2,26},{3,27},{4,28},{5,29},{6,30},{7,31},{8,0},{9,1... | collective-permute-start | bytes 602120 | tf_op jit(solution)/shard_map/ppermute | solution.py:183
  9.8 0.7 collective-permute-start.4
  10.5 0.0 collective-permute-done
  10.5 1.0 %pad_maximum_fusion.refs_0_ = bf16[1568,128]{1,0:T(8,128)(2,1)S(1)} fusion(bf16[784,128]{1,0:T(8,128)(2,1)S(1)} %collective-permute-done, bf16[784,128]{1,0:T(8,128)(2,1)} %shard_map.94), kind=kLoop, calls=%fused_computation | loop fusion | flops 802816 | bytes 802816 | tf_op jit(solution)/shard_map/concatenate | solution.py:200
  11.4 0.1 collective-permute-start.2
  11.5 1.6 %collective-permute-start.1 = (bf16[1568,128]{1,0:T(8,128)(2,1)S(1)}, bf16[1568,128]{1,0:T(8,128)(2,1)S(1)}, u32[]{:S(2)}, u32[]{:S(2)}) collective-permute-start(bf16[1568,128]{1,0:T(8,128)(2,1)S(1)} %pad_maximum_fusion.refs_0_), channel_id=1, source_target_pairs={{0,4},{1,3},{2,6},{3,1},{4,0},{5,7},{6,2},{7,5},{8,12},{9,11},{10,... | collective-permute-start | bytes 1204232 | tf_op jit(solution)/shard_map/ppermute | solution.py:183
  13.1 7.2 %collective-permute-done.14 = bf16[784,128]{1,0:T(8,128)(2,1)S(1)} collective-permute-done((bf16[784,128]{1,0:T(8,128)(2,1)}, bf16[784,128]{1,0:T(8,128)(2,1)S(1)}, u32[]{:S(2)}, u32[]{:S(2)}) %collective-permute-start.14) | collective-permute-done | bytes 200736 | tf_op jit(solution)/shard_map/ppermute | solution.py:183
  20.3 0.0 collective-permute-start.15
  20.3 2.9 %collective-permute-done.4 = bf16[784,128]{1,0:T(8,128)(2,1)S(1)} collective-permute-done((bf16[784,128]{1,0:T(8,128)(2,1)}, bf16[784,128]{1,0:T(8,128)(2,1)S(1)}, u32[]{:S(2)}, u32[]{:S(2)}) %collective-permute-start.4) | collective-permute-done | bytes 200736 | tf_op jit(solution)/shard_map/ppermute | solution.py:183
  23.2 1.5 %collective-permute-start.5 = (bf16[784,128]{1,0:T(8,128)(2,1)S(1)}, bf16[784,128]{1,0:T(8,128)(2,1)S(1)}, u32[]{:S(2)}, u32[]{:S(2)}) collective-permute-start(bf16[784,128]{1,0:T(8,128)(2,1)S(1)} %collective-permute-done.4), channel_id=1, source_target_pairs={{0,2},{1,5},{2,0},{3,7},{4,6},{5,1},{6,4},{7,3},{8,10},{9,13},{10,... | collective-permute-start | bytes 602120 | tf_op jit(solution)/shard_map/ppermute | solution.py:183
  24.7 0.0 collective-permute-done.9
  24.7 0.6 collective-permute-start.10
  25.4 0.0 copy-start
  25.4 0.0 copy-start.1
  25.4 0.6 collective-permute-done.15
  26.0 0.1 collective-permute-start.17
  26.1 5.0 %collective-permute-done.10 = bf16[784,128]{1,0:T(8,128)(2,1)S(1)} collective-permute-done((bf16[784,128]{1,0:T(8,128)(2,1)S(1)}, bf16[784,128]{1,0:T(8,128)(2,1)S(1)}, u32[]{:S(2)}, u32[]{:S(2)}) %collective-permute-start.10) | collective-permute-done | bytes 200736 | tf_op jit(solution)/shard_map/ppermute | solution.py:183
  31.1 3.7 %collective-permute-start.16 = (bf16[1568,128]{1,0:T(8,128)(2,1)S(1)}, bf16[1568,128]{1,0:T(8,128)(2,1)S(1)}, u32[]{:S(2)}, u32[]{:S(2)}) collective-permute-start(bf16[1568,128]{1,0:T(8,128)(2,1)S(1)} %constant_dynamic-update-slice_fusion.4.refs_12_), channel_id=1, source_target_pairs={{0,4},{1,3},{2,6},{3,1},{4,0},{5,7},{6,2},{7,5},{8,12},{9,11},{10,... | collective-permute-start | bytes 1204232 | tf_op jit(solution)/shard_map/ppermute | solution.py:183
  34.8 0.0 collective-permute-done.5
  34.8 0.1 collective-permute-start.12
  34.9 0.0 collective-permute-done.2.refs_2_
  34.9 0.1 collective-permute-start.11
  35.0 0.0 collective-permute-done.1.refs_1_
  35.0 2.0 %collective-permute-start.6 = (bf16[1568,128]{1,0:T(8,128)(2,1)S(1)}, bf16[1568,128]{1,0:T(8,128)(2,1)S(1)}, u32[]{:S(2)}, u32[]{:S(2)}) collective-permute-start(bf16[1568,128]{1,0:T(8,128)(2,1)S(1)} %constant_dynamic-update-slice_fusion.refs_4_), channel_id=1, source_target_pairs={{0,4},{1,3},{2,6},{3,1},{4,0},{5,7},{6,2},{7,5},{8,12},{9,11},{10,... | collective-permute-start | bytes 1204232 | tf_op jit(solution)/shard_map/ppermute | solution.py:183
  37.0 0.0 collective-permute-done.17.refs_14_
  37.0 0.0 collective-permute-start.7
  37.0 3.6 %collective-permute-done.16.refs_13_ = bf16[1568,128]{1,0:T(8,128)(2,1)S(1)} collective-permute-done((bf16[1568,128]{1,0:T(8,128)(2,1)S(1)}, bf16[1568,128]{1,0:T(8,128)(2,1)S(1)}, u32[]{:S(2)}, u32[]{:S(2)}) %collective-permute-start.16) | collective-permute-done | bytes 401440 | tf_op jit(solution)/shard_map/ppermute | solution.py:183
  40.6 0.0 collective-permute-start.3
  40.6 0.0 collective-permute-done.12.refs_10_
  40.6 0.5 collective-permute-start.18
  41.1 3.8 %collective-permute-done.11.refs_9_ = bf16[1568,128]{1,0:T(8,128)(2,1)S(1)} collective-permute-done((bf16[1568,128]{1,0:T(8,128)(2,1)S(1)}, bf16[1568,128]{1,0:T(8,128)(2,1)S(1)}, u32[]{:S(2)}, u32[]{:S(2)}) %collective-permute-start.11) | collective-permute-done | bytes 401440 | tf_op jit(solution)/shard_map/ppermute | solution.py:183
  44.9 0.0 collective-permute-start.13
  44.9 4.3 %collective-permute-done.6.refs_5_ = bf16[1568,128]{1,0:T(8,128)(2,1)S(1)} collective-permute-done((bf16[1568,128]{1,0:T(8,128)(2,1)S(1)}, bf16[1568,128]{1,0:T(8,128)(2,1)S(1)}, u32[]{:S(2)}, u32[]{:S(2)}) %collective-permute-start.6) | collective-permute-done | bytes 401440 | tf_op jit(solution)/shard_map/ppermute | solution.py:183
  49.2 0.0 collective-permute-start.8
  49.2 0.0 collective-permute-done.7.refs_6_
  49.2 0.0 collective-permute-done.3.refs_3_
  49.2 0.0 collective-permute-done.18.refs_15_
  49.2 0.0 collective-permute-done.13.refs_11_
  49.2 1.7 %collective-permute-done.8.refs_7_ = bf16[1568,128]{1,0:T(8,128)(2,1)S(1)} collective-permute-done((bf16[1568,128]{1,0:T(8,128)(2,1)S(1)}, bf16[1568,128]{1,0:T(8,128)(2,1)S(1)}, u32[]{:S(2)}, u32[]{:S(2)}) %collective-permute-start.8) | collective-permute-done | bytes 401440 | tf_op jit(solution)/shard_map/ppermute | solution.py:183
  51.0 0.0 copy-done
  51.0 0.0 copy-done.1
  51.0 31.8 %shard_map.95 = (bf16[64,512]{1,0:T(8,128)(2,1)}, f32[512,512]{1,0:T(8,128)}, f32[512,512]{1,0:T(8,128)}) custom-call(bf16[1568,128]{1,0:T(8,128)(2,1)S(1)} %pad_maximum_fusion.refs_0_, bf16[1568,128]{1,0:T(8,128)(2,1)S(1)} %collective-permute-done.1.refs_1_, bf16[1568,128]{1,0:T(8,128)(2,1)S(1)} %collective-permute-done.2.refs_2_, ...), custom_call_target="tpu_custom_call" | custom-call | tf_op jit(solution)/shard_map/pallas_call | solution.py:341
  (6 shorter events, 0.1 us)
Async XLA Ops:
  2.9 7.6 %collective-permute-start = (bf16[784,128]{1,0:T(8,128)(2,1)}, bf16[784,128]{1,0:T(8,128)(2,1)S(1)}, u32[]{:S(2)}, u32[]{:S(2)}) collective-permute-start(bf16[784,128]{1,0:T(8,128)(2,1)} %shard_map.94), channel_id=1, source_target_pairs={{0,2},{1,5},{2,0},{3,7},{4,6},{5,1},{6,4},{7,3},{8,10},{9,13},{10,... | collective-permute-start | bytes 602120 | tf_op jit(solution)/shard_map/ppermute | solution.py:183
  5.8 14.4 %collective-permute-start.14 = (bf16[784,128]{1,0:T(8,128)(2,1)}, bf16[784,128]{1,0:T(8,128)(2,1)S(1)}, u32[]{:S(2)}, u32[]{:S(2)}) collective-permute-start(bf16[784,128]{1,0:T(8,128)(2,1)} %shard_map.94), channel_id=1, source_target_pairs={{0,16},{1,17},{2,18},{3,19},{4,20},{5,21},{6,22},{7,23},{8,24},{9,... | collective-permute-start | bytes 602120 | tf_op jit(solution)/shard_map/ppermute | solution.py:183
  8.4 16.3 %collective-permute-start.9 = (bf16[784,128]{1,0:T(8,128)(2,1)}, bf16[784,128]{1,0:T(8,128)(2,1)S(1)}, u32[]{:S(2)}, u32[]{:S(2)}) collective-permute-start(bf16[784,128]{1,0:T(8,128)(2,1)} %shard_map.94), channel_id=1, source_target_pairs={{0,24},{1,25},{2,26},{3,27},{4,28},{5,29},{6,30},{7,31},{8,0},{9,1... | collective-permute-start | bytes 602120 | tf_op jit(solution)/shard_map/ppermute | solution.py:183
  9.8 13.4 %collective-permute-start.4 = (bf16[784,128]{1,0:T(8,128)(2,1)}, bf16[784,128]{1,0:T(8,128)(2,1)S(1)}, u32[]{:S(2)}, u32[]{:S(2)}) collective-permute-start(bf16[784,128]{1,0:T(8,128)(2,1)} %shard_map.94), channel_id=1, source_target_pairs={{0,8},{1,9},{2,10},{3,11},{4,12},{5,13},{6,14},{7,15},{8,16},{9,17... | collective-permute-start | bytes 602120 | tf_op jit(solution)/shard_map/ppermute | solution.py:183
  11.4 23.5 %collective-permute-start.2 = (bf16[1568,128]{1,0:T(8,128)(2,1)S(1)}, bf16[1568,128]{1,0:T(8,128)(2,1)S(1)}, u32[]{:S(2)}, u32[]{:S(2)}) collective-permute-start(bf16[1568,128]{1,0:T(8,128)(2,1)S(1)} %pad_maximum_fusion.refs_0_), channel_id=1, source_target_pairs={{0,1},{1,0},{2,3},{3,2},{4,5},{5,4},{6,7},{7,6},{8,9},{9,8},{10,11... | collective-permute-start | bytes 1204232 | tf_op jit(solution)/shard_map/ppermute | solution.py:183
  11.5 23.5 %collective-permute-start.1 = (bf16[1568,128]{1,0:T(8,128)(2,1)S(1)}, bf16[1568,128]{1,0:T(8,128)(2,1)S(1)}, u32[]{:S(2)}, u32[]{:S(2)}) collective-permute-start(bf16[1568,128]{1,0:T(8,128)(2,1)S(1)} %pad_maximum_fusion.refs_0_), channel_id=1, source_target_pairs={{0,4},{1,3},{2,6},{3,1},{4,0},{5,7},{6,2},{7,5},{8,12},{9,11},{10,... | collective-permute-start | bytes 1204232 | tf_op jit(solution)/shard_map/ppermute | solution.py:183
  20.3 5.7 %collective-permute-start.15 = (bf16[784,128]{1,0:T(8,128)(2,1)S(1)}, bf16[784,128]{1,0:T(8,128)(2,1)S(1)}, u32[]{:S(2)}, u32[]{:S(2)}) collective-permute-start(bf16[784,128]{1,0:T(8,128)(2,1)S(1)} %collective-permute-done.14), channel_id=1, source_target_pairs={{0,2},{1,5},{2,0},{3,7},{4,6},{5,1},{6,4},{7,3},{8,10},{9,13},{10,... | collective-permute-start | bytes 602120 | tf_op jit(solution)/shard_map/ppermute | solution.py:183
  23.2 11.6 %collective-permute-start.5 = (bf16[784,128]{1,0:T(8,128)(2,1)S(1)}, bf16[784,128]{1,0:T(8,128)(2,1)S(1)}, u32[]{:S(2)}, u32[]{:S(2)}) collective-permute-start(bf16[784,128]{1,0:T(8,128)(2,1)S(1)} %collective-permute-done.4), channel_id=1, source_target_pairs={{0,2},{1,5},{2,0},{3,7},{4,6},{5,1},{6,4},{7,3},{8,10},{9,13},{10,... | collective-permute-start | bytes 602120 | tf_op jit(solution)/shard_map/ppermute | solution.py:183
  24.7 6.3 %collective-permute-start.10 = (bf16[784,128]{1,0:T(8,128)(2,1)S(1)}, bf16[784,128]{1,0:T(8,128)(2,1)S(1)}, u32[]{:S(2)}, u32[]{:S(2)}) collective-permute-start(bf16[784,128]{1,0:T(8,128)(2,1)S(1)} %collective-permute-done.9), channel_id=1, source_target_pairs={{0,2},{1,5},{2,0},{3,7},{4,6},{5,1},{6,4},{7,3},{8,10},{9,13},{10,... | collective-permute-start | bytes 602120 | tf_op jit(solution)/shard_map/ppermute | solution.py:183
  25.4 25.6 %copy-start = (bf16[512,512]{1,0:T(8,128)(2,1)S(1)}, bf16[512,512]{1,0:T(8,128)(2,1)}, u32[]{:S(2)}) copy-start(bf16[512,512]{1,0:T(8,128)(2,1)} %refs_16_.1) | copy-start | bytes 1572868
  25.4 25.6 %copy-start.1 = (bf16[512,512]{1,0:T(8,128)(2,1)S(1)}, bf16[512,512]{1,0:T(8,128)(2,1)}, u32[]{:S(2)}) copy-start(bf16[512,512]{1,0:T(8,128)(2,1)} %refs_17_.1) | copy-start | bytes 1572868
  26.0 11.0 %collective-permute-start.17 = (bf16[1568,128]{1,0:T(8,128)(2,1)S(1)}, bf16[1568,128]{1,0:T(8,128)(2,1)S(1)}, u32[]{:S(2)}, u32[]{:S(2)}) collective-permute-start(bf16[1568,128]{1,0:T(8,128)(2,1)S(1)} %constant_dynamic-update-slice_fusion.4.refs_12_), channel_id=1, source_target_pairs={{0,1},{1,0},{2,3},{3,2},{4,5},{5,4},{6,7},{7,6},{8,9},{9,8},{10,11... | collective-permute-start | bytes 1204232 | tf_op jit(solution)/shard_map/ppermute | solution.py:183
  31.1 9.5 %collective-permute-start.16 = (bf16[1568,128]{1,0:T(8,128)(2,1)S(1)}, bf16[1568,128]{1,0:T(8,128)(2,1)S(1)}, u32[]{:S(2)}, u32[]{:S(2)}) collective-permute-start(bf16[1568,128]{1,0:T(8,128)(2,1)S(1)} %constant_dynamic-update-slice_fusion.4.refs_12_), channel_id=1, source_target_pairs={{0,4},{1,3},{2,6},{3,1},{4,0},{5,7},{6,2},{7,5},{8,12},{9,11},{10,... | collective-permute-start | bytes 1204232 | tf_op jit(solution)/shard_map/ppermute | solution.py:183
  34.8 5.8 %collective-permute-start.12 = (bf16[1568,128]{1,0:T(8,128)(2,1)S(1)}, bf16[1568,128]{1,0:T(8,128)(2,1)S(1)}, u32[]{:S(2)}, u32[]{:S(2)}) collective-permute-start(bf16[1568,128]{1,0:T(8,128)(2,1)S(1)} %constant_dynamic-update-slice_fusion.2.refs_8_), channel_id=1, source_target_pairs={{0,1},{1,0},{2,3},{3,2},{4,5},{5,4},{6,7},{7,6},{8,9},{9,8},{10,11... | collective-permute-start | bytes 1204232 | tf_op jit(solution)/shard_map/ppermute | solution.py:183
  34.9 10.0 %collective-permute-start.11 = (bf16[1568,128]{1,0:T(8,128)(2,1)S(1)}, bf16[1568,128]{1,0:T(8,128)(2,1)S(1)}, u32[]{:S(2)}, u32[]{:S(2)}) collective-permute-start(bf16[1568,128]{1,0:T(8,128)(2,1)S(1)} %constant_dynamic-update-slice_fusion.2.refs_8_), channel_id=1, source_target_pairs={{0,4},{1,3},{2,6},{3,1},{4,0},{5,7},{6,2},{7,5},{8,12},{9,11},{10,... | collective-permute-start | bytes 1204232 | tf_op jit(solution)/shard_map/ppermute | solution.py:183
  35.0 14.2 %collective-permute-start.6 = (bf16[1568,128]{1,0:T(8,128)(2,1)S(1)}, bf16[1568,128]{1,0:T(8,128)(2,1)S(1)}, u32[]{:S(2)}, u32[]{:S(2)}) collective-permute-start(bf16[1568,128]{1,0:T(8,128)(2,1)S(1)} %constant_dynamic-update-slice_fusion.refs_4_), channel_id=1, source_target_pairs={{0,4},{1,3},{2,6},{3,1},{4,0},{5,7},{6,2},{7,5},{8,12},{9,11},{10,... | collective-permute-start | bytes 1204232 | tf_op jit(solution)/shard_map/ppermute | solution.py:183
  37.0 12.2 %collective-permute-start.7 = (bf16[1568,128]{1,0:T(8,128)(2,1)S(1)}, bf16[1568,128]{1,0:T(8,128)(2,1)S(1)}, u32[]{:S(2)}, u32[]{:S(2)}) collective-permute-start(bf16[1568,128]{1,0:T(8,128)(2,1)S(1)} %constant_dynamic-update-slice_fusion.refs_4_), channel_id=1, source_target_pairs={{0,1},{1,0},{2,3},{3,2},{4,5},{5,4},{6,7},{7,6},{8,9},{9,8},{10,11... | collective-permute-start | bytes 1204232 | tf_op jit(solution)/shard_map/ppermute | solution.py:183
  40.6 8.6 %collective-permute-start.3 = (bf16[1568,128]{1,0:T(8,128)(2,1)S(1)}, bf16[1568,128]{1,0:T(8,128)(2,1)S(1)}, u32[]{:S(2)}, u32[]{:S(2)}) collective-permute-start(bf16[1568,128]{1,0:T(8,128)(2,1)S(1)} %collective-permute-done.1.refs_1_), channel_id=1, source_target_pairs={{0,1},{1,0},{2,3},{3,2},{4,5},{5,4},{6,7},{7,6},{8,9},{9,8},{10,11... | collective-permute-start | bytes 1204232 | tf_op jit(solution)/shard_map/ppermute | solution.py:183
  40.6 8.6 %collective-permute-start.18 = (bf16[1568,128]{1,0:T(8,128)(2,1)S(1)}, bf16[1568,128]{1,0:T(8,128)(2,1)S(1)}, u32[]{:S(2)}, u32[]{:S(2)}) collective-permute-start(bf16[1568,128]{1,0:T(8,128)(2,1)S(1)} %collective-permute-done.16.refs_13_), channel_id=1, source_target_pairs={{0,1},{1,0},{2,3},{3,2},{4,5},{5,4},{6,7},{7,6},{8,9},{9,8},{10,11... | collective-permute-start | bytes 1204232 | tf_op jit(solution)/shard_map/ppermute | solution.py:183
  44.9 4.3 %collective-permute-start.13 = (bf16[1568,128]{1,0:T(8,128)(2,1)S(1)}, bf16[1568,128]{1,0:T(8,128)(2,1)S(1)}, u32[]{:S(2)}, u32[]{:S(2)}) collective-permute-start(bf16[1568,128]{1,0:T(8,128)(2,1)S(1)} %collective-permute-done.11.refs_9_), channel_id=1, source_target_pairs={{0,1},{1,0},{2,3},{3,2},{4,5},{5,4},{6,7},{7,6},{8,9},{9,8},{10,11... | collective-permute-start | bytes 1204232 | tf_op jit(solution)/shard_map/ppermute | solution.py:183
  49.2 1.7 %collective-permute-start.8 = (bf16[1568,128]{1,0:T(8,128)(2,1)S(1)}, bf16[1568,128]{1,0:T(8,128)(2,1)S(1)}, u32[]{:S(2)}, u32[]{:S(2)}) collective-permute-start(bf16[1568,128]{1,0:T(8,128)(2,1)S(1)} %collective-permute-done.6.refs_5_), channel_id=1, source_target_pairs={{0,1},{1,0},{2,3},{3,2},{4,5},{5,4},{6,7},{7,6},{8,9},{9,8},{10,11... | collective-permute-start | bytes 1204232 | tf_op jit(solution)/shard_map/ppermute | solution.py:183

commit v2 on v1

--- a/solution.py
+++ b/solution.py
@@ -106,6 +106,11 @@
     return (out_second, grad_first, grad_second)
 
 
+VMEM_SPEC = pl.BlockSpec(memory_space=pltpu.VMEM)
+VMEM_LIMIT = 12 * 1024 * 1024
+SMALL_LIMIT = 2 * 1024 * 1024
+
+
 class Sizes:
     def __init__(self, mesh, features, block_values):
         self.n_row, self.n_col = mesh.shape["row"], mesh.shape["col"]
@@ -130,45 +135,68 @@
             whole <= REPLICATE_BYTES
             and self.n_col == 4
             and self.n_row % 2 == 0
+            and self.n_row & (self.n_row - 1) == 0
             and 2 * self.rows == self.block
             and self.blk_rows == 2
             and self.n_blocks % 2 == 0
         )
 
 
-def pack_kernel(sz, index_ref, count_ref, feat_ref, cot_ref, val_ref, out_ref):
+def pack_kernel(sz, index_ref, count_ref, feat_ref, cot_ref, val_ref, out_ref, sems):
+    copies = []
     for k in range(sz.chunks):
         lanes = pl.ds(k * sz.block, sz.block)
-        out_ref[pl.ds(k * sz.rows, sz.rows), :] = feat_ref[:, lanes]
-        out_ref[pl.ds(sz.at_cot + k * sz.rows, sz.rows), :] = cot_ref[:, lanes]
+        copies.append((feat_ref.at[:, lanes], k * sz.rows, sz.rows))
+        copies.append((cot_ref.at[:, lanes], sz.at_cot + k * sz.rows, sz.rows))
     for s in range(sz.live):
-        out_ref[pl.ds(sz.at_val + s * sz.block, sz.block), :] = val_ref[0, 0, s]
+        copies.append((val_ref.at[0, 0, s], sz.at_val + s * sz.block, sz.block))
+    copies = [
+        pltpu.make_async_copy(src, out_ref.at[pl.ds(at, rows)], sems.at[n])
+        for n, (src, at, rows) in enumerate(copies)
+    ]
+    for copy in copies:
+        copy.start()
     lane = lax.broadcasted_iota(jnp.int32, (16, sz.block), 1)
     info = jnp.where(lane == 0, count_ref[0, 0], 0)
     for s in range(sz.live):
         info = jnp.where(lane == s + 1, index_ref[0, 0, s], info)
     out_ref[pl.ds(sz.at_info, 16), :] = info.astype(jnp.float32).astype(jnp.bfloat16)
+    for copy in copies:
+        copy.wait()
 
 
 def pack(sz, features, block_index, block_count, block_values, cotangent):
-    vmem = pl.BlockSpec(memory_space=pltpu.VMEM)
     smem = pl.BlockSpec(memory_space=pltpu.SMEM)
+    far = pl.BlockSpec(memory_space=pl.ANY)
     return pl.pallas_call(
         functools.partial(pack_kernel, sz),
-        grid=(1,),
-        out_shape=jax.ShapeDtypeStruct((sz.payload, sz.block), jnp.bfloat16),
-        in_specs=[
-            smem,
-            smem,
-            pl.BlockSpec((sz.rows, sz.width), lambda i: (0, 0)),
-            pl.BlockSpec((sz.rows, sz.width), lambda i: (0, 0)),
-            pl.BlockSpec((1, 1, sz.live, sz.block, sz.block), lambda i: (0, 0, 0, 0, 0)),
-        ],
-        out_specs=pl.BlockSpec((sz.payload, sz.block), lambda i: (0, 0)),
-    )(block_index, block_count, features, cotangent, block_values)
-
-
-def gather_parts(sz, payload):
+        out_shape=pltpu.VMEM((sz.payload, sz.block), jnp.bfloat16),
+        in_specs=[smem, smem, far, far, far],
+        out_specs=VMEM_SPEC,
+        scratch_shapes=[pltpu.SemaphoreType.DMA((2 * sz.chunks + sz.live,))],
+        compiler_params=pltpu.CompilerParams(vmem_limit_bytes=SMALL_LIMIT),
+    )(
+        block_index,
+        block_count,
+        *(
+            pltpu.with_memory_space_constraint(a, pltpu.HBM)
+            for a in (features, cotangent, block_values)
+        ),
+    )
+
+
+def hold(value, token):
+    return pl.pallas_call(
+        lambda value_ref, token_ref, out_ref: None,
+        out_shape=pltpu.VMEM(value.shape, value.dtype),
+        in_specs=[VMEM_SPEC, pl.BlockSpec(memory_space=pl.ANY)],
+        out_specs=VMEM_SPEC,
+        input_output_aliases={0: 0},
+        compiler_params=pltpu.CompilerParams(vmem_limit_bytes=SMALL_LIMIT),
+    )(pltpu.with_memory_space_constraint(value, pltpu.VMEM), token)
+
+
+def collect(sz, payload):
     n_z = sz.n_row // 2
 
     def send(value, to):
@@ -191,92 +219,115 @@
     def sibling(z, y, x, c):
         return (z, y, x, 1 - c)
 
-    shifts = sorted(range(n_z), key=lambda d: min(d, n_z - d))
-    parts = []
-    for d in shifts:
-        own = payload
-        if d:
-            own = send(payload, lambda z, y, x, c: ((z + d) % n_z, y, x, c))
-        near = jnp.concatenate([own, send(own, first_way)], axis=0)
+    def plane(own, token):
+        one = send(own, first_way)
+        if token is not None:
+            two, three = hold(send(own, second_way), token), send(one, second_way)
+            near = jnp.concatenate([own, one], axis=0)
+            far = jnp.concatenate([two, three], axis=0)
+            return near, far, send(near, sibling), send(far, sibling)
+        near = jnp.concatenate([own, one], axis=0)
         far = send(near, second_way)
-        parts.append((d, near, far, send(near, sibling), send(far, sibling)))
-    return parts
-
-
-def main_kernel(sz, shifts, *refs):
-    n_parts = 4 * len(shifts)
-    part_refs = refs[:n_parts]
-    w1_ref, w2_ref, out_ref, gf_ref, gs_ref = refs[n_parts : n_parts + 5]
-    buf, info_v, info_s, fct, gb, act, w1t, rows_out, sem, info_sem = refs[n_parts + 5 :]
-    n_z = sz.n_row // 2
+        return near, far, send(near, sibling), send(far, sibling)
+
+    def flip(d):
+        return lambda z, y, x, c: (z ^ d, y, x, c)
+
+    held = {0: payload}
+    low = 1
+    while low < n_z:
+        whole = 2 * low - 1
+        arrived = send(payload, flip(whole))
+        for d in list(held):
+            held[whole ^ d] = arrived if d == 0 else send(arrived, flip(d))
+        low *= 2
+    order = sorted(held, key=lambda d: (d.bit_length(), -d))
+    sums = None
+    for d in order:
+        token = sums[1] if d == order[-1] else None
+        sums = add_plane(sz, plane(held[d], token), sums)
+    return sums
+
+
+def place():
+    row, col = lax.axis_index("row"), lax.axis_index("col")
+    return row // 2, row % 2, col // 2, col % 2
+
+
+def plane_kernel(sz, first, *refs):
+    parts, refs = refs[:4], refs[4:]
+    if first:
+        sums, info_v, vals_out = refs[:3]
+    else:
+        sums, info_v = refs[1:3]
+    buf, info_s, turned, sem = refs[3:]
+    _, _, x, c = place()
+    block, size = sz.block, sz.payload
+
+    for mine in range(2):
+
+        @pl.when(c == mine)
+        def _():
+            for q in range(2):
+                for n in range(4):
+                    core = mine if q == 0 else 1 - mine
+                    m = n if core == 0 else (n // 2) + 2 * (n % 2)
+                    buf[m, core] = parts[2 * q + n // 2][pl.ds((n % 2) * size, size), :]
+
+    line = lax.broadcasted_iota(jnp.int32, (8, block), 0)
+    info = jnp.zeros((8, block), jnp.int32)
+    for m in range(4):
+        for e in range(2):
+            rows = buf[m, e, pl.ds(sz.at_info, 16), :].astype(jnp.float32).astype(jnp.int32)
+            info = jnp.where(line == 2 * m + e, rows[0:8], info)
+    info_v[...] = info
+    info_copy = pltpu.make_async_copy(info_v, info_s, sem)
+    info_copy.start()
+
+    if first:
+        sums[...] = jnp.zeros_like(sums)
+        for m in range(2):
+            for e in range(2):
+                vals_out[2 * m + e] = buf[m, e, pl.ds(sz.at_val, sz.live * block), :]
+
+    for m in range(4):
+        dx, dy = m % 2, m // 2
+        for k in range(2 * sz.chunks):
+            at = pl.ds(k * sz.rows, sz.rows)
+            piece = jnp.concatenate([buf[m, 0, at, :], buf[m, 1, at, :]], axis=0)
+            turned[2 * dy + (x ^ dx), pl.ds(k * block, block), :] = jnp.transpose(piece)
+    info_copy.wait()
+
+    for m in range(4):
+        dx, dy = m % 2, m // 2
+        for e in range(2):
+            j = (x ^ dx) * 2 + e
+            count = info_s[2 * m + e, 0]
+            for s in range(sz.live):
+                p = info_s[2 * m + e, s + 1]
+
+                @pl.when(s < count)
+                def _():
+                    r, cb = p // sz.blk_cols, lax.rem(p, sz.blk_cols)
+                    value = buf[m, e, pl.ds(sz.at_val + s * block, block), :]
+                    sums[j * sz.blk_cols + cb] += jnp.dot(
+                        turned[2 * dy + r], value, preferred_element_type=jnp.float32
+                    )
+
+
+def dense_kernel(
+    sz, sums, vals, info_v, w1_ref, w2_ref, out_ref, gf_ref, gs_ref, act, w1t, rows_out, info_s, sem
+):
     block, width = sz.block, sz.width
-    row, col = lax.axis_index("row"), lax.axis_index("col")
-    z, y, x, c = row // 2, row % 2, col // 2, col % 2
-
-    copies = []
-    for n, d in enumerate(shifts):
-        for q in range(4):
-            for k in range(2):
-                core = c if q < 2 else 1 - c
-                first, second = k, q % 2
-                dx = jnp.where(core == 0, first, second)
-                dy = jnp.where(core == 0, second, first)
-                from_z = lax.rem(z + n_z - d, n_z)
-                from_y, from_x = lax.rem(y + dy, 2), lax.rem(x + dx, 2)
-                dev = (from_z * 2 + from_y) * 4 + from_x * 2 + core
-                copy = pltpu.make_async_copy(
-                    part_refs[4 * n + q].at[pl.ds(k * sz.payload, sz.payload)],
-                    buf.at[dev],
-                    sem.at[(4 * n + q) * 2 + k],
-                )
-                copy.start()
-                copies.append(copy)
-
-    w1t[...] = jnp.transpose(w1_ref[...].astype(jnp.float32)).astype(jnp.bfloat16)
-    gb[...] = jnp.zeros_like(gb)
-    for copy in copies:
-        copy.wait()
-
-    for t in range(sz.n_dev):
-        line = buf[t, pl.ds(sz.at_info, 16), :]
-        info_v[pl.ds(t * 8, 8), :] = line.astype(jnp.float32).astype(jnp.int32)[0:8]
-    info_copy = pltpu.make_async_copy(info_v, info_s, info_sem)
+    _, _, x, c = place()
+    info_copy = pltpu.make_async_copy(info_v, info_s, sem)
     info_copy.start()
-    info_copy.wait()
-
-    def tile_blocks(t):
-        count = info_s[t * 8, 0]
-        for s in range(sz.live):
-            p = info_s[t * 8, s + 1]
-            yield s < count, p // sz.blk_cols, lax.rem(p, sz.blk_cols), s
-
-    def values(t, s):
-        return buf[t, pl.ds(sz.at_val + s * block, block), :]
-
-    def tile_row(i, carry):
-        for r in range(sz.blk_rows):
-            t0 = i * sz.n_col + 2 * r
-            for k in range(2 * sz.chunks):
-                at = pl.ds(k * sz.rows, sz.rows)
-                piece = jnp.concatenate([buf[t0, at, :], buf[t0 + 1, at, :]], axis=0)
-                fct[r, pl.ds(k * block, block), :] = jnp.transpose(piece)
-        for j in range(sz.n_col):
-            t = i * sz.n_col + j
-            for live, r, cb, s in tile_blocks(t):
-
-                @pl.when(live)
-                def _():
-                    gb[j * sz.blk_cols + cb] += jnp.dot(
-                        fct[r], values(t, s), preferred_element_type=jnp.float32
-                    )
-
-        return carry
-
-    lax.fori_loop(0, sz.n_row, tile_row, 0)
+    w1t[...] = jnp.transpose(w1_ref[...])
+    nt = (((1,), (1,)), ((), ()))
 
     def chunk(n, carry):
         both = jnp.concatenate(
-            [gb[2 * n].astype(jnp.bfloat16), gb[2 * n + 1].astype(jnp.bfloat16)], axis=1
+            [sums[2 * n].astype(jnp.bfloat16), sums[2 * n + 1].astype(jnp.bfloat16)], axis=1
         )
         g, b = both[:width], both[width:]
         v = jnp.dot(w1t[...], g, preferred_element_type=jnp.float32)
@@ -289,7 +340,6 @@
         act[2 * n + 1] = a[:, block:]
         back = jnp.dot(w2_ref[...], b, preferred_element_type=jnp.float32)
         bf = (back * slope).astype(jnp.bfloat16)
-        nt = (((1,), (1,)), ((), ()))
         gs = lax.dot_general(a, b, nt, preferred_element_type=jnp.float32)
         gf = lax.dot_general(g, bf, nt, preferred_element_type=jnp.float32)
 
@@ -306,20 +356,25 @@
         return carry
 
     lax.fori_loop(0, sz.n_blocks // 2, chunk, 0)
+    info_copy.wait()
 
     rows_out[...] = jnp.zeros_like(rows_out)
-    for j in range(sz.n_col):
-        t = row * sz.n_col + j
-        for live, r, cb, s in tile_blocks(t):
-
-            @pl.when(live & (r == x))
-            def _():
-                rows_out[...] += lax.dot_general(
-                    act[j * sz.blk_cols + cb],
-                    values(t, s),
-                    (((1,), (1,)), ((), ())),
-                    preferred_element_type=jnp.float32,
-                )
+    for dx in range(2):
+        for e in range(2):
+            q = 2 * dx + e
+            count = info_s[q, 0]
+            for s in range(sz.live):
+                p = info_s[q, s + 1]
+
+                @pl.when((s < count) & (p // sz.blk_cols == x))
+                def _():
+                    cb = ((x ^ dx) * 2 + e) * sz.blk_cols + lax.rem(p, sz.blk_cols)
+                    rows_out[...] += lax.dot_general(
+                        act[cb],
+                        vals[q, pl.ds(s * block, block), :],
+                        nt,
+                        preferred_element_type=jnp.float32,
+                    )
 
     h = jnp.transpose(rows_out[...])
     high = h.astype(jnp.bfloat16)
@@ -330,34 +385,65 @@
     out_ref[...] = out.astype(jnp.bfloat16)
 
 
-def replicated_local(sz, features, w_first, w_second, block_index, block_count, block_values, cotangent):
-    payload = pack(sz, features, block_index, block_count, block_values, cotangent)
-    parts = gather_parts(sz, payload)
-    shifts = [p[0] for p in parts]
-    arrays = [a for p in parts for a in p[1:]]
-    vmem = pl.BlockSpec(memory_space=pltpu.VMEM)
+def add_plane(sz, parts, sums):
+    parts = [pltpu.with_memory_space_constraint(a, pltpu.VMEM) for a in parts]
+    sums_type = pltpu.VMEM((sz.n_blocks, 2 * sz.width, sz.block), jnp.float32)
+    token_type = pltpu.VMEM((8, sz.block), jnp.int32)
+    params = dict(
+        scratch_shapes=[
+            pltpu.VMEM((4, 2, sz.payload, sz.block), jnp.bfloat16),
+            pltpu.SMEM((8, sz.block), jnp.int32),
+            pltpu.VMEM((4, 2 * sz.width, sz.block), jnp.bfloat16),
+            pltpu.SemaphoreType.DMA,
+        ],
+        compiler_params=pltpu.CompilerParams(vmem_limit_bytes=VMEM_LIMIT),
+    )
+    if sums is None:
+        vals_type = pltpu.VMEM((4, sz.live * sz.block, sz.block), jnp.bfloat16)
+        total, token, vals = pl.pallas_call(
+            functools.partial(plane_kernel, sz, True),
+            out_shape=(sums_type, token_type, vals_type),
+            in_specs=[VMEM_SPEC] * 4,
+            out_specs=[VMEM_SPEC] * 3,
+            **params,
+        )(*parts)
+        return total, token, vals, token
+    total, token = pl.pallas_call(
+        functools.partial(plane_kernel, sz, False),
+        out_shape=(sums_type, token_type),
+        in_specs=[VMEM_SPEC] * 5,
+        out_specs=[VMEM_SPEC] * 2,
+        input_output_aliases={4: 0},
+        **params,
+    )(*parts, pltpu.with_memory_space_constraint(sums[0], pltpu.VMEM))
+    return total, token, *sums[2:]
+
+
+def dense(sz, sums, vals, info, w_first, w_second):
     grad = jax.ShapeDtypeStruct((sz.width, sz.width), jnp.float32)
+    inputs = [pltpu.with_memory_space_constraint(a, pltpu.VMEM) for a in (sums, vals, info)]
     return tuple(
         pl.pallas_call(
-            functools.partial(main_kernel, sz, shifts),
+            functools.partial(dense_kernel, sz),
             out_shape=(jax.ShapeDtypeStruct((sz.rows, sz.width), jnp.bfloat16), grad, grad),
-            in_specs=[pl.BlockSpec(memory_space=pl.ANY)] * len(arrays) + [vmem] * 2,
-            out_specs=(vmem, vmem, vmem),
+            in_specs=[VMEM_SPEC] * 5,
+            out_specs=[VMEM_SPEC] * 3,
             scratch_shapes=[
-                pltpu.VMEM((sz.n_dev, sz.payload, sz.block), jnp.bfloat16),
-                pltpu.VMEM((sz.n_dev * 8, sz.block), jnp.int32),
-                pltpu.SMEM((sz.n_dev * 8, sz.block), jnp.int32),
-                pltpu.VMEM((sz.blk_rows, 2 * sz.width, sz.block), jnp.bfloat16),
-                pltpu.VMEM((sz.n_blocks, 2 * sz.width, sz.block), jnp.float32),
                 pltpu.VMEM((sz.n_blocks, sz.width, sz.block), jnp.bfloat16),
                 pltpu.VMEM((sz.width, sz.width), jnp.bfloat16),
                 pltpu.VMEM((sz.width, sz.block), jnp.float32),
-                pltpu.SemaphoreType.DMA((2 * len(arrays),)),
+                pltpu.SMEM((8, sz.block), jnp.int32),
                 pltpu.SemaphoreType.DMA,
             ],
-            compiler_params=pltpu.CompilerParams(vmem_limit_bytes=40 * 1024 * 1024),
-        )(*arrays, w_first, w_second)
-    )
+            compiler_params=pltpu.CompilerParams(vmem_limit_bytes=VMEM_LIMIT),
+        )(*inputs, w_first, w_second)
+    )
+
+
+def replicated_local(sz, features, w_first, w_second, block_index, block_count, block_values, cotangent):
+    payload = pack(sz, features, block_index, block_count, block_values, cotangent)
+    sums, _, vals, info = collect(sz, payload)
+    return dense(sz, sums, vals, info, w_first, w_second)
 
 
 def solution(mesh):

time: 82.4 us -> 63.5 us (0.77)
  Pallas kernels: 33.4 us -> 23.9 us
  waiting for transfers between devices: 29.1 us -> 20.1 us
  other arithmetic: 0.98 us -> 0.06 us
    pallas_call x2 -> x7, Pallas kernels: 33.4 us -> 23.9 us  [the longest x1 10.8 us: dense(): pl.pallas_call(functools.partial(dense_kernel, sz), out_shape=(jax.ShapeD...]
    ppermute x19 -> x20, waiting for transfers between devices: 29.1 us -> 20.1 us  [send(): return lax.ppermute(value, AXES, pairs)]
    concatenate x1 -> x2, other arithmetic: 0.98 us -> 0.06 us  [the longest x1 0.03 us: plane(): far = jnp.concatenate([two, three], axis=0)]
    ppermute x19 -> x20, starting transfers between devices: 17.7 us -> 17.5 us  [send(): return lax.ppermute(value, AXES, pairs)]
  transfers between devices with their start and end apart: 19 -> 20, of which waited for: 8 -> 6; matrix products, arithmetic and copies ran while one was open for 1% -> 0% of each run, Pallas kernels for 0% -> 13%
where the time goes in v2:
time: 63.5 us; the launch traced here: 63.9 us
  Pallas kernels  23.9 us (38%)
  waiting for transfers between devices  20.1 us (32%)
  starting transfers between devices  17.5 us (28%)
  between operations  1.47 us (2%)
  local copies, waits for them, and re-layouts  0.79 us (1%)
    ppermute x20, waiting for transfers between devices, send(): return lax.ppermute(value, AXES, pairs)  20.1 us
    ppermute x20, starting transfers between devices, send(): return lax.ppermute(value, AXES, pairs)  17.5 us
    pallas_call x1, Pallas kernels, dense(): pl.pallas_call(functools.partial(dense_kernel, sz), out_shape=(jax.ShapeD...  10.8 us
    pallas_call x3, Pallas kernels, add_plane(): pl.pallas_call(functools.partial(plane_kernel, sz, False), out_shape=(sum...  9.17 us
    pallas_call x1, Pallas kernels, add_plane(): pl.pallas_call(functools.partial(plane_kernel, sz, True), out_shape=(sums...  2.44 us
    pallas_call x1, Pallas kernels, pack(): pl.pallas_call(functools.partial(pack_kernel, sz), out_shape=pltpu.VMEM((...  1.53 us
  transfers between devices with their start and end apart: 20, of which 6 were waited for; matrix products, arithmetic and copies ran while one was open for 0% of the time, Pallas kernels for 13%

profile of v2, /device:TPU:0, one launch (start us, length us, event | category | flops | bytes accessed | tf_op | source)
XLA Modules:
  0.0 63.9 jit_solution(10503368528442675242)
XLA Ops:
  1.3 0.6 %copy-done.2 = s32[1,1,8]{2,1,0:T(1,128)S(1)} copy-done((s32[1,1,8]{2,1,0:T(1,128)S(1)}, s32[1,1,8]{2,1,0:T(1,128)}, u32[]{:S(2)}) %copy-start.2) | copy-done | bytes 56
  1.9 1.5 %shard_map.94 = bf16[784,128]{1,0:T(8,128)(2,1)S(1)} custom-call(s32[1,1,8]{2,1,0:T(1,128)S(1)} %copy-done.2, s32[1,1]{1,0:T(1,128)S(6)} %copy.21.count_ref, bf16[64,512]{1,0:T(8,128)(2,1)} %feat_ref.1, bf16[64,512]{1,0:T(8,128)(2,1)} %cot_ref.1, bf16[1,1,8,128,128]{4,3,2,1,0:T(8,128)(2,1)} %val_ref.1), custom_call_target="tpu_custom_call" | custom-call | tf_op jit(solution)/shard_map/pallas_call | solution.py:171
  3.5 3.0 %collective-permute-start.13 = (bf16[784,128]{1,0:T(8,128)(2,1)S(1)}, bf16[784,128]{1,0:T(8,128)(2,1)S(1)}, u32[]{:S(2)}, u32[]{:S(2)}) collective-permute-start(bf16[784,128]{1,0:T(8,128)(2,1)S(1)} %shard_map.94), channel_id=1, source_target_pairs={{0,2},{1,5},{2,0},{3,7},{4,6},{5,1},{6,4},{7,3},{8,10},{9,13},{10,... | collective-permute-start | bytes 602120 | tf_op jit(solution)/shard_map/ppermute | solution.py:211
  6.5 1.6 %collective-permute-start.8 = (bf16[784,128]{1,0:T(8,128)(2,1)S(1)}, bf16[784,128]{1,0:T(8,128)(2,1)S(1)}, u32[]{:S(2)}, u32[]{:S(2)}) collective-permute-start(bf16[784,128]{1,0:T(8,128)(2,1)S(1)} %shard_map.94), channel_id=1, source_target_pairs={{0,8},{1,9},{2,10},{3,11},{4,12},{5,13},{6,14},{7,15},{8,0},{9,1},... | collective-permute-start | bytes 602120 | tf_op jit(solution)/shard_map/ppermute | solution.py:211
  8.1 2.5 %collective-permute-start = (bf16[784,128]{1,0:T(8,128)(2,1)S(1)}, bf16[784,128]{1,0:T(8,128)(2,1)S(1)}, u32[]{:S(2)}, u32[]{:S(2)}) collective-permute-start(bf16[784,128]{1,0:T(8,128)(2,1)S(1)} %shard_map.94), channel_id=1, source_target_pairs={{0,24},{1,25},{2,26},{3,27},{4,28},{5,29},{6,30},{7,31},{8,16},{9,... | collective-permute-start | bytes 602120 | tf_op jit(solution)/shard_map/ppermute | solution.py:211
  10.5 0.0 collective-permute-done.13
  10.6 1.8 %collective-permute-start.14 = (bf16[1568,128]{1,0:T(8,128)(2,1)S(1)}, bf16[1568,128]{1,0:T(8,128)(2,1)S(1)}, u32[]{:S(2)}, u32[]{:S(2)}) collective-permute-start(bf16[1568,128]{1,0:T(8,128)(2,1)S(1)} %pad_maximum_fusion.refs_0_), channel_id=1, source_target_pairs={{0,4},{1,3},{2,6},{3,1},{4,0},{5,7},{6,2},{7,5},{8,12},{9,11},{10,... | collective-permute-start | bytes 1204232 | tf_op jit(solution)/shard_map/ppermute | solution.py:211
  12.3 0.0 collective-permute-start.15
  12.3 1.2 %collective-permute-done.8 = bf16[784,128]{1,0:T(8,128)(2,1)S(1)} collective-permute-done((bf16[784,128]{1,0:T(8,128)(2,1)S(1)}, bf16[784,128]{1,0:T(8,128)(2,1)S(1)}, u32[]{:S(2)}, u32[]{:S(2)}) %collective-permute-start.8) | collective-permute-done | bytes 200736 | tf_op jit(solution)/shard_map/ppermute | solution.py:211
  13.5 0.9 %collective-permute-start.9 = (bf16[784,128]{1,0:T(8,128)(2,1)S(1)}, bf16[784,128]{1,0:T(8,128)(2,1)S(1)}, u32[]{:S(2)}, u32[]{:S(2)}) collective-permute-start(bf16[784,128]{1,0:T(8,128)(2,1)S(1)} %collective-permute-done.8), channel_id=1, source_target_pairs={{0,2},{1,5},{2,0},{3,7},{4,6},{5,1},{6,4},{7,3},{8,10},{9,13},{10,... | collective-permute-start | bytes 602120 | tf_op jit(solution)/shard_map/ppermute | solution.py:211
  14.4 5.0 %collective-permute-done = bf16[784,128]{1,0:T(8,128)(2,1)S(1)} collective-permute-done((bf16[784,128]{1,0:T(8,128)(2,1)S(1)}, bf16[784,128]{1,0:T(8,128)(2,1)S(1)}, u32[]{:S(2)}, u32[]{:S(2)}) %collective-permute-start) | collective-permute-done | bytes 200736 | tf_op jit(solution)/shard_map/ppermute | solution.py:211
  19.4 1.5 %collective-permute-start.4 = (bf16[784,128]{1,0:T(8,128)(2,1)S(1)}, bf16[784,128]{1,0:T(8,128)(2,1)S(1)}, u32[]{:S(2)}, u32[]{:S(2)}) collective-permute-start(bf16[784,128]{1,0:T(8,128)(2,1)S(1)} %collective-permute-done), channel_id=1, source_target_pairs={{0,2},{1,5},{2,0},{3,7},{4,6},{5,1},{6,4},{7,3},{8,10},{9,13},{10,... | collective-permute-start | bytes 602120 | tf_op jit(solution)/shard_map/ppermute | solution.py:211
  20.9 0.6 %collective-permute-start.1 = (bf16[784,128]{1,0:T(8,128)(2,1)S(1)}, bf16[784,128]{1,0:T(8,128)(2,1)S(1)}, u32[]{:S(2)}, u32[]{:S(2)}) collective-permute-start(bf16[784,128]{1,0:T(8,128)(2,1)S(1)} %collective-permute-done), channel_id=1, source_target_pairs={{0,8},{1,9},{2,10},{3,11},{4,12},{5,13},{6,14},{7,15},{8,0},{9,1},... | collective-permute-start | bytes 602120 | tf_op jit(solution)/shard_map/ppermute | solution.py:211
  21.6 0.0 collective-permute-done.9
  21.6 0.6 collective-permute-start.10
  22.2 5.0 %collective-permute-done.4 = bf16[784,128]{1,0:T(8,128)(2,1)S(1)} collective-permute-done((bf16[784,128]{1,0:T(8,128)(2,1)S(1)}, bf16[784,128]{1,0:T(8,128)(2,1)S(1)}, u32[]{:S(2)}, u32[]{:S(2)}) %collective-permute-start.4) | collective-permute-done | bytes 200736 | tf_op jit(solution)/shard_map/ppermute | solution.py:211
  27.2 0.6 collective-permute-start.5
  27.8 0.0 collective-permute-done.1
  27.8 0.0 collective-permute-start.11
  27.8 0.0 collective-permute-done.14.refs_1_
  27.8 0.5 collective-permute-start.16
  28.3 0.0 collective-permute-done.15.refs_2_
  28.3 1.3 %collective-permute-start.2 = (bf16[784,128]{1,0:T(8,128)(2,1)S(1)}, bf16[784,128]{1,0:T(8,128)(2,1)S(1)}, u32[]{:S(2)}, u32[]{:S(2)}) collective-permute-start(bf16[784,128]{1,0:T(8,128)(2,1)S(1)} %collective-permute-done.1), channel_id=1, source_target_pairs={{0,2},{1,5},{2,0},{3,7},{4,6},{5,1},{6,4},{7,3},{8,10},{9,13},{10,... | collective-permute-start | bytes 602120 | tf_op jit(solution)/shard_map/ppermute | solution.py:211
  29.7 0.0 collective-permute-done.10.refs_1_
  29.7 0.0 collective-permute-start.12
  29.7 5.8 %collective-permute-done.2 = bf16[784,128]{1,0:T(8,128)(2,1)S(1)} collective-permute-done((bf16[784,128]{1,0:T(8,128)(2,1)S(1)}, bf16[784,128]{1,0:T(8,128)(2,1)S(1)}, u32[]{:S(2)}, u32[]{:S(2)}) %collective-permute-start.2) | collective-permute-done | bytes 200736 | tf_op jit(solution)/shard_map/ppermute | solution.py:211
  35.5 0.0 collective-permute-start.6
  35.5 1.8 %collective-permute-done.5.refs_1_ = bf16[1568,128]{1,0:T(8,128)(2,1)S(1)} collective-permute-done((bf16[1568,128]{1,0:T(8,128)(2,1)S(1)}, bf16[1568,128]{1,0:T(8,128)(2,1)S(1)}, u32[]{:S(2)}, u32[]{:S(2)}) %collective-permute-start.5) | collective-permute-done | bytes 401440 | tf_op jit(solution)/shard_map/ppermute | solution.py:211
  37.3 0.0 collective-permute-start.7
  37.3 0.0 collective-permute-done.11.refs_2_
  37.3 0.5 collective-permute-start.3
  37.8 0.0 collective-permute-done.16.refs_3_
  37.8 1.5 %collective-permute-start.17 = (bf16[784,128]{1,0:T(8,128)(2,1)S(1)}, bf16[784,128]{1,0:T(8,128)(2,1)S(1)}, u32[]{:S(2)}, u32[]{:S(2)}) collective-permute-start(bf16[784,128]{1,0:T(8,128)(2,1)S(1)} %collective-permute-done.2), channel_id=1, source_target_pairs={{0,4},{1,3},{2,6},{3,1},{4,0},{5,7},{6,2},{7,5},{8,12},{9,11},{10,... | collective-permute-start | bytes 602120 | tf_op jit(solution)/shard_map/ppermute | solution.py:211
  39.4 2.4 %shard_map.95 = (f32[16,1024,128]{2,1,0:T(8,128)S(1)}, s32[8,128]{1,0:T(8,128)S(1)}, bf16[4,256,128]{2,1,0:T(8,128)(2,1)S(1)}) custom-call(bf16[1568,128]{1,0:T(8,128)(2,1)S(1)} %pad_maximum_fusion.refs_0_, bf16[1568,128]{1,0:T(8,128)(2,1)S(1)} %collective-permute-done.14.refs_1_, bf16[1568,128]{1,0:T(8,128)(2,1)S(1)} %collective-permute-done.15.refs_2_, ...), custom_call_target="tpu_custom_call" | custom-call | tf_op jit(solution)/shard_map/pallas_call | solution.py:403
  41.8 0.0 collective-permute-done.12.refs_3_
  41.8 0.1 collective-permute-start.18
  41.9 2.7 %shard_map.96 = (f32[16,1024,128]{2,1,0:T(8,128)S(1)}, s32[8,128]{1,0:T(8,128)}) custom-call(bf16[1568,128]{1,0:T(8,128)(2,1)S(1)} %constant_dynamic-update-slice_fusion.4.refs_0_, bf16[1568,128]{1,0:T(8,128)(2,1)S(1)} %collective-permute-done.10.refs_1_, bf16[1568,128]{1,0:T(8,128)(2,1)S(1)} %collective-permute-done.11.refs_2_, ...), custom_call_target="tpu_custom_call", output_to_operand_aliasing={{0}: (4, {})} | custom-call | tf_op jit(solution)/shard_map/pallas_call | solution.py:411
  44.6 0.0 collective-permute-done.6.refs_2_
  44.6 0.0 collective-permute-done.7.refs_3_
  44.6 0.0 copy-start
  44.6 0.0 copy-start.1
  44.7 2.9 %shard_map.97 = (f32[16,1024,128]{2,1,0:T(8,128)S(1)}, s32[8,128]{1,0:T(8,128)S(1)}) custom-call(bf16[1568,128]{1,0:T(8,128)(2,1)S(1)} %constant_dynamic-update-slice_fusion.2.refs_0_, bf16[1568,128]{1,0:T(8,128)(2,1)S(1)} %collective-permute-done.5.refs_1_, bf16[1568,128]{1,0:T(8,128)(2,1)S(1)} %collective-permute-done.6.refs_2_, ...), custom_call_target="tpu_custom_call", output_to_operand_aliasing={{0}: (4, {})} | custom-call | tf_op jit(solution)/shard_map/pallas_call | solution.py:411
  47.6 0.0 collective-permute-done.3.value_ref
  47.7 0.5 collective-permute-start.19
  48.2 0.0 collective-permute-done.18.refs_2_
  48.2 1.4 %collective-permute-done.19.refs_3_ = bf16[1568,128]{1,0:T(8,128)(2,1)S(1)} collective-permute-done((bf16[1568,128]{1,0:T(8,128)(2,1)S(1)}, bf16[1568,128]{1,0:T(8,128)(2,1)S(1)}, u32[]{:S(2)}, u32[]{:S(2)}) %collective-permute-start.19) | collective-permute-done | bytes 401440 | tf_op jit(solution)/shard_map/ppermute | solution.py:211
  49.6 3.5 %shard_map.99 = (f32[16,1024,128]{2,1,0:T(8,128)S(1)}, s32[8,128]{1,0:T(8,128)}) custom-call(bf16[1568,128]{1,0:T(8,128)(2,1)S(1)} %constant_dynamic-update-slice_fusion.refs_0_, bf16[1568,128]{1,0:T(8,128)(2,1)S(1)} %pad_maximum_fusion.1.refs_1_, bf16[1568,128]{1,0:T(8,128)(2,1)S(1)} %collective-permute-done.18.refs_2_, ...), custom_call_target="tpu_custom_call", output_to_operand_aliasing={{0}: (4, {})} | custom-call | tf_op jit(solution)/shard_map/pallas_call | solution.py:411
  53.1 10.8 %shard_map.100 = (bf16[64,512]{1,0:T(8,128)(2,1)}, f32[512,512]{1,0:T(8,128)}, f32[512,512]{1,0:T(8,128)}) custom-call(f32[16,1024,128]{2,1,0:T(8,128)S(1)} %get-tuple-element.14.sums, bf16[4,256,128]{2,1,0:T(8,128)(2,1)S(1)} %get-tuple-element.15.vals, s32[8,128]{1,0:T(8,128)S(1)} %get-tuple-element.16.info_v, bf16[512,512]{1,0:T(8,128)(2,1)S(1)} %copy-done, ...), custom_call_target="tpu_custom_call" | custom-call | tf_op jit(solution)/shard_map/pallas_call | solution.py:426
  (13 shorter events, 0.2 us)
Async XLA Ops:
  1.3 0.7 %copy-start.2 = (s32[1,1,8]{2,1,0:T(1,128)S(1)}, s32[1,1,8]{2,1,0:T(1,128)}, u32[]{:S(2)}) copy-start(s32[1,1,8]{2,1,0:T(1,128)} %index_ref.1) | copy-start | bytes 100
  3.5 7.1 %collective-permute-start.13 = (bf16[784,128]{1,0:T(8,128)(2,1)S(1)}, bf16[784,128]{1,0:T(8,128)(2,1)S(1)}, u32[]{:S(2)}, u32[]{:S(2)}) collective-permute-start(bf16[784,128]{1,0:T(8,128)(2,1)S(1)} %shard_map.94), channel_id=1, source_target_pairs={{0,2},{1,5},{2,0},{3,7},{4,6},{5,1},{6,4},{7,3},{8,10},{9,13},{10,... | collective-permute-start | bytes 602120 | tf_op jit(solution)/shard_map/ppermute | solution.py:211
  6.5 7.0 %collective-permute-start.8 = (bf16[784,128]{1,0:T(8,128)(2,1)S(1)}, bf16[784,128]{1,0:T(8,128)(2,1)S(1)}, u32[]{:S(2)}, u32[]{:S(2)}) collective-permute-start(bf16[784,128]{1,0:T(8,128)(2,1)S(1)} %shard_map.94), channel_id=1, source_target_pairs={{0,8},{1,9},{2,10},{3,11},{4,12},{5,13},{6,14},{7,15},{8,0},{9,1},... | collective-permute-start | bytes 602120 | tf_op jit(solution)/shard_map/ppermute | solution.py:211
  8.1 11.3 %collective-permute-start = (bf16[784,128]{1,0:T(8,128)(2,1)S(1)}, bf16[784,128]{1,0:T(8,128)(2,1)S(1)}, u32[]{:S(2)}, u32[]{:S(2)}) collective-permute-start(bf16[784,128]{1,0:T(8,128)(2,1)S(1)} %shard_map.94), channel_id=1, source_target_pairs={{0,24},{1,25},{2,26},{3,27},{4,28},{5,29},{6,30},{7,31},{8,16},{9,... | collective-permute-start | bytes 602120 | tf_op jit(solution)/shard_map/ppermute | solution.py:211
  10.6 17.2 %collective-permute-start.14 = (bf16[1568,128]{1,0:T(8,128)(2,1)S(1)}, bf16[1568,128]{1,0:T(8,128)(2,1)S(1)}, u32[]{:S(2)}, u32[]{:S(2)}) collective-permute-start(bf16[1568,128]{1,0:T(8,128)(2,1)S(1)} %pad_maximum_fusion.refs_0_), channel_id=1, source_target_pairs={{0,4},{1,3},{2,6},{3,1},{4,0},{5,7},{6,2},{7,5},{8,12},{9,11},{10,... | collective-permute-start | bytes 1204232 | tf_op jit(solution)/shard_map/ppermute | solution.py:211
  12.3 16.0 %collective-permute-start.15 = (bf16[1568,128]{1,0:T(8,128)(2,1)S(1)}, bf16[1568,128]{1,0:T(8,128)(2,1)S(1)}, u32[]{:S(2)}, u32[]{:S(2)}) collective-permute-start(bf16[1568,128]{1,0:T(8,128)(2,1)S(1)} %pad_maximum_fusion.refs_0_), channel_id=1, source_target_pairs={{0,1},{1,0},{2,3},{3,2},{4,5},{5,4},{6,7},{7,6},{8,9},{9,8},{10,11... | collective-permute-start | bytes 1204232 | tf_op jit(solution)/shard_map/ppermute | solution.py:211
  13.5 8.1 %collective-permute-start.9 = (bf16[784,128]{1,0:T(8,128)(2,1)S(1)}, bf16[784,128]{1,0:T(8,128)(2,1)S(1)}, u32[]{:S(2)}, u32[]{:S(2)}) collective-permute-start(bf16[784,128]{1,0:T(8,128)(2,1)S(1)} %collective-permute-done.8), channel_id=1, source_target_pairs={{0,2},{1,5},{2,0},{3,7},{4,6},{5,1},{6,4},{7,3},{8,10},{9,13},{10,... | collective-permute-start | bytes 602120 | tf_op jit(solution)/shard_map/ppermute | solution.py:211
  19.4 7.8 %collective-permute-start.4 = (bf16[784,128]{1,0:T(8,128)(2,1)S(1)}, bf16[784,128]{1,0:T(8,128)(2,1)S(1)}, u32[]{:S(2)}, u32[]{:S(2)}) collective-permute-start(bf16[784,128]{1,0:T(8,128)(2,1)S(1)} %collective-permute-done), channel_id=1, source_target_pairs={{0,2},{1,5},{2,0},{3,7},{4,6},{5,1},{6,4},{7,3},{8,10},{9,13},{10,... | collective-permute-start | bytes 602120 | tf_op jit(solution)/shard_map/ppermute | solution.py:211
  20.9 6.9 %collective-permute-start.1 = (bf16[784,128]{1,0:T(8,128)(2,1)S(1)}, bf16[784,128]{1,0:T(8,128)(2,1)S(1)}, u32[]{:S(2)}, u32[]{:S(2)}) collective-permute-start(bf16[784,128]{1,0:T(8,128)(2,1)S(1)} %collective-permute-done), channel_id=1, source_target_pairs={{0,8},{1,9},{2,10},{3,11},{4,12},{5,13},{6,14},{7,15},{8,0},{9,1},... | collective-permute-start | bytes 602120 | tf_op jit(solution)/shard_map/ppermute | solution.py:211
  21.6 8.1 %collective-permute-start.10 = (bf16[1568,128]{1,0:T(8,128)(2,1)S(1)}, bf16[1568,128]{1,0:T(8,128)(2,1)S(1)}, u32[]{:S(2)}, u32[]{:S(2)}) collective-permute-start(bf16[1568,128]{1,0:T(8,128)(2,1)S(1)} %constant_dynamic-update-slice_fusion.4.refs_0_), channel_id=1, source_target_pairs={{0,4},{1,3},{2,6},{3,1},{4,0},{5,7},{6,2},{7,5},{8,12},{9,11},{10,... | collective-permute-start | bytes 1204232 | tf_op jit(solution)/shard_map/ppermute | solution.py:211
  27.2 10.1 %collective-permute-start.5 = (bf16[1568,128]{1,0:T(8,128)(2,1)S(1)}, bf16[1568,128]{1,0:T(8,128)(2,1)S(1)}, u32[]{:S(2)}, u32[]{:S(2)}) collective-permute-start(bf16[1568,128]{1,0:T(8,128)(2,1)S(1)} %constant_dynamic-update-slice_fusion.2.refs_0_), channel_id=1, source_target_pairs={{0,4},{1,3},{2,6},{3,1},{4,0},{5,7},{6,2},{7,5},{8,12},{9,11},{10,... | collective-permute-start | bytes 1204232 | tf_op jit(solution)/shard_map/ppermute | solution.py:211
  27.8 9.5 %collective-permute-start.11 = (bf16[1568,128]{1,0:T(8,128)(2,1)S(1)}, bf16[1568,128]{1,0:T(8,128)(2,1)S(1)}, u32[]{:S(2)}, u32[]{:S(2)}) collective-permute-start(bf16[1568,128]{1,0:T(8,128)(2,1)S(1)} %constant_dynamic-update-slice_fusion.4.refs_0_), channel_id=1, source_target_pairs={{0,1},{1,0},{2,3},{3,2},{4,5},{5,4},{6,7},{7,6},{8,9},{9,8},{10,11... | collective-permute-start | bytes 1204232 | tf_op jit(solution)/shard_map/ppermute | solution.py:211
  27.8 10.0 %collective-permute-start.16 = (bf16[1568,128]{1,0:T(8,128)(2,1)S(1)}, bf16[1568,128]{1,0:T(8,128)(2,1)S(1)}, u32[]{:S(2)}, u32[]{:S(2)}) collective-permute-start(bf16[1568,128]{1,0:T(8,128)(2,1)S(1)} %collective-permute-done.14.refs_1_), channel_id=1, source_target_pairs={{0,1},{1,0},{2,3},{3,2},{4,5},{5,4},{6,7},{7,6},{8,9},{9,8},{10,11... | collective-permute-start | bytes 1204232 | tf_op jit(solution)/shard_map/ppermute | solution.py:211
  28.3 7.1 %collective-permute-start.2 = (bf16[784,128]{1,0:T(8,128)(2,1)S(1)}, bf16[784,128]{1,0:T(8,128)(2,1)S(1)}, u32[]{:S(2)}, u32[]{:S(2)}) collective-permute-start(bf16[784,128]{1,0:T(8,128)(2,1)S(1)} %collective-permute-done.1), channel_id=1, source_target_pairs={{0,2},{1,5},{2,0},{3,7},{4,6},{5,1},{6,4},{7,3},{8,10},{9,13},{10,... | collective-permute-start | bytes 602120 | tf_op jit(solution)/shard_map/ppermute | solution.py:211
  29.7 12.2 %collective-permute-start.12 = (bf16[1568,128]{1,0:T(8,128)(2,1)S(1)}, bf16[1568,128]{1,0:T(8,128)(2,1)S(1)}, u32[]{:S(2)}, u32[]{:S(2)}) collective-permute-start(bf16[1568,128]{1,0:T(8,128)(2,1)S(1)} %collective-permute-done.10.refs_1_), channel_id=1, source_target_pairs={{0,1},{1,0},{2,3},{3,2},{4,5},{5,4},{6,7},{7,6},{8,9},{9,8},{10,11... | collective-permute-start | bytes 1204232 | tf_op jit(solution)/shard_map/ppermute | solution.py:211
  35.5 9.2 %collective-permute-start.6 = (bf16[1568,128]{1,0:T(8,128)(2,1)S(1)}, bf16[1568,128]{1,0:T(8,128)(2,1)S(1)}, u32[]{:S(2)}, u32[]{:S(2)}) collective-permute-start(bf16[1568,128]{1,0:T(8,128)(2,1)S(1)} %constant_dynamic-update-slice_fusion.2.refs_0_), channel_id=1, source_target_pairs={{0,1},{1,0},{2,3},{3,2},{4,5},{5,4},{6,7},{7,6},{8,9},{9,8},{10,11... | collective-permute-start | bytes 1204232 | tf_op jit(solution)/shard_map/ppermute | solution.py:211
  37.3 7.4 %collective-permute-start.7 = (bf16[1568,128]{1,0:T(8,128)(2,1)S(1)}, bf16[1568,128]{1,0:T(8,128)(2,1)S(1)}, u32[]{:S(2)}, u32[]{:S(2)}) collective-permute-start(bf16[1568,128]{1,0:T(8,128)(2,1)S(1)} %collective-permute-done.5.refs_1_), channel_id=1, source_target_pairs={{0,1},{1,0},{2,3},{3,2},{4,5},{5,4},{6,7},{7,6},{8,9},{9,8},{10,11... | collective-permute-start | bytes 1204232 | tf_op jit(solution)/shard_map/ppermute | solution.py:211
  37.3 10.3 %collective-permute-start.3 = (bf16[784,128]{1,0:T(8,128)(2,1)S(1)}, bf16[784,128]{1,0:T(8,128)(2,1)S(1)}, u32[]{:S(2)}, u32[]{:S(2)}) collective-permute-start(bf16[784,128]{1,0:T(8,128)(2,1)S(1)} %collective-permute-done.1), channel_id=1, source_target_pairs={{0,4},{1,3},{2,6},{3,1},{4,0},{5,7},{6,2},{7,5},{8,12},{9,11},{10,... | collective-permute-start | bytes 602120 | tf_op jit(solution)/shard_map/ppermute | solution.py:211
  37.8 9.8 %collective-permute-start.17 = (bf16[784,128]{1,0:T(8,128)(2,1)S(1)}, bf16[784,128]{1,0:T(8,128)(2,1)S(1)}, u32[]{:S(2)}, u32[]{:S(2)}) collective-permute-start(bf16[784,128]{1,0:T(8,128)(2,1)S(1)} %collective-permute-done.2), channel_id=1, source_target_pairs={{0,4},{1,3},{2,6},{3,1},{4,0},{5,7},{6,2},{7,5},{8,12},{9,11},{10,... | collective-permute-start | bytes 602120 | tf_op jit(solution)/shard_map/ppermute | solution.py:211
  41.8 6.4 %collective-permute-start.18 = (bf16[1568,128]{1,0:T(8,128)(2,1)S(1)}, bf16[1568,128]{1,0:T(8,128)(2,1)S(1)}, u32[]{:S(2)}, u32[]{:S(2)}) collective-permute-start(bf16[1568,128]{1,0:T(8,128)(2,1)S(1)} %constant_dynamic-update-slice_fusion.refs_0_), channel_id=1, source_target_pairs={{0,1},{1,0},{2,3},{3,2},{4,5},{5,4},{6,7},{7,6},{8,9},{9,8},{10,11... | collective-permute-start | bytes 1204232 | tf_op jit(solution)/shard_map/ppermute | solution.py:211
  44.6 8.5 %copy-start = (bf16[512,512]{1,0:T(8,128)(2,1)S(1)}, bf16[512,512]{1,0:T(8,128)(2,1)}, u32[]{:S(2)}) copy-start(bf16[512,512]{1,0:T(8,128)(2,1)} %w1_ref.1) | copy-start | bytes 1572868
  44.6 8.5 %copy-start.1 = (bf16[512,512]{1,0:T(8,128)(2,1)S(1)}, bf16[512,512]{1,0:T(8,128)(2,1)}, u32[]{:S(2)}) copy-start(bf16[512,512]{1,0:T(8,128)(2,1)} %w2_ref.1) | copy-start | bytes 1572868
  47.7 1.9 %collective-permute-start.19 = (bf16[1568,128]{1,0:T(8,128)(2,1)S(1)}, bf16[1568,128]{1,0:T(8,128)(2,1)S(1)}, u32[]{:S(2)}, u32[]{:S(2)}) collective-permute-start(bf16[1568,128]{1,0:T(8,128)(2,1)S(1)} %pad_maximum_fusion.1.refs_1_), channel_id=1, source_target_pairs={{0,1},{1,0},{2,3},{3,2},{4,5},{5,4},{6,7},{7,6},{8,9},{9,8},{10,11... | collective-permute-start | bytes 1204232 | tf_op jit(solution)/shard_map/ppermute | solution.py:211

commit v3 on v2

--- a/solution.py
+++ b/solution.py
@@ -108,6 +108,7 @@
 
 VMEM_SPEC = pl.BlockSpec(memory_space=pltpu.VMEM)
 VMEM_LIMIT = 12 * 1024 * 1024
+DENSE_LIMIT = 20 * 1024 * 1024
 SMALL_LIMIT = 2 * 1024 * 1024
 
 
@@ -136,6 +137,7 @@
             and self.n_col == 4
             and self.n_row % 2 == 0
             and self.n_row & (self.n_row - 1) == 0
+            and self.n_row >= 4
             and 2 * self.rows == self.block
             and self.blk_rows == 2
             and self.n_blocks % 2 == 0
@@ -196,7 +198,7 @@
     )(pltpu.with_memory_space_constraint(value, pltpu.VMEM), token)
 
 
-def collect(sz, payload):
+def collect(sz, payload, w_first):
     n_z = sz.n_row // 2
 
     def send(value, to):
@@ -219,34 +221,40 @@
     def sibling(z, y, x, c):
         return (z, y, x, 1 - c)
 
-    def plane(own, token):
-        one = send(own, first_way)
-        if token is not None:
-            two, three = hold(send(own, second_way), token), send(one, second_way)
-            near = jnp.concatenate([own, one], axis=0)
-            far = jnp.concatenate([two, three], axis=0)
-            return near, far, send(near, sibling), send(far, sibling)
-        near = jnp.concatenate([own, one], axis=0)
-        far = send(near, second_way)
-        return near, far, send(near, sibling), send(far, sibling)
-
     def flip(d):
         return lambda z, y, x, c: (z ^ d, y, x, c)
 
-    held = {0: payload}
-    low = 1
+    def pair(a, b):
+        return jnp.concatenate([a, b], axis=0)
+
+    def plane(near, far):
+        return near, far, send(near, sibling), send(far, sibling)
+
+    one = send(payload, first_way)
+    near = pair(payload, one)
+    planes = [(near, send(near, second_way))]
+    near = send(near, flip(1))
+    planes.append((near, send(near, second_way)))
+    sums, token, w1t = init(sz, w_first, one)
+
+    low = 2
     while low < n_z:
-        whole = 2 * low - 1
-        arrived = send(payload, flip(whole))
-        for d in list(held):
-            held[whole ^ d] = arrived if d == 0 else send(arrived, flip(d))
+        own = hold(send(payload, flip(2 * low - 1)), token)
+        one = send(own, first_way)
+        near = pair(own, one)
+        planes.append((near, pair(send(own, second_way), send(one, second_way))))
+        for d in range(1, low):
+            passed = send(near, flip(d))
+            planes.append((passed, send(passed, second_way)))
         low *= 2
-    order = sorted(held, key=lambda d: (d.bit_length(), -d))
-    sums = None
-    for d in order:
-        token = sums[1] if d == order[-1] else None
-        sums = add_plane(sz, plane(held[d], token), sums)
-    return sums
+
+    sums, info, vals = add_plane(sz, plane(*planes[0]), sums, True)
+    token = info
+    for near, far in planes[1:-1]:
+        sums, token = add_plane(sz, plane(near, far), sums, False)
+    near, far = planes[-1]
+    sums, token = add_plane(sz, plane(near, hold(far, token)), sums, False)
+    return sums, vals, info, w1t
 
 
 def place():
@@ -256,11 +264,9 @@
 
 def plane_kernel(sz, first, *refs):
     parts, refs = refs[:4], refs[4:]
-    if first:
-        sums, info_v, vals_out = refs[:3]
-    else:
-        sums, info_v = refs[1:3]
-    buf, info_s, turned, sem = refs[3:]
+    sums, info_v = refs[1:3]
+    vals_out = refs[3] if first else None
+    buf, info_s, turned, sem = refs[-4:]
     _, _, x, c = place()
     block, size = sz.block, sz.payload
 
@@ -285,7 +291,6 @@
     info_copy.start()
 
     if first:
-        sums[...] = jnp.zeros_like(sums)
         for m in range(2):
             for e in range(2):
                 vals_out[2 * m + e] = buf[m, e, pl.ds(sz.at_val, sz.live * block), :]
@@ -316,20 +321,23 @@
 
 
 def dense_kernel(
-    sz, sums, vals, info_v, w1_ref, w2_ref, out_ref, gf_ref, gs_ref, act, w1t, rows_out, info_s, sem
+    sz, sums, vals, info_v, w1t, w2_ref, out_ref, gf_ref, gs_ref, act, rows_out, info_s, sems, *wide
 ):
     block, width = sz.block, sz.width
     _, _, x, c = place()
-    info_copy = pltpu.make_async_copy(info_v, info_s, sem)
+    info_copy = pltpu.make_async_copy(info_v, info_s, sems.at[0])
     info_copy.start()
-    w1t[...] = jnp.transpose(w1_ref[...])
     nt = (((1,), (1,)), ((), ()))
-
-    def chunk(n, carry):
+    all_g, all_b, all_a, all_f, gs, gf = wide
+
+    for n in range(sz.n_blocks // 2):
+        lanes = pl.ds(2 * n * block, 2 * block)
         both = jnp.concatenate(
             [sums[2 * n].astype(jnp.bfloat16), sums[2 * n + 1].astype(jnp.bfloat16)], axis=1
         )
         g, b = both[:width], both[width:]
+        all_g[:, lanes] = g
+        all_b[:, lanes] = b
         v = jnp.dot(w1t[...], g, preferred_element_type=jnp.float32)
         sq = v * v
         t = jnp.tanh(GELU_C * (v + GELU_A * sq * v))
@@ -338,24 +346,16 @@
         slope = half + 0.5 * v * (1.0 - t * t) * (GELU_C * (1.0 + 3.0 * GELU_A * sq))
         act[2 * n] = a[:, :block]
         act[2 * n + 1] = a[:, block:]
+        all_a[:, lanes] = a
         back = jnp.dot(w2_ref[...], b, preferred_element_type=jnp.float32)
-        bf = (back * slope).astype(jnp.bfloat16)
-        gs = lax.dot_general(a, b, nt, preferred_element_type=jnp.float32)
-        gf = lax.dot_general(g, bf, nt, preferred_element_type=jnp.float32)
-
-        @pl.when(n == 0)
-        def _():
-            gs_ref[...] = gs
-            gf_ref[...] = gf
-
-        @pl.when(n > 0)
-        def _():
-            gs_ref[...] += gs
-            gf_ref[...] += gf
-
-        return carry
-
-    lax.fori_loop(0, sz.n_blocks // 2, chunk, 0)
+        all_f[:, lanes] = (back * slope).astype(jnp.bfloat16)
+
+    gs[...] = lax.dot_general(all_a[...], all_b[...], nt, preferred_element_type=jnp.float32)
+    gs_copy = pltpu.make_async_copy(gs, gs_ref, sems.at[1])
+    gs_copy.start()
+    gf[...] = lax.dot_general(all_g[...], all_f[...], nt, preferred_element_type=jnp.float32)
+    gf_copy = pltpu.make_async_copy(gf, gf_ref, sems.at[2])
+    gf_copy.start()
     info_copy.wait()
 
     rows_out[...] = jnp.zeros_like(rows_out)
@@ -383,13 +383,44 @@
     out += jnp.dot(low, w2_ref[...], preferred_element_type=jnp.float32)
     out = jnp.where(c == 0, out[: sz.rows], out[sz.rows :])
     out_ref[...] = out.astype(jnp.bfloat16)
-
-
-def add_plane(sz, parts, sums):
-    parts = [pltpu.with_memory_space_constraint(a, pltpu.VMEM) for a in parts]
-    sums_type = pltpu.VMEM((sz.n_blocks, 2 * sz.width, sz.block), jnp.float32)
-    token_type = pltpu.VMEM((8, sz.block), jnp.int32)
-    params = dict(
+    gs_copy.wait()
+    gf_copy.wait()
+
+
+def init_kernel(w1_ref, dep_ref, sums, token, w1t):
+    sums[...] = jnp.zeros_like(sums)
+    token[...] = jnp.zeros_like(token)
+    w1t[...] = jnp.transpose(w1_ref[...])
+
+
+def init(sz, w_first, dep):
+    return pl.pallas_call(
+        init_kernel,
+        out_shape=(
+            pltpu.VMEM((sz.n_blocks, 2 * sz.width, sz.block), jnp.float32),
+            pltpu.VMEM((8, sz.block), jnp.int32),
+            pltpu.VMEM((sz.width, sz.width), jnp.bfloat16),
+        ),
+        in_specs=[VMEM_SPEC, pl.BlockSpec(memory_space=pl.ANY)],
+        out_specs=[VMEM_SPEC] * 3,
+        compiler_params=pltpu.CompilerParams(vmem_limit_bytes=SMALL_LIMIT),
+    )(w_first, dep)
+
+
+def add_plane(sz, parts, sums, first):
+    parts = [pltpu.with_memory_space_constraint(a, pltpu.VMEM) for a in (*parts, sums)]
+    out_shape = [
+        pltpu.VMEM((sz.n_blocks, 2 * sz.width, sz.block), jnp.float32),
+        pltpu.VMEM((8, sz.block), jnp.int32),
+    ]
+    if first:
+        out_shape.append(pltpu.VMEM((4, sz.live * sz.block, sz.block), jnp.bfloat16))
+    return pl.pallas_call(
+        functools.partial(plane_kernel, sz, first),
+        out_shape=tuple(out_shape),
+        in_specs=[VMEM_SPEC] * 5,
+        out_specs=[VMEM_SPEC] * len(out_shape),
+        input_output_aliases={4: 0},
         scratch_shapes=[
             pltpu.VMEM((4, 2, sz.payload, sz.block), jnp.bfloat16),
             pltpu.SMEM((8, sz.block), jnp.int32),
@@ -397,53 +428,36 @@
             pltpu.SemaphoreType.DMA,
         ],
         compiler_params=pltpu.CompilerParams(vmem_limit_bytes=VMEM_LIMIT),
-    )
-    if sums is None:
-        vals_type = pltpu.VMEM((4, sz.live * sz.block, sz.block), jnp.bfloat16)
-        total, token, vals = pl.pallas_call(
-            functools.partial(plane_kernel, sz, True),
-            out_shape=(sums_type, token_type, vals_type),
-            in_specs=[VMEM_SPEC] * 4,
-            out_specs=[VMEM_SPEC] * 3,
-            **params,
-        )(*parts)
-        return total, token, vals, token
-    total, token = pl.pallas_call(
-        functools.partial(plane_kernel, sz, False),
-        out_shape=(sums_type, token_type),
-        in_specs=[VMEM_SPEC] * 5,
-        out_specs=[VMEM_SPEC] * 2,
-        input_output_aliases={4: 0},
-        **params,
-    )(*parts, pltpu.with_memory_space_constraint(sums[0], pltpu.VMEM))
-    return total, token, *sums[2:]
-
-
-def dense(sz, sums, vals, info, w_first, w_second):
+    )(*parts)
+
+
+def dense(sz, sums, vals, info, w1t, w_second):
     grad = jax.ShapeDtypeStruct((sz.width, sz.width), jnp.float32)
-    inputs = [pltpu.with_memory_space_constraint(a, pltpu.VMEM) for a in (sums, vals, info)]
+    inputs = [pltpu.with_memory_space_constraint(a, pltpu.VMEM) for a in (sums, vals, info, w1t)]
+    far = pl.BlockSpec(memory_space=pl.ANY)
     return tuple(
         pl.pallas_call(
             functools.partial(dense_kernel, sz),
             out_shape=(jax.ShapeDtypeStruct((sz.rows, sz.width), jnp.bfloat16), grad, grad),
             in_specs=[VMEM_SPEC] * 5,
-            out_specs=[VMEM_SPEC] * 3,
+            out_specs=[VMEM_SPEC, far, far],
             scratch_shapes=[
                 pltpu.VMEM((sz.n_blocks, sz.width, sz.block), jnp.bfloat16),
-                pltpu.VMEM((sz.width, sz.width), jnp.bfloat16),
                 pltpu.VMEM((sz.width, sz.block), jnp.float32),
                 pltpu.SMEM((8, sz.block), jnp.int32),
-                pltpu.SemaphoreType.DMA,
-            ],
-            compiler_params=pltpu.CompilerParams(vmem_limit_bytes=VMEM_LIMIT),
-        )(*inputs, w_first, w_second)
+                pltpu.SemaphoreType.DMA((3,)),
+            ]
+            + [pltpu.VMEM((sz.width, sz.nodes), jnp.bfloat16)] * 4
+            + [pltpu.VMEM((sz.width, sz.width), jnp.float32)] * 2,
+            compiler_params=pltpu.CompilerParams(vmem_limit_bytes=DENSE_LIMIT),
+        )(*inputs, w_second)
     )
 
 
 def replicated_local(sz, features, w_first, w_second, block_index, block_count, block_values, cotangent):
     payload = pack(sz, features, block_index, block_count, block_values, cotangent)
-    sums, _, vals, info = collect(sz, payload)
-    return dense(sz, sums, vals, info, w_first, w_second)
+    sums, vals, info, w1t = collect(sz, payload, w_first)
+    return dense(sz, sums, vals, info, w1t, w_second)
 
 
 def solution(mesh):

time: 63.5 us -> 57.4 us (0.904); the launches traced: 63.9 us -> 57.1 us
  waiting for transfers between devices: 20.1 us -> 15.9 us
  Pallas kernels: 23.9 us -> 20.4 us
  local copies, waits for them, and re-layouts: 0.79 us -> 1.74 us
    ppermute x20 -> x18, waiting for transfers between devices: 20.1 us -> 15.9 us  [send(): return lax.ppermute(value, AXES, pairs)]
    pallas_call x1, Pallas kernels: 10.8 us -> 7.63 us  [dense(): pl.pallas_call(functools.partial(dense_kernel, sz), out_shape=(jax.ShapeD...]
    unnamed x9 -> x7, local copies, waits for them, and re-layouts: 0.7 us -> 1.71 us
    pallas_call x4 -> x5, Pallas kernels: 11.6 us -> 11.2 us  [the longest x4 10.6 us: add_plane(): pl.pallas_call(functools.partial(plane_kernel, sz, first), out_shape=tupl...]
    ppermute x20 -> x18, starting transfers between devices: 17.5 us -> 17.4 us  [send(): return lax.ppermute(value, AXES, pairs)]
  transfers between devices with their start and end apart: 20 -> 18, of which waited for: 6 -> 6; matrix products, arithmetic and copies ran while one was open for 0% -> 0% of each run, Pallas kernels for 13% -> 15%
where the time goes in v3:
time: 57.4 us; the launch traced here: 57.1 us
  Pallas kernels  20.4 us (36%)
  starting transfers between devices  17.4 us (30%)
  waiting for transfers between devices  15.9 us (28%)
  local copies, waits for them, and re-layouts  1.74 us (3%)
  between operations  1.59 us (3%)
    ppermute x18, starting transfers between devices, send(): return lax.ppermute(value, AXES, pairs)  17.4 us
    ppermute x18, waiting for transfers between devices, send(): return lax.ppermute(value, AXES, pairs)  15.9 us
    pallas_call x4, Pallas kernels, add_plane(): pl.pallas_call(functools.partial(plane_kernel, sz, first), out_shape=tupl...  10.6 us
    pallas_call x1, Pallas kernels, dense(): pl.pallas_call(functools.partial(dense_kernel, sz), out_shape=(jax.ShapeD...  7.63 us
    unnamed x7, local copies, waits for them, and re-layouts  1.71 us
    pallas_call x1, Pallas kernels, pack(): pl.pallas_call(functools.partial(pack_kernel, sz), out_shape=pltpu.VMEM((...  1.53 us
  transfers between devices with their start and end apart: 18, of which 6 were waited for; matrix products, arithmetic and copies ran while one was open for 0% of the time, Pallas kernels for 15%

profile of v3, /device:TPU:0, one launch (start us, length us, event | category | flops | bytes accessed | tf_op | source)
XLA Modules:
  0.0 57.1 jit_solution(12487739484877375982)
XLA Ops:
  1.3 0.0 copy-start.2
  1.3 0.6 %copy-done.2 = s32[1,1,8]{2,1,0:T(1,128)S(1)} copy-done((s32[1,1,8]{2,1,0:T(1,128)S(1)}, s32[1,1,8]{2,1,0:T(1,128)}, u32[]{:S(2)}) %copy-start.2) | copy-done | bytes 56
  1.9 1.5 %shard_map.94 = bf16[784,128]{1,0:T(8,128)(2,1)S(1)} custom-call(s32[1,1,8]{2,1,0:T(1,128)S(1)} %copy-done.2, s32[1,1]{1,0:T(1,128)S(6)} %copy.23.count_ref, bf16[64,512]{1,0:T(8,128)(2,1)} %feat_ref.1, bf16[64,512]{1,0:T(8,128)(2,1)} %cot_ref.1, bf16[1,1,8,128,128]{4,3,2,1,0:T(8,128)(2,1)} %val_ref.1), custom_call_target="tpu_custom_call" | custom-call | tf_op jit(solution)/shard_map/pallas_call | solution.py:173
  3.5 3.0 %collective-permute-start.1 = (bf16[784,128]{1,0:T(8,128)(2,1)S(1)}, bf16[784,128]{1,0:T(8,128)(2,1)S(1)}, u32[]{:S(2)}, u32[]{:S(2)}) collective-permute-start(bf16[784,128]{1,0:T(8,128)(2,1)S(1)} %shard_map.94), channel_id=1, source_target_pairs={{0,2},{1,5},{2,0},{3,7},{4,6},{5,1},{6,4},{7,3},{8,10},{9,13},{10,... | collective-permute-start | bytes 602120 | tf_op jit(solution)/shard_map/ppermute | solution.py:213
  6.5 3.6 %collective-permute-start = (bf16[784,128]{1,0:T(8,128)(2,1)S(1)}, bf16[784,128]{1,0:T(8,128)(2,1)S(1)}, u32[]{:S(2)}, u32[]{:S(2)}) collective-permute-start(bf16[784,128]{1,0:T(8,128)(2,1)S(1)} %shard_map.94), channel_id=1, source_target_pairs={{0,24},{1,25},{2,26},{3,27},{4,28},{5,29},{6,30},{7,31},{8,16},{9,... | collective-permute-start | bytes 602120 | tf_op jit(solution)/shard_map/ppermute | solution.py:213
  10.1 0.1 collective-permute-done.1.dep_ref
  10.2 2.2 %collective-permute-start.9 = (bf16[1568,128]{1,0:T(8,128)(2,1)S(1)}, bf16[1568,128]{1,0:T(8,128)(2,1)S(1)}, u32[]{:S(2)}, u32[]{:S(2)}) collective-permute-start(bf16[1568,128]{1,0:T(8,128)(2,1)S(1)} %pad_maximum_fusion.1.refs_0_), channel_id=1, source_target_pairs={{0,8},{1,9},{2,10},{3,11},{4,12},{5,13},{6,14},{7,15},{8,0},{9,1},... | collective-permute-start | bytes 1204232 | tf_op jit(solution)/shard_map/ppermute | solution.py:213
  12.4 1.0 %copy-done.1 = bf16[512,512]{1,0:T(8,128)(2,1)S(1)} copy-done((bf16[512,512]{1,0:T(8,128)(2,1)S(1)}, bf16[512,512]{1,0:T(8,128)(2,1)}, u32[]{:S(2)}) %copy-start.1) | copy-done | bytes 524312
  13.4 0.7 %shard_map.95 = (f32[16,1024,128]{2,1,0:T(8,128)S(1)}, s32[8,128]{1,0:T(8,128)S(1)}, bf16[512,512]{1,0:T(8,128)(2,1)S(1)}) custom-call(bf16[512,512]{1,0:T(8,128)(2,1)S(1)} %copy-done.1, bf16[784,128]{1,0:T(8,128)(2,1)S(1)} %collective-permute-done.1.dep_ref), custom_call_target="tpu_custom_call" | custom-call | tf_op jit(solution)/shard_map/pallas_call | solution.py:397
  14.1 1.4 %collective-permute-done.value_ref = bf16[784,128]{1,0:T(8,128)(2,1)S(1)} collective-permute-done((bf16[784,128]{1,0:T(8,128)(2,1)S(1)}, bf16[784,128]{1,0:T(8,128)(2,1)S(1)}, u32[]{:S(2)}, u32[]{:S(2)}) %collective-permute-start) | collective-permute-done | bytes 200736 | tf_op jit(solution)/shard_map/ppermute | solution.py:213
  15.5 1.0 %collective-permute-start.2 = (bf16[784,128]{1,0:T(8,128)(2,1)S(1)}, bf16[784,128]{1,0:T(8,128)(2,1)S(1)}, u32[]{:S(2)}, u32[]{:S(2)}) collective-permute-start(bf16[784,128]{1,0:T(8,128)(2,1)S(1)} %shard_map.96), channel_id=1, source_target_pairs={{0,2},{1,5},{2,0},{3,7},{4,6},{5,1},{6,4},{7,3},{8,10},{9,13},{10,... | collective-permute-start | bytes 602120 | tf_op jit(solution)/shard_map/ppermute | solution.py:213
  16.5 1.0 %collective-permute-start.13 = (bf16[1568,128]{1,0:T(8,128)(2,1)S(1)}, bf16[1568,128]{1,0:T(8,128)(2,1)S(1)}, u32[]{:S(2)}, u32[]{:S(2)}) collective-permute-start(bf16[1568,128]{1,0:T(8,128)(2,1)S(1)} %pad_maximum_fusion.1.refs_0_), channel_id=1, source_target_pairs={{0,4},{1,3},{2,6},{3,1},{4,0},{5,7},{6,2},{7,5},{8,12},{9,11},{10,... | collective-permute-start | bytes 1204232 | tf_op jit(solution)/shard_map/ppermute | solution.py:213
  17.6 0.0 collective-permute-start.14
  17.6 1.0 %collective-permute-start.5 = (bf16[784,128]{1,0:T(8,128)(2,1)S(1)}, bf16[784,128]{1,0:T(8,128)(2,1)S(1)}, u32[]{:S(2)}, u32[]{:S(2)}) collective-permute-start(bf16[784,128]{1,0:T(8,128)(2,1)S(1)} %shard_map.96), channel_id=1, source_target_pairs={{0,4},{1,3},{2,6},{3,1},{4,0},{5,7},{6,2},{7,5},{8,12},{9,11},{10,... | collective-permute-start | bytes 602120 | tf_op jit(solution)/shard_map/ppermute | solution.py:213
  18.6 5.0 %collective-permute-done.9.refs_0_ = bf16[1568,128]{1,0:T(8,128)(2,1)S(1)} collective-permute-done((bf16[1568,128]{1,0:T(8,128)(2,1)S(1)}, bf16[1568,128]{1,0:T(8,128)(2,1)S(1)}, u32[]{:S(2)}, u32[]{:S(2)}) %collective-permute-start.9) | collective-permute-done | bytes 401440 | tf_op jit(solution)/shard_map/ppermute | solution.py:213
  23.5 0.6 %collective-permute-start.10 = (bf16[1568,128]{1,0:T(8,128)(2,1)S(1)}, bf16[1568,128]{1,0:T(8,128)(2,1)S(1)}, u32[]{:S(2)}, u32[]{:S(2)}) collective-permute-start(bf16[1568,128]{1,0:T(8,128)(2,1)S(1)} %collective-permute-done.9.refs_0_), channel_id=1, source_target_pairs={{0,4},{1,3},{2,6},{3,1},{4,0},{5,7},{6,2},{7,5},{8,12},{9,11},{10,... | collective-permute-start | bytes 1204232 | tf_op jit(solution)/shard_map/ppermute | solution.py:213
  24.2 0.0 collective-permute-done.2
  24.2 2.7 %collective-permute-start.3 = (bf16[1568,128]{1,0:T(8,128)(2,1)S(1)}, bf16[1568,128]{1,0:T(8,128)(2,1)S(1)}, u32[]{:S(2)}, u32[]{:S(2)}) collective-permute-start(bf16[1568,128]{1,0:T(8,128)(2,1)S(1)} %pad_maximum_fusion.refs_0_), channel_id=1, source_target_pairs={{0,8},{1,9},{2,10},{3,11},{4,12},{5,13},{6,14},{7,15},{8,0},{9,1},... | collective-permute-start | bytes 1204232 | tf_op jit(solution)/shard_map/ppermute | solution.py:213
  26.8 0.0 collective-permute-done.13.refs_1_
  26.9 0.0 collective-permute-start.15
  26.9 0.0 collective-permute-done.5
  26.9 0.7 %collective-permute-start.6 = (bf16[784,128]{1,0:T(8,128)(2,1)S(1)}, bf16[784,128]{1,0:T(8,128)(2,1)S(1)}, u32[]{:S(2)}, u32[]{:S(2)}) collective-permute-start(bf16[784,128]{1,0:T(8,128)(2,1)S(1)} %collective-permute-done.2), channel_id=1, source_target_pairs={{0,4},{1,3},{2,6},{3,1},{4,0},{5,7},{6,2},{7,5},{8,12},{9,11},{10,... | collective-permute-start | bytes 602120 | tf_op jit(solution)/shard_map/ppermute | solution.py:213
  27.6 5.9 %collective-permute-done.6 = bf16[784,128]{1,0:T(8,128)(2,1)S(1)} collective-permute-done((bf16[784,128]{1,0:T(8,128)(2,1)S(1)}, bf16[784,128]{1,0:T(8,128)(2,1)S(1)}, u32[]{:S(2)}, u32[]{:S(2)}) %collective-permute-start.6) | collective-permute-done | bytes 200736 | tf_op jit(solution)/shard_map/ppermute | solution.py:213
  33.5 0.0 collective-permute-start.11
  33.6 0.0 collective-permute-done.10.refs_1_
  33.6 0.6 %collective-permute-start.12 = (bf16[1568,128]{1,0:T(8,128)(2,1)S(1)}, bf16[1568,128]{1,0:T(8,128)(2,1)S(1)}, u32[]{:S(2)}, u32[]{:S(2)}) collective-permute-start(bf16[1568,128]{1,0:T(8,128)(2,1)S(1)} %collective-permute-done.10.refs_1_), channel_id=1, source_target_pairs={{0,1},{1,0},{2,3},{3,2},{4,5},{5,4},{6,7},{7,6},{8,9},{9,8},{10,11... | collective-permute-start | bytes 1204232 | tf_op jit(solution)/shard_map/ppermute | solution.py:213
  34.2 0.0 collective-permute-done.14.refs_2_
  34.2 0.1 collective-permute-start.7
  34.2 1.8 %collective-permute-done.3.refs_0_ = bf16[1568,128]{1,0:T(8,128)(2,1)S(1)} collective-permute-done((bf16[1568,128]{1,0:T(8,128)(2,1)S(1)}, bf16[1568,128]{1,0:T(8,128)(2,1)S(1)}, u32[]{:S(2)}, u32[]{:S(2)}) %collective-permute-start.3) | collective-permute-done | bytes 401440 | tf_op jit(solution)/shard_map/ppermute | solution.py:213
  36.0 0.0 collective-permute-start.8
  36.0 0.0 collective-permute-done.15.refs_3_
  36.0 0.1 collective-permute-start.4
  36.1 2.5 %shard_map.97 = (f32[16,1024,128]{2,1,0:T(8,128)S(1)}, s32[8,128]{1,0:T(8,128)S(1)}, bf16[4,256,128]{2,1,0:T(8,128)(2,1)S(1)}) custom-call(bf16[1568,128]{1,0:T(8,128)(2,1)S(1)} %pad_maximum_fusion.1.refs_0_, bf16[1568,128]{1,0:T(8,128)(2,1)S(1)} %collective-permute-done.13.refs_1_, ...), custom_call_target="tpu_custom_call", output_to_operand_aliasing={{0}: (4, {})} | custom-call | tf_op jit(solution)/shard_map/pallas_call | solution.py:418
  38.6 0.0 collective-permute-done.11.refs_2_
  38.7 0.7 %collective-permute-start.16 = (bf16[1568,128]{1,0:T(8,128)(2,1)S(1)}, bf16[1568,128]{1,0:T(8,128)(2,1)S(1)}, u32[]{:S(2)}, u32[]{:S(2)}) collective-permute-start(bf16[1568,128]{1,0:T(8,128)(2,1)S(1)} %collective-permute-done.3.refs_0_), channel_id=1, source_target_pairs={{0,1},{1,0},{2,3},{3,2},{4,5},{5,4},{6,7},{7,6},{8,9},{9,8},{10,11... | collective-permute-start | bytes 1204232 | tf_op jit(solution)/shard_map/ppermute | solution.py:213
  39.4 0.0 collective-permute-done.12.refs_3_
  39.4 2.9 %shard_map.98 = (f32[16,1024,128]{2,1,0:T(8,128)S(1)}, s32[8,128]{1,0:T(8,128)}) custom-call(bf16[1568,128]{1,0:T(8,128)(2,1)S(1)} %collective-permute-done.9.refs_0_, bf16[1568,128]{1,0:T(8,128)(2,1)S(1)} %collective-permute-done.10.refs_1_, bf16[1568,128]{1,0:T(8,128)(2,1)S(1)} %collective-permute-done.11.refs_2_, ...), custom_call_target="tpu_custom_call", output_to_operand_aliasing={{0}: (4, {})} | custom-call | tf_op jit(solution)/shard_map/pallas_call | solution.py:418
  42.3 0.0 collective-permute-done.7.refs_2_
  42.3 0.0 collective-permute-done.8.refs_3_
  42.3 0.0 copy-start
  42.3 2.3 %shard_map.99 = (f32[16,1024,128]{2,1,0:T(8,128)S(1)}, s32[8,128]{1,0:T(8,128)S(1)}) custom-call(bf16[1568,128]{1,0:T(8,128)(2,1)S(1)} %pad_maximum_fusion.refs_0_, bf16[1568,128]{1,0:T(8,128)(2,1)S(1)} %constant_dynamic-update-slice_fusion.refs_1_, bf16[1568,128]{1,0:T(8,128)(2,1)S(1)} %collective-permute-done.7.refs_2_, ...), custom_call_target="tpu_custom_call", output_to_operand_aliasing={{0}: (4, {})} | custom-call | tf_op jit(solution)/shard_map/pallas_call | solution.py:418
  44.6 0.0 collective-permute-done.4.value_ref
  44.7 0.1 collective-permute-start.17
  44.8 0.0 collective-permute-done.16.refs_2_
  44.8 1.7 %collective-permute-done.17.refs_3_ = bf16[1568,128]{1,0:T(8,128)(2,1)S(1)} collective-permute-done((bf16[1568,128]{1,0:T(8,128)(2,1)S(1)}, bf16[1568,128]{1,0:T(8,128)(2,1)S(1)}, u32[]{:S(2)}, u32[]{:S(2)}) %collective-permute-start.17) | collective-permute-done | bytes 401440 | tf_op jit(solution)/shard_map/ppermute | solution.py:213
  46.5 2.9 %shard_map.101 = (f32[16,1024,128]{2,1,0:T(8,128)S(1)}, s32[8,128]{1,0:T(8,128)}) custom-call(bf16[1568,128]{1,0:T(8,128)(2,1)S(1)} %collective-permute-done.3.refs_0_, bf16[1568,128]{1,0:T(8,128)(2,1)S(1)} %shard_map.100.refs_1_, bf16[1568,128]{1,0:T(8,128)(2,1)S(1)} %collective-permute-done.16.refs_2_, ...), custom_call_target="tpu_custom_call", output_to_operand_aliasing={{0}: (4, {})} | custom-call | tf_op jit(solution)/shard_map/pallas_call | solution.py:418
  49.3 0.0 copy-done
  49.3 7.6 %shard_map.102 = (bf16[64,512]{1,0:T(8,128)(2,1)}, f32[512,512]{1,0:T(8,128)}, f32[512,512]{1,0:T(8,128)}) custom-call(f32[16,1024,128]{2,1,0:T(8,128)S(1)} %get-tuple-element.19.sums, bf16[4,256,128]{2,1,0:T(8,128)(2,1)S(1)} %get-tuple-element.20.vals, s32[8,128]{1,0:T(8,128)S(1)} %get-tuple-element.21.info_v, bf16[512,512]{1,0:T(8,128)(2,1)S(1)} %get-tuple-element.22.w1t, ...), custom_call_target="tpu_custom_call" | custom-call | tf_op jit(solution)/shard_map/pallas_call | solution.py:439
  (7 shorter events, 0.1 us)
Async XLA Ops:
  1.3 0.7 %copy-start.2 = (s32[1,1,8]{2,1,0:T(1,128)S(1)}, s32[1,1,8]{2,1,0:T(1,128)}, u32[]{:S(2)}) copy-start(s32[1,1,8]{2,1,0:T(1,128)} %index_ref.1) | copy-start | bytes 100
  3.5 6.7 %collective-permute-start.1 = (bf16[784,128]{1,0:T(8,128)(2,1)S(1)}, bf16[784,128]{1,0:T(8,128)(2,1)S(1)}, u32[]{:S(2)}, u32[]{:S(2)}) collective-permute-start(bf16[784,128]{1,0:T(8,128)(2,1)S(1)} %shard_map.94), channel_id=1, source_target_pairs={{0,2},{1,5},{2,0},{3,7},{4,6},{5,1},{6,4},{7,3},{8,10},{9,13},{10,... | collective-permute-start | bytes 602120 | tf_op jit(solution)/shard_map/ppermute | solution.py:213
  6.5 9.0 %collective-permute-start = (bf16[784,128]{1,0:T(8,128)(2,1)S(1)}, bf16[784,128]{1,0:T(8,128)(2,1)S(1)}, u32[]{:S(2)}, u32[]{:S(2)}) collective-permute-start(bf16[784,128]{1,0:T(8,128)(2,1)S(1)} %shard_map.94), channel_id=1, source_target_pairs={{0,24},{1,25},{2,26},{3,27},{4,28},{5,29},{6,30},{7,31},{8,16},{9,... | collective-permute-start | bytes 602120 | tf_op jit(solution)/shard_map/ppermute | solution.py:213
  10.2 13.3 %collective-permute-start.9 = (bf16[1568,128]{1,0:T(8,128)(2,1)S(1)}, bf16[1568,128]{1,0:T(8,128)(2,1)S(1)}, u32[]{:S(2)}, u32[]{:S(2)}) collective-permute-start(bf16[1568,128]{1,0:T(8,128)(2,1)S(1)} %pad_maximum_fusion.1.refs_0_), channel_id=1, source_target_pairs={{0,8},{1,9},{2,10},{3,11},{4,12},{5,13},{6,14},{7,15},{8,0},{9,1},... | collective-permute-start | bytes 1204232 | tf_op jit(solution)/shard_map/ppermute | solution.py:213
  12.4 1.0 %copy-start.1 = (bf16[512,512]{1,0:T(8,128)(2,1)S(1)}, bf16[512,512]{1,0:T(8,128)(2,1)}, u32[]{:S(2)}) copy-start(bf16[512,512]{1,0:T(8,128)(2,1)} %w1_ref.1) | copy-start | bytes 1572868
  15.5 8.7 %collective-permute-start.2 = (bf16[784,128]{1,0:T(8,128)(2,1)S(1)}, bf16[784,128]{1,0:T(8,128)(2,1)S(1)}, u32[]{:S(2)}, u32[]{:S(2)}) collective-permute-start(bf16[784,128]{1,0:T(8,128)(2,1)S(1)} %shard_map.96), channel_id=1, source_target_pairs={{0,2},{1,5},{2,0},{3,7},{4,6},{5,1},{6,4},{7,3},{8,10},{9,13},{10,... | collective-permute-start | bytes 602120 | tf_op jit(solution)/shard_map/ppermute | solution.py:213
  16.5 10.3 %collective-permute-start.13 = (bf16[1568,128]{1,0:T(8,128)(2,1)S(1)}, bf16[1568,128]{1,0:T(8,128)(2,1)S(1)}, u32[]{:S(2)}, u32[]{:S(2)}) collective-permute-start(bf16[1568,128]{1,0:T(8,128)(2,1)S(1)} %pad_maximum_fusion.1.refs_0_), channel_id=1, source_target_pairs={{0,4},{1,3},{2,6},{3,1},{4,0},{5,7},{6,2},{7,5},{8,12},{9,11},{10,... | collective-permute-start | bytes 1204232 | tf_op jit(solution)/shard_map/ppermute | solution.py:213
  17.6 16.6 %collective-permute-start.14 = (bf16[1568,128]{1,0:T(8,128)(2,1)S(1)}, bf16[1568,128]{1,0:T(8,128)(2,1)S(1)}, u32[]{:S(2)}, u32[]{:S(2)}) collective-permute-start(bf16[1568,128]{1,0:T(8,128)(2,1)S(1)} %pad_maximum_fusion.1.refs_0_), channel_id=1, source_target_pairs={{0,1},{1,0},{2,3},{3,2},{4,5},{5,4},{6,7},{7,6},{8,9},{9,8},{10,11... | collective-permute-start | bytes 1204232 | tf_op jit(solution)/shard_map/ppermute | solution.py:213
  17.6 9.3 %collective-permute-start.5 = (bf16[784,128]{1,0:T(8,128)(2,1)S(1)}, bf16[784,128]{1,0:T(8,128)(2,1)S(1)}, u32[]{:S(2)}, u32[]{:S(2)}) collective-permute-start(bf16[784,128]{1,0:T(8,128)(2,1)S(1)} %shard_map.96), channel_id=1, source_target_pairs={{0,4},{1,3},{2,6},{3,1},{4,0},{5,7},{6,2},{7,5},{8,12},{9,11},{10,... | collective-permute-start | bytes 602120 | tf_op jit(solution)/shard_map/ppermute | solution.py:213
  23.5 10.1 %collective-permute-start.10 = (bf16[1568,128]{1,0:T(8,128)(2,1)S(1)}, bf16[1568,128]{1,0:T(8,128)(2,1)S(1)}, u32[]{:S(2)}, u32[]{:S(2)}) collective-permute-start(bf16[1568,128]{1,0:T(8,128)(2,1)S(1)} %collective-permute-done.9.refs_0_), channel_id=1, source_target_pairs={{0,4},{1,3},{2,6},{3,1},{4,0},{5,7},{6,2},{7,5},{8,12},{9,11},{10,... | collective-permute-start | bytes 1204232 | tf_op jit(solution)/shard_map/ppermute | solution.py:213
  24.2 11.8 %collective-permute-start.3 = (bf16[1568,128]{1,0:T(8,128)(2,1)S(1)}, bf16[1568,128]{1,0:T(8,128)(2,1)S(1)}, u32[]{:S(2)}, u32[]{:S(2)}) collective-permute-start(bf16[1568,128]{1,0:T(8,128)(2,1)S(1)} %pad_maximum_fusion.refs_0_), channel_id=1, source_target_pairs={{0,8},{1,9},{2,10},{3,11},{4,12},{5,13},{6,14},{7,15},{8,0},{9,1},... | collective-permute-start | bytes 1204232 | tf_op jit(solution)/shard_map/ppermute | solution.py:213
  26.9 9.2 %collective-permute-start.15 = (bf16[1568,128]{1,0:T(8,128)(2,1)S(1)}, bf16[1568,128]{1,0:T(8,128)(2,1)S(1)}, u32[]{:S(2)}, u32[]{:S(2)}) collective-permute-start(bf16[1568,128]{1,0:T(8,128)(2,1)S(1)} %collective-permute-done.13.refs_1_), channel_id=1, source_target_pairs={{0,1},{1,0},{2,3},{3,2},{4,5},{5,4},{6,7},{7,6},{8,9},{9,8},{10,11... | collective-permute-start | bytes 1204232 | tf_op jit(solution)/shard_map/ppermute | solution.py:213
  26.9 6.7 %collective-permute-start.6 = (bf16[784,128]{1,0:T(8,128)(2,1)S(1)}, bf16[784,128]{1,0:T(8,128)(2,1)S(1)}, u32[]{:S(2)}, u32[]{:S(2)}) collective-permute-start(bf16[784,128]{1,0:T(8,128)(2,1)S(1)} %collective-permute-done.2), channel_id=1, source_target_pairs={{0,4},{1,3},{2,6},{3,1},{4,0},{5,7},{6,2},{7,5},{8,12},{9,11},{10,... | collective-permute-start | bytes 602120 | tf_op jit(solution)/shard_map/ppermute | solution.py:213
  33.5 5.1 %collective-permute-start.11 = (bf16[1568,128]{1,0:T(8,128)(2,1)S(1)}, bf16[1568,128]{1,0:T(8,128)(2,1)S(1)}, u32[]{:S(2)}, u32[]{:S(2)}) collective-permute-start(bf16[1568,128]{1,0:T(8,128)(2,1)S(1)} %collective-permute-done.9.refs_0_), channel_id=1, source_target_pairs={{0,1},{1,0},{2,3},{3,2},{4,5},{5,4},{6,7},{7,6},{8,9},{9,8},{10,11... | collective-permute-start | bytes 1204232 | tf_op jit(solution)/shard_map/ppermute | solution.py:213
  33.6 5.8 %collective-permute-start.12 = (bf16[1568,128]{1,0:T(8,128)(2,1)S(1)}, bf16[1568,128]{1,0:T(8,128)(2,1)S(1)}, u32[]{:S(2)}, u32[]{:S(2)}) collective-permute-start(bf16[1568,128]{1,0:T(8,128)(2,1)S(1)} %collective-permute-done.10.refs_1_), channel_id=1, source_target_pairs={{0,1},{1,0},{2,3},{3,2},{4,5},{5,4},{6,7},{7,6},{8,9},{9,8},{10,11... | collective-permute-start | bytes 1204232 | tf_op jit(solution)/shard_map/ppermute | solution.py:213
  34.2 8.1 %collective-permute-start.7 = (bf16[1568,128]{1,0:T(8,128)(2,1)S(1)}, bf16[1568,128]{1,0:T(8,128)(2,1)S(1)}, u32[]{:S(2)}, u32[]{:S(2)}) collective-permute-start(bf16[1568,128]{1,0:T(8,128)(2,1)S(1)} %pad_maximum_fusion.refs_0_), channel_id=1, source_target_pairs={{0,1},{1,0},{2,3},{3,2},{4,5},{5,4},{6,7},{7,6},{8,9},{9,8},{10,11... | collective-permute-start | bytes 1204232 | tf_op jit(solution)/shard_map/ppermute | solution.py:213
  36.0 6.3 %collective-permute-start.8 = (bf16[1568,128]{1,0:T(8,128)(2,1)S(1)}, bf16[1568,128]{1,0:T(8,128)(2,1)S(1)}, u32[]{:S(2)}, u32[]{:S(2)}) collective-permute-start(bf16[1568,128]{1,0:T(8,128)(2,1)S(1)} %constant_dynamic-update-slice_fusion.refs_1_), channel_id=1, source_target_pairs={{0,1},{1,0},{2,3},{3,2},{4,5},{5,4},{6,7},{7,6},{8,9},{9,8},{10,11... | collective-permute-start | bytes 1204232 | tf_op jit(solution)/shard_map/ppermute | solution.py:213
  36.0 8.6 %collective-permute-start.4 = (bf16[1568,128]{1,0:T(8,128)(2,1)S(1)}, bf16[1568,128]{1,0:T(8,128)(2,1)S(1)}, u32[]{:S(2)}, u32[]{:S(2)}) collective-permute-start(bf16[1568,128]{1,0:T(8,128)(2,1)S(1)} %collective-permute-done.3.refs_0_), channel_id=1, source_target_pairs={{0,4},{1,3},{2,6},{3,1},{4,0},{5,7},{6,2},{7,5},{8,12},{9,11},{10,... | collective-permute-start | bytes 1204232 | tf_op jit(solution)/shard_map/ppermute | solution.py:213
  38.7 6.1 %collective-permute-start.16 = (bf16[1568,128]{1,0:T(8,128)(2,1)S(1)}, bf16[1568,128]{1,0:T(8,128)(2,1)S(1)}, u32[]{:S(2)}, u32[]{:S(2)}) collective-permute-start(bf16[1568,128]{1,0:T(8,128)(2,1)S(1)} %collective-permute-done.3.refs_0_), channel_id=1, source_target_pairs={{0,1},{1,0},{2,3},{3,2},{4,5},{5,4},{6,7},{7,6},{8,9},{9,8},{10,11... | collective-permute-start | bytes 1204232 | tf_op jit(solution)/shard_map/ppermute | solution.py:213
  42.3 7.0 %copy-start = (bf16[512,512]{1,0:T(8,128)(2,1)S(1)}, bf16[512,512]{1,0:T(8,128)(2,1)}, u32[]{:S(2)}) copy-start(bf16[512,512]{1,0:T(8,128)(2,1)} %w2_ref.1) | copy-start | bytes 1572868
  44.7 1.8 %collective-permute-start.17 = (bf16[1568,128]{1,0:T(8,128)(2,1)S(1)}, bf16[1568,128]{1,0:T(8,128)(2,1)S(1)}, u32[]{:S(2)}, u32[]{:S(2)}) collective-permute-start(bf16[1568,128]{1,0:T(8,128)(2,1)S(1)} %shard_map.100.refs_1_), channel_id=1, source_target_pairs={{0,1},{1,0},{2,3},{3,2},{4,5},{5,4},{6,7},{7,6},{8,9},{9,8},{10,11... | collective-permute-start | bytes 1204232 | tf_op jit(solution)/shard_map/ppermute | solution.py:213

commit v4 on v3

--- a/solution.py
+++ b/solution.py
@@ -144,7 +144,14 @@
         )
 
 
-def pack_kernel(sz, index_ref, count_ref, feat_ref, cot_ref, val_ref, out_ref, sems):
+def pack_kernel(
+    sz, index_ref, count_ref, feat_ref, cot_ref, val_ref, out_ref, index_s, small_sems, sems
+):
+    small = [
+        pltpu.make_async_copy(index_ref, index_s, small_sems.at[0]),
+    ]
+    for copy in small:
+        copy.start()
     copies = []
     for k in range(sz.chunks):
         lanes = pl.ds(k * sz.block, sz.block)
@@ -158,27 +165,32 @@
     ]
     for copy in copies:
         copy.start()
+    for copy in small:
+        copy.wait()
     lane = lax.broadcasted_iota(jnp.int32, (16, sz.block), 1)
     info = jnp.where(lane == 0, count_ref[0, 0], 0)
     for s in range(sz.live):
-        info = jnp.where(lane == s + 1, index_ref[0, 0, s], info)
+        info = jnp.where(lane == s + 1, index_s[0, 0, s], info)
     out_ref[pl.ds(sz.at_info, 16), :] = info.astype(jnp.float32).astype(jnp.bfloat16)
     for copy in copies:
         copy.wait()
 
 
 def pack(sz, features, block_index, block_count, block_values, cotangent):
-    smem = pl.BlockSpec(memory_space=pltpu.SMEM)
     far = pl.BlockSpec(memory_space=pl.ANY)
     return pl.pallas_call(
         functools.partial(pack_kernel, sz),
         out_shape=pltpu.VMEM((sz.payload, sz.block), jnp.bfloat16),
-        in_specs=[smem, smem, far, far, far],
+        in_specs=[far, pl.BlockSpec(memory_space=pltpu.SMEM), far, far, far],
         out_specs=VMEM_SPEC,
-        scratch_shapes=[pltpu.SemaphoreType.DMA((2 * sz.chunks + sz.live,))],
+        scratch_shapes=[
+            pltpu.SMEM(block_index.shape, jnp.int32),
+            pltpu.SemaphoreType.DMA((1,)),
+            pltpu.SemaphoreType.DMA((2 * sz.chunks + sz.live,)),
+        ],
         compiler_params=pltpu.CompilerParams(vmem_limit_bytes=SMALL_LIMIT),
     )(
-        block_index,
+        pltpu.with_memory_space_constraint(block_index, pltpu.HBM),
         block_count,
         *(
             pltpu.with_memory_space_constraint(a, pltpu.HBM)
@@ -339,11 +351,11 @@
         all_g[:, lanes] = g
         all_b[:, lanes] = b
         v = jnp.dot(w1t[...], g, preferred_element_type=jnp.float32)
-        sq = v * v
-        t = jnp.tanh(GELU_C * (v + GELU_A * sq * v))
-        half = 0.5 * (1.0 + t)
-        a = (v * half).astype(jnp.bfloat16)
-        slope = half + 0.5 * v * (1.0 - t * t) * (GELU_C * (1.0 + 3.0 * GELU_A * sq))
+        p = GELU_C + (GELU_C * GELU_A) * (v * v)
+        half = 0.5 + 0.5 * jnp.tanh(v * p)
+        value = v * half
+        slope = half + (value * (1.0 - half)) * (6.0 * p - 4.0 * GELU_C)
+        a = value.astype(jnp.bfloat16)
         act[2 * n] = a[:, :block]
         act[2 * n + 1] = a[:, block:]
         all_a[:, lanes] = a

time: 57.4 us -> 55.1 us (0.960)
  Pallas kernels: 20.4 us -> 18.7 us
  local copies, waits for them, and re-layouts: 1.74 us -> 1.09 us
    unnamed x7 -> x5, local copies, waits for them, and re-layouts: 1.71 us -> 1.06 us
    pallas_call x4, Pallas kernels: 10.6 us -> 9.96 us  [add_plane(): pl.pallas_call(functools.partial(plane_kernel, sz, first), out_shape=tupl...]
where the time goes in v4:
time: 55.1 us; the launch traced here: 54.8 us
  Pallas kernels  18.7 us (34%)
  starting transfers between devices  17.4 us (32%)
  waiting for transfers between devices  15.9 us (29%)
  between operations  1.58 us (3%)
  local copies, waits for them, and re-layouts  1.09 us (2%)
    ppermute x18, starting transfers between devices, send(): return lax.ppermute(value, AXES, pairs)  17.4 us
    ppermute x18, waiting for transfers between devices, send(): return lax.ppermute(value, AXES, pairs)  15.9 us
    pallas_call x4, Pallas kernels, add_plane(): pl.pallas_call(functools.partial(plane_kernel, sz, first), out_shape=tupl...  9.96 us
    pallas_call x1, Pallas kernels, dense(): pl.pallas_call(functools.partial(dense_kernel, sz), out_shape=(jax.ShapeD...  7.1 us
  transfers between devices with their start and end apart: 18, of which 6 were waited for; matrix products, arithmetic and copies ran while one was open for 0% of the time, Pallas kernels for 15%

profile of v4, /device:TPU:0, one launch (start us, length us, event | category | flops | bytes accessed | tf_op | source)
XLA Modules:
  0.0 54.8 jit_solution(7883093135356481210)
XLA Ops:
  1.3 1.0 %shard_map.94 = bf16[784,128]{1,0:T(8,128)(2,1)S(1)} custom-call(s32[1,1,8]{2,1,0:T(1,128)} %index_ref.1, s32[1,1]{1,0:T(1,128)S(6)} %copy.23.count_ref, bf16[64,512]{1,0:T(8,128)(2,1)} %feat_ref.1, bf16[64,512]{1,0:T(8,128)(2,1)} %cot_ref.1, bf16[1,1,8,128,128]{4,3,2,1,0:T(8,128)(2,1)} %val_ref.1), custom_call_target="tpu_custom_call" | custom-call | tf_op jit(solution)/shard_map/pallas_call | solution.py:181
  2.3 3.0 %collective-permute-start.1 = (bf16[784,128]{1,0:T(8,128)(2,1)S(1)}, bf16[784,128]{1,0:T(8,128)(2,1)S(1)}, u32[]{:S(2)}, u32[]{:S(2)}) collective-permute-start(bf16[784,128]{1,0:T(8,128)(2,1)S(1)} %shard_map.94), channel_id=1, source_target_pairs={{0,2},{1,5},{2,0},{3,7},{4,6},{5,1},{6,4},{7,3},{8,10},{9,13},{10,... | collective-permute-start | bytes 602120 | tf_op jit(solution)/shard_map/ppermute | solution.py:225
  5.3 3.6 %collective-permute-start = (bf16[784,128]{1,0:T(8,128)(2,1)S(1)}, bf16[784,128]{1,0:T(8,128)(2,1)S(1)}, u32[]{:S(2)}, u32[]{:S(2)}) collective-permute-start(bf16[784,128]{1,0:T(8,128)(2,1)S(1)} %shard_map.94), channel_id=1, source_target_pairs={{0,24},{1,25},{2,26},{3,27},{4,28},{5,29},{6,30},{7,31},{8,16},{9,... | collective-permute-start | bytes 602120 | tf_op jit(solution)/shard_map/ppermute | solution.py:225
  8.9 0.1 collective-permute-done.1.dep_ref
  9.0 2.2 %collective-permute-start.9 = (bf16[1568,128]{1,0:T(8,128)(2,1)S(1)}, bf16[1568,128]{1,0:T(8,128)(2,1)S(1)}, u32[]{:S(2)}, u32[]{:S(2)}) collective-permute-start(bf16[1568,128]{1,0:T(8,128)(2,1)S(1)} %pad_maximum_fusion.1.refs_0_), channel_id=1, source_target_pairs={{0,8},{1,9},{2,10},{3,11},{4,12},{5,13},{6,14},{7,15},{8,0},{9,1},... | collective-permute-start | bytes 1204232 | tf_op jit(solution)/shard_map/ppermute | solution.py:225
  11.2 0.0 copy-start.1
  11.2 1.0 %copy-done.1 = bf16[512,512]{1,0:T(8,128)(2,1)S(1)} copy-done((bf16[512,512]{1,0:T(8,128)(2,1)S(1)}, bf16[512,512]{1,0:T(8,128)(2,1)}, u32[]{:S(2)}) %copy-start.1) | copy-done | bytes 524312
  12.2 0.7 %shard_map.95 = (f32[16,1024,128]{2,1,0:T(8,128)S(1)}, s32[8,128]{1,0:T(8,128)S(1)}, bf16[512,512]{1,0:T(8,128)(2,1)S(1)}) custom-call(bf16[512,512]{1,0:T(8,128)(2,1)S(1)} %copy-done.1, bf16[784,128]{1,0:T(8,128)(2,1)S(1)} %collective-permute-done.1.dep_ref), custom_call_target="tpu_custom_call" | custom-call | tf_op jit(solution)/shard_map/pallas_call | solution.py:409
  12.9 1.4 %collective-permute-done.value_ref = bf16[784,128]{1,0:T(8,128)(2,1)S(1)} collective-permute-done((bf16[784,128]{1,0:T(8,128)(2,1)S(1)}, bf16[784,128]{1,0:T(8,128)(2,1)S(1)}, u32[]{:S(2)}, u32[]{:S(2)}) %collective-permute-start) | collective-permute-done | bytes 200736 | tf_op jit(solution)/shard_map/ppermute | solution.py:225
  14.3 1.0 %collective-permute-start.2 = (bf16[784,128]{1,0:T(8,128)(2,1)S(1)}, bf16[784,128]{1,0:T(8,128)(2,1)S(1)}, u32[]{:S(2)}, u32[]{:S(2)}) collective-permute-start(bf16[784,128]{1,0:T(8,128)(2,1)S(1)} %shard_map.96), channel_id=1, source_target_pairs={{0,2},{1,5},{2,0},{3,7},{4,6},{5,1},{6,4},{7,3},{8,10},{9,13},{10,... | collective-permute-start | bytes 602120 | tf_op jit(solution)/shard_map/ppermute | solution.py:225
  15.3 1.0 %collective-permute-start.13 = (bf16[1568,128]{1,0:T(8,128)(2,1)S(1)}, bf16[1568,128]{1,0:T(8,128)(2,1)S(1)}, u32[]{:S(2)}, u32[]{:S(2)}) collective-permute-start(bf16[1568,128]{1,0:T(8,128)(2,1)S(1)} %pad_maximum_fusion.1.refs_0_), channel_id=1, source_target_pairs={{0,4},{1,3},{2,6},{3,1},{4,0},{5,7},{6,2},{7,5},{8,12},{9,11},{10,... | collective-permute-start | bytes 1204232 | tf_op jit(solution)/shard_map/ppermute | solution.py:225
  16.4 0.0 collective-permute-start.14
  16.4 1.0 %collective-permute-start.5 = (bf16[784,128]{1,0:T(8,128)(2,1)S(1)}, bf16[784,128]{1,0:T(8,128)(2,1)S(1)}, u32[]{:S(2)}, u32[]{:S(2)}) collective-permute-start(bf16[784,128]{1,0:T(8,128)(2,1)S(1)} %shard_map.96), channel_id=1, source_target_pairs={{0,4},{1,3},{2,6},{3,1},{4,0},{5,7},{6,2},{7,5},{8,12},{9,11},{10,... | collective-permute-start | bytes 602120 | tf_op jit(solution)/shard_map/ppermute | solution.py:225
  17.4 5.0 %collective-permute-done.9.refs_0_ = bf16[1568,128]{1,0:T(8,128)(2,1)S(1)} collective-permute-done((bf16[1568,128]{1,0:T(8,128)(2,1)S(1)}, bf16[1568,128]{1,0:T(8,128)(2,1)S(1)}, u32[]{:S(2)}, u32[]{:S(2)}) %collective-permute-start.9) | collective-permute-done | bytes 401440 | tf_op jit(solution)/shard_map/ppermute | solution.py:225
  22.3 0.6 %collective-permute-start.10 = (bf16[1568,128]{1,0:T(8,128)(2,1)S(1)}, bf16[1568,128]{1,0:T(8,128)(2,1)S(1)}, u32[]{:S(2)}, u32[]{:S(2)}) collective-permute-start(bf16[1568,128]{1,0:T(8,128)(2,1)S(1)} %collective-permute-done.9.refs_0_), channel_id=1, source_target_pairs={{0,4},{1,3},{2,6},{3,1},{4,0},{5,7},{6,2},{7,5},{8,12},{9,11},{10,... | collective-permute-start | bytes 1204232 | tf_op jit(solution)/shard_map/ppermute | solution.py:225
  23.0 0.0 collective-permute-done.2
  23.0 2.7 %collective-permute-start.3 = (bf16[1568,128]{1,0:T(8,128)(2,1)S(1)}, bf16[1568,128]{1,0:T(8,128)(2,1)S(1)}, u32[]{:S(2)}, u32[]{:S(2)}) collective-permute-start(bf16[1568,128]{1,0:T(8,128)(2,1)S(1)} %pad_maximum_fusion.refs_0_), channel_id=1, source_target_pairs={{0,8},{1,9},{2,10},{3,11},{4,12},{5,13},{6,14},{7,15},{8,0},{9,1},... | collective-permute-start | bytes 1204232 | tf_op jit(solution)/shard_map/ppermute | solution.py:225
  25.7 0.0 collective-permute-done.13.refs_1_
  25.7 0.0 collective-permute-start.15
  25.7 0.0 collective-permute-done.5
  25.7 0.7 %collective-permute-start.6 = (bf16[784,128]{1,0:T(8,128)(2,1)S(1)}, bf16[784,128]{1,0:T(8,128)(2,1)S(1)}, u32[]{:S(2)}, u32[]{:S(2)}) collective-permute-start(bf16[784,128]{1,0:T(8,128)(2,1)S(1)} %collective-permute-done.2), channel_id=1, source_target_pairs={{0,4},{1,3},{2,6},{3,1},{4,0},{5,7},{6,2},{7,5},{8,12},{9,11},{10,... | collective-permute-start | bytes 602120 | tf_op jit(solution)/shard_map/ppermute | solution.py:225
  26.4 5.9 %collective-permute-done.6 = bf16[784,128]{1,0:T(8,128)(2,1)S(1)} collective-permute-done((bf16[784,128]{1,0:T(8,128)(2,1)S(1)}, bf16[784,128]{1,0:T(8,128)(2,1)S(1)}, u32[]{:S(2)}, u32[]{:S(2)}) %collective-permute-start.6) | collective-permute-done | bytes 200736 | tf_op jit(solution)/shard_map/ppermute | solution.py:225
  32.3 0.0 collective-permute-start.11
  32.4 0.0 collective-permute-done.10.refs_1_
  32.4 0.6 %collective-permute-start.12 = (bf16[1568,128]{1,0:T(8,128)(2,1)S(1)}, bf16[1568,128]{1,0:T(8,128)(2,1)S(1)}, u32[]{:S(2)}, u32[]{:S(2)}) collective-permute-start(bf16[1568,128]{1,0:T(8,128)(2,1)S(1)} %collective-permute-done.10.refs_1_), channel_id=1, source_target_pairs={{0,1},{1,0},{2,3},{3,2},{4,5},{5,4},{6,7},{7,6},{8,9},{9,8},{10,11... | collective-permute-start | bytes 1204232 | tf_op jit(solution)/shard_map/ppermute | solution.py:225
  33.0 0.0 collective-permute-done.14.refs_2_
  33.0 0.1 collective-permute-start.7
  33.1 1.8 %collective-permute-done.3.refs_0_ = bf16[1568,128]{1,0:T(8,128)(2,1)S(1)} collective-permute-done((bf16[1568,128]{1,0:T(8,128)(2,1)S(1)}, bf16[1568,128]{1,0:T(8,128)(2,1)S(1)}, u32[]{:S(2)}, u32[]{:S(2)}) %collective-permute-start.3) | collective-permute-done | bytes 401440 | tf_op jit(solution)/shard_map/ppermute | solution.py:225
  34.9 0.0 collective-permute-start.8
  34.9 0.0 collective-permute-done.15.refs_3_
  34.9 0.1 collective-permute-start.4
  34.9 1.9 %shard_map.97 = (f32[16,1024,128]{2,1,0:T(8,128)S(1)}, s32[8,128]{1,0:T(8,128)S(1)}, bf16[4,256,128]{2,1,0:T(8,128)(2,1)S(1)}) custom-call(bf16[1568,128]{1,0:T(8,128)(2,1)S(1)} %pad_maximum_fusion.1.refs_0_, bf16[1568,128]{1,0:T(8,128)(2,1)S(1)} %collective-permute-done.13.refs_1_, ...), custom_call_target="tpu_custom_call", output_to_operand_aliasing={{0}: (4, {})} | custom-call | tf_op jit(solution)/shard_map/pallas_call | solution.py:430
  36.9 0.0 collective-permute-done.11.refs_2_
  36.9 0.7 %collective-permute-start.16 = (bf16[1568,128]{1,0:T(8,128)(2,1)S(1)}, bf16[1568,128]{1,0:T(8,128)(2,1)S(1)}, u32[]{:S(2)}, u32[]{:S(2)}) collective-permute-start(bf16[1568,128]{1,0:T(8,128)(2,1)S(1)} %collective-permute-done.3.refs_0_), channel_id=1, source_target_pairs={{0,1},{1,0},{2,3},{3,2},{4,5},{5,4},{6,7},{7,6},{8,9},{9,8},{10,11... | collective-permute-start | bytes 1204232 | tf_op jit(solution)/shard_map/ppermute | solution.py:225
  37.6 0.0 collective-permute-done.12.refs_3_
  37.6 3.3 %shard_map.98 = (f32[16,1024,128]{2,1,0:T(8,128)S(1)}, s32[8,128]{1,0:T(8,128)}) custom-call(bf16[1568,128]{1,0:T(8,128)(2,1)S(1)} %collective-permute-done.9.refs_0_, bf16[1568,128]{1,0:T(8,128)(2,1)S(1)} %collective-permute-done.10.refs_1_, bf16[1568,128]{1,0:T(8,128)(2,1)S(1)} %collective-permute-done.11.refs_2_, ...), custom_call_target="tpu_custom_call", output_to_operand_aliasing={{0}: (4, {})} | custom-call | tf_op jit(solution)/shard_map/pallas_call | solution.py:430
  40.9 0.0 collective-permute-done.7.refs_2_
  40.9 0.0 collective-permute-done.8.refs_3_
  40.9 0.0 copy-start
  41.0 2.1 %shard_map.99 = (f32[16,1024,128]{2,1,0:T(8,128)S(1)}, s32[8,128]{1,0:T(8,128)S(1)}) custom-call(bf16[1568,128]{1,0:T(8,128)(2,1)S(1)} %pad_maximum_fusion.refs_0_, bf16[1568,128]{1,0:T(8,128)(2,1)S(1)} %constant_dynamic-update-slice_fusion.refs_1_, bf16[1568,128]{1,0:T(8,128)(2,1)S(1)} %collective-permute-done.7.refs_2_, ...), custom_call_target="tpu_custom_call", output_to_operand_aliasing={{0}: (4, {})} | custom-call | tf_op jit(solution)/shard_map/pallas_call | solution.py:430
  43.1 0.0 collective-permute-done.4.value_ref
  43.1 0.1 collective-permute-start.17
  43.2 0.0 collective-permute-done.16.refs_2_
  43.2 1.7 %collective-permute-done.17.refs_3_ = bf16[1568,128]{1,0:T(8,128)(2,1)S(1)} collective-permute-done((bf16[1568,128]{1,0:T(8,128)(2,1)S(1)}, bf16[1568,128]{1,0:T(8,128)(2,1)S(1)}, u32[]{:S(2)}, u32[]{:S(2)}) %collective-permute-start.17) | collective-permute-done | bytes 401440 | tf_op jit(solution)/shard_map/ppermute | solution.py:225
  44.9 2.7 %shard_map.101 = (f32[16,1024,128]{2,1,0:T(8,128)S(1)}, s32[8,128]{1,0:T(8,128)}) custom-call(bf16[1568,128]{1,0:T(8,128)(2,1)S(1)} %collective-permute-done.3.refs_0_, bf16[1568,128]{1,0:T(8,128)(2,1)S(1)} %shard_map.100.refs_1_, bf16[1568,128]{1,0:T(8,128)(2,1)S(1)} %collective-permute-done.16.refs_2_, ...), custom_call_target="tpu_custom_call", output_to_operand_aliasing={{0}: (4, {})} | custom-call | tf_op jit(solution)/shard_map/pallas_call | solution.py:430
  47.5 0.0 copy-done
  47.6 7.1 %shard_map.102 = (bf16[64,512]{1,0:T(8,128)(2,1)}, f32[512,512]{1,0:T(8,128)}, f32[512,512]{1,0:T(8,128)}) custom-call(f32[16,1024,128]{2,1,0:T(8,128)S(1)} %get-tuple-element.19.sums, bf16[4,256,128]{2,1,0:T(8,128)(2,1)S(1)} %get-tuple-element.20.vals, s32[8,128]{1,0:T(8,128)S(1)} %get-tuple-element.21.info_v, bf16[512,512]{1,0:T(8,128)(2,1)S(1)} %get-tuple-element.22.w1t, ...), custom_call_target="tpu_custom_call" | custom-call | tf_op jit(solution)/shard_map/pallas_call | solution.py:451
  (6 shorter events, 0.1 us)
Async XLA Ops:
  2.3 6.7 %collective-permute-start.1 = (bf16[784,128]{1,0:T(8,128)(2,1)S(1)}, bf16[784,128]{1,0:T(8,128)(2,1)S(1)}, u32[]{:S(2)}, u32[]{:S(2)}) collective-permute-start(bf16[784,128]{1,0:T(8,128)(2,1)S(1)} %shard_map.94), channel_id=1, source_target_pairs={{0,2},{1,5},{2,0},{3,7},{4,6},{5,1},{6,4},{7,3},{8,10},{9,13},{10,... | collective-permute-start | bytes 602120 | tf_op jit(solution)/shard_map/ppermute | solution.py:225
  5.3 9.0 %collective-permute-start = (bf16[784,128]{1,0:T(8,128)(2,1)S(1)}, bf16[784,128]{1,0:T(8,128)(2,1)S(1)}, u32[]{:S(2)}, u32[]{:S(2)}) collective-permute-start(bf16[784,128]{1,0:T(8,128)(2,1)S(1)} %shard_map.94), channel_id=1, source_target_pairs={{0,24},{1,25},{2,26},{3,27},{4,28},{5,29},{6,30},{7,31},{8,16},{9,... | collective-permute-start | bytes 602120 | tf_op jit(solution)/shard_map/ppermute | solution.py:225
  9.0 13.3 %collective-permute-start.9 = (bf16[1568,128]{1,0:T(8,128)(2,1)S(1)}, bf16[1568,128]{1,0:T(8,128)(2,1)S(1)}, u32[]{:S(2)}, u32[]{:S(2)}) collective-permute-start(bf16[1568,128]{1,0:T(8,128)(2,1)S(1)} %pad_maximum_fusion.1.refs_0_), channel_id=1, source_target_pairs={{0,8},{1,9},{2,10},{3,11},{4,12},{5,13},{6,14},{7,15},{8,0},{9,1},... | collective-permute-start | bytes 1204232 | tf_op jit(solution)/shard_map/ppermute | solution.py:225
  11.2 1.0 %copy-start.1 = (bf16[512,512]{1,0:T(8,128)(2,1)S(1)}, bf16[512,512]{1,0:T(8,128)(2,1)}, u32[]{:S(2)}) copy-start(bf16[512,512]{1,0:T(8,128)(2,1)} %w1_ref.1) | copy-start | bytes 1572868
  14.3 8.7 %collective-permute-start.2 = (bf16[784,128]{1,0:T(8,128)(2,1)S(1)}, bf16[784,128]{1,0:T(8,128)(2,1)S(1)}, u32[]{:S(2)}, u32[]{:S(2)}) collective-permute-start(bf16[784,128]{1,0:T(8,128)(2,1)S(1)} %shard_map.96), channel_id=1, source_target_pairs={{0,2},{1,5},{2,0},{3,7},{4,6},{5,1},{6,4},{7,3},{8,10},{9,13},{10,... | collective-permute-start | bytes 602120 | tf_op jit(solution)/shard_map/ppermute | solution.py:225
  15.3 10.3 %collective-permute-start.13 = (bf16[1568,128]{1,0:T(8,128)(2,1)S(1)}, bf16[1568,128]{1,0:T(8,128)(2,1)S(1)}, u32[]{:S(2)}, u32[]{:S(2)}) collective-permute-start(bf16[1568,128]{1,0:T(8,128)(2,1)S(1)} %pad_maximum_fusion.1.refs_0_), channel_id=1, source_target_pairs={{0,4},{1,3},{2,6},{3,1},{4,0},{5,7},{6,2},{7,5},{8,12},{9,11},{10,... | collective-permute-start | bytes 1204232 | tf_op jit(solution)/shard_map/ppermute | solution.py:225
  16.4 16.6 %collective-permute-start.14 = (bf16[1568,128]{1,0:T(8,128)(2,1)S(1)}, bf16[1568,128]{1,0:T(8,128)(2,1)S(1)}, u32[]{:S(2)}, u32[]{:S(2)}) collective-permute-start(bf16[1568,128]{1,0:T(8,128)(2,1)S(1)} %pad_maximum_fusion.1.refs_0_), channel_id=1, source_target_pairs={{0,1},{1,0},{2,3},{3,2},{4,5},{5,4},{6,7},{7,6},{8,9},{9,8},{10,11... | collective-permute-start | bytes 1204232 | tf_op jit(solution)/shard_map/ppermute | solution.py:225
  16.4 9.3 %collective-permute-start.5 = (bf16[784,128]{1,0:T(8,128)(2,1)S(1)}, bf16[784,128]{1,0:T(8,128)(2,1)S(1)}, u32[]{:S(2)}, u32[]{:S(2)}) collective-permute-start(bf16[784,128]{1,0:T(8,128)(2,1)S(1)} %shard_map.96), channel_id=1, source_target_pairs={{0,4},{1,3},{2,6},{3,1},{4,0},{5,7},{6,2},{7,5},{8,12},{9,11},{10,... | collective-permute-start | bytes 602120 | tf_op jit(solution)/shard_map/ppermute | solution.py:225
  22.3 10.1 %collective-permute-start.10 = (bf16[1568,128]{1,0:T(8,128)(2,1)S(1)}, bf16[1568,128]{1,0:T(8,128)(2,1)S(1)}, u32[]{:S(2)}, u32[]{:S(2)}) collective-permute-start(bf16[1568,128]{1,0:T(8,128)(2,1)S(1)} %collective-permute-done.9.refs_0_), channel_id=1, source_target_pairs={{0,4},{1,3},{2,6},{3,1},{4,0},{5,7},{6,2},{7,5},{8,12},{9,11},{10,... | collective-permute-start | bytes 1204232 | tf_op jit(solution)/shard_map/ppermute | solution.py:225
  23.0 11.8 %collective-permute-start.3 = (bf16[1568,128]{1,0:T(8,128)(2,1)S(1)}, bf16[1568,128]{1,0:T(8,128)(2,1)S(1)}, u32[]{:S(2)}, u32[]{:S(2)}) collective-permute-start(bf16[1568,128]{1,0:T(8,128)(2,1)S(1)} %pad_maximum_fusion.refs_0_), channel_id=1, source_target_pairs={{0,8},{1,9},{2,10},{3,11},{4,12},{5,13},{6,14},{7,15},{8,0},{9,1},... | collective-permute-start | bytes 1204232 | tf_op jit(solution)/shard_map/ppermute | solution.py:225
  25.7 9.2 %collective-permute-start.15 = (bf16[1568,128]{1,0:T(8,128)(2,1)S(1)}, bf16[1568,128]{1,0:T(8,128)(2,1)S(1)}, u32[]{:S(2)}, u32[]{:S(2)}) collective-permute-start(bf16[1568,128]{1,0:T(8,128)(2,1)S(1)} %collective-permute-done.13.refs_1_), channel_id=1, source_target_pairs={{0,1},{1,0},{2,3},{3,2},{4,5},{5,4},{6,7},{7,6},{8,9},{9,8},{10,11... | collective-permute-start | bytes 1204232 | tf_op jit(solution)/shard_map/ppermute | solution.py:225
  25.7 6.7 %collective-permute-start.6 = (bf16[784,128]{1,0:T(8,128)(2,1)S(1)}, bf16[784,128]{1,0:T(8,128)(2,1)S(1)}, u32[]{:S(2)}, u32[]{:S(2)}) collective-permute-start(bf16[784,128]{1,0:T(8,128)(2,1)S(1)} %collective-permute-done.2), channel_id=1, source_target_pairs={{0,4},{1,3},{2,6},{3,1},{4,0},{5,7},{6,2},{7,5},{8,12},{9,11},{10,... | collective-permute-start | bytes 602120 | tf_op jit(solution)/shard_map/ppermute | solution.py:225
  32.3 4.5 %collective-permute-start.11 = (bf16[1568,128]{1,0:T(8,128)(2,1)S(1)}, bf16[1568,128]{1,0:T(8,128)(2,1)S(1)}, u32[]{:S(2)}, u32[]{:S(2)}) collective-permute-start(bf16[1568,128]{1,0:T(8,128)(2,1)S(1)} %collective-permute-done.9.refs_0_), channel_id=1, source_target_pairs={{0,1},{1,0},{2,3},{3,2},{4,5},{5,4},{6,7},{7,6},{8,9},{9,8},{10,11... | collective-permute-start | bytes 1204232 | tf_op jit(solution)/shard_map/ppermute | solution.py:225
  32.4 5.2 %collective-permute-start.12 = (bf16[1568,128]{1,0:T(8,128)(2,1)S(1)}, bf16[1568,128]{1,0:T(8,128)(2,1)S(1)}, u32[]{:S(2)}, u32[]{:S(2)}) collective-permute-start(bf16[1568,128]{1,0:T(8,128)(2,1)S(1)} %collective-permute-done.10.refs_1_), channel_id=1, source_target_pairs={{0,1},{1,0},{2,3},{3,2},{4,5},{5,4},{6,7},{7,6},{8,9},{9,8},{10,11... | collective-permute-start | bytes 1204232 | tf_op jit(solution)/shard_map/ppermute | solution.py:225
  33.0 8.0 %collective-permute-start.7 = (bf16[1568,128]{1,0:T(8,128)(2,1)S(1)}, bf16[1568,128]{1,0:T(8,128)(2,1)S(1)}, u32[]{:S(2)}, u32[]{:S(2)}) collective-permute-start(bf16[1568,128]{1,0:T(8,128)(2,1)S(1)} %pad_maximum_fusion.refs_0_), channel_id=1, source_target_pairs={{0,1},{1,0},{2,3},{3,2},{4,5},{5,4},{6,7},{7,6},{8,9},{9,8},{10,11... | collective-permute-start | bytes 1204232 | tf_op jit(solution)/shard_map/ppermute | solution.py:225
  34.9 6.1 %collective-permute-start.8 = (bf16[1568,128]{1,0:T(8,128)(2,1)S(1)}, bf16[1568,128]{1,0:T(8,128)(2,1)S(1)}, u32[]{:S(2)}, u32[]{:S(2)}) collective-permute-start(bf16[1568,128]{1,0:T(8,128)(2,1)S(1)} %constant_dynamic-update-slice_fusion.refs_1_), channel_id=1, source_target_pairs={{0,1},{1,0},{2,3},{3,2},{4,5},{5,4},{6,7},{7,6},{8,9},{9,8},{10,11... | collective-permute-start | bytes 1204232 | tf_op jit(solution)/shard_map/ppermute | solution.py:225
  34.9 8.2 %collective-permute-start.4 = (bf16[1568,128]{1,0:T(8,128)(2,1)S(1)}, bf16[1568,128]{1,0:T(8,128)(2,1)S(1)}, u32[]{:S(2)}, u32[]{:S(2)}) collective-permute-start(bf16[1568,128]{1,0:T(8,128)(2,1)S(1)} %collective-permute-done.3.refs_0_), channel_id=1, source_target_pairs={{0,4},{1,3},{2,6},{3,1},{4,0},{5,7},{6,2},{7,5},{8,12},{9,11},{10,... | collective-permute-start | bytes 1204232 | tf_op jit(solution)/shard_map/ppermute | solution.py:225
  36.9 6.3 %collective-permute-start.16 = (bf16[1568,128]{1,0:T(8,128)(2,1)S(1)}, bf16[1568,128]{1,0:T(8,128)(2,1)S(1)}, u32[]{:S(2)}, u32[]{:S(2)}) collective-permute-start(bf16[1568,128]{1,0:T(8,128)(2,1)S(1)} %collective-permute-done.3.refs_0_), channel_id=1, source_target_pairs={{0,1},{1,0},{2,3},{3,2},{4,5},{5,4},{6,7},{7,6},{8,9},{9,8},{10,11... | collective-permute-start | bytes 1204232 | tf_op jit(solution)/shard_map/ppermute | solution.py:225
  40.9 6.6 %copy-start = (bf16[512,512]{1,0:T(8,128)(2,1)S(1)}, bf16[512,512]{1,0:T(8,128)(2,1)}, u32[]{:S(2)}) copy-start(bf16[512,512]{1,0:T(8,128)(2,1)} %w2_ref.1) | copy-start | bytes 1572868
  43.1 1.8 %collective-permute-start.17 = (bf16[1568,128]{1,0:T(8,128)(2,1)S(1)}, bf16[1568,128]{1,0:T(8,128)(2,1)S(1)}, u32[]{:S(2)}, u32[]{:S(2)}) collective-permute-start(bf16[1568,128]{1,0:T(8,128)(2,1)S(1)} %shard_map.100.refs_1_), channel_id=1, source_target_pairs={{0,1},{1,0},{2,3},{3,2},{4,5},{5,4},{6,7},{7,6},{8,9},{9,8},{10,11... | collective-permute-start | bytes 1204232 | tf_op jit(solution)/shard_map/ppermute | solution.py:225

commit v5 on v4

--- a/solution.py
+++ b/solution.py
@@ -320,16 +320,26 @@
         for e in range(2):
             j = (x ^ dx) * 2 + e
             count = info_s[2 * m + e, 0]
-            for s in range(sz.live):
+
+            def product(s):
                 p = info_s[2 * m + e, s + 1]
-
-                @pl.when(s < count)
+                value = buf[m, e, pl.ds(sz.at_val + s * block, block), :]
+                return j * sz.blk_cols + lax.rem(p, sz.blk_cols), jnp.dot(
+                    turned[2 * dy + p // sz.blk_cols], value, preferred_element_type=jnp.float32
+                )
+
+            for s in range(0, sz.live, 2):
+
+                @pl.when(s + 1 == count)
                 def _():
-                    r, cb = p // sz.blk_cols, lax.rem(p, sz.blk_cols)
-                    value = buf[m, e, pl.ds(sz.at_val + s * block, block), :]
-                    sums[j * sz.blk_cols + cb] += jnp.dot(
-                        turned[2 * dy + r], value, preferred_element_type=jnp.float32
-                    )
+                    at, term = product(s)
+                    sums[at] += term
+
+                @pl.when(s + 1 < count)
+                def _():
+                    (at, term), (next_at, next_term) = product(s), product(s + 1)
+                    sums[at] += term
+                    sums[next_at] += next_term
 
 
 def dense_kernel(

time: 55.1 us -> 55.6 us (level); the launches traced: 54.8 us -> 56 us
  Pallas kernels: 18.7 us -> 19.9 us
    pallas_call x4, Pallas kernels: 9.96 us -> 11.1 us  [add_plane(): pl.pallas_call(functools.partial(plane_kernel, sz, first), out_shape=tupl...]
  transfers between devices with their start and end apart: 18 -> 18, of which waited for: 6 -> 6; matrix products, arithmetic and copies ran while one was open for 0% -> 0% of each run, Pallas kernels for 15% -> 16%
where the time goes in v5:
time: 55.6 us; the launch traced here: 56 us
  Pallas kernels  19.9 us (36%)
  starting transfers between devices  17.4 us (31%)
  waiting for transfers between devices  15.9 us (29%)
  between operations  1.58 us (3%)
  local copies, waits for them, and re-layouts  1.09 us (2%)
    ppermute x18, starting transfers between devices, send(): return lax.ppermute(value, AXES, pairs)  17.4 us
    ppermute x18, waiting for transfers between devices, send(): return lax.ppermute(value, AXES, pairs)  15.9 us
    pallas_call x4, Pallas kernels, add_plane(): pl.pallas_call(functools.partial(plane_kernel, sz, first), out_shape=tupl...  11.1 us
    pallas_call x1, Pallas kernels, dense(): pl.pallas_call(functools.partial(dense_kernel, sz), out_shape=(jax.ShapeD...  7.09 us
  transfers between devices with their start and end apart: 18, of which 6 were waited for; matrix products, arithmetic and copies ran while one was open for 0% of the time, Pallas kernels for 16%

profile of v5, /device:TPU:0, one launch (start us, length us, event | category | flops | bytes accessed | tf_op | source)
XLA Modules:
  0.0 56.0 jit_solution(980126360512432657)
XLA Ops:
  1.3 1.0 %shard_map.94 = bf16[784,128]{1,0:T(8,128)(2,1)S(1)} custom-call(s32[1,1,8]{2,1,0:T(1,128)} %index_ref.1, s32[1,1]{1,0:T(1,128)S(6)} %copy.23.count_ref, bf16[64,512]{1,0:T(8,128)(2,1)} %feat_ref.1, bf16[64,512]{1,0:T(8,128)(2,1)} %cot_ref.1, bf16[1,1,8,128,128]{4,3,2,1,0:T(8,128)(2,1)} %val_ref.1), custom_call_target="tpu_custom_call" | custom-call | tf_op jit(solution)/shard_map/pallas_call | solution.py:181
  2.3 3.0 %collective-permute-start.1 = (bf16[784,128]{1,0:T(8,128)(2,1)S(1)}, bf16[784,128]{1,0:T(8,128)(2,1)S(1)}, u32[]{:S(2)}, u32[]{:S(2)}) collective-permute-start(bf16[784,128]{1,0:T(8,128)(2,1)S(1)} %shard_map.94), channel_id=1, source_target_pairs={{0,2},{1,5},{2,0},{3,7},{4,6},{5,1},{6,4},{7,3},{8,10},{9,13},{10,... | collective-permute-start | bytes 602120 | tf_op jit(solution)/shard_map/ppermute | solution.py:225
  5.3 3.6 %collective-permute-start = (bf16[784,128]{1,0:T(8,128)(2,1)S(1)}, bf16[784,128]{1,0:T(8,128)(2,1)S(1)}, u32[]{:S(2)}, u32[]{:S(2)}) collective-permute-start(bf16[784,128]{1,0:T(8,128)(2,1)S(1)} %shard_map.94), channel_id=1, source_target_pairs={{0,24},{1,25},{2,26},{3,27},{4,28},{5,29},{6,30},{7,31},{8,16},{9,... | collective-permute-start | bytes 602120 | tf_op jit(solution)/shard_map/ppermute | solution.py:225
  8.9 0.1 collective-permute-done.1.dep_ref
  9.0 2.2 %collective-permute-start.9 = (bf16[1568,128]{1,0:T(8,128)(2,1)S(1)}, bf16[1568,128]{1,0:T(8,128)(2,1)S(1)}, u32[]{:S(2)}, u32[]{:S(2)}) collective-permute-start(bf16[1568,128]{1,0:T(8,128)(2,1)S(1)} %pad_maximum_fusion.1.refs_0_), channel_id=1, source_target_pairs={{0,8},{1,9},{2,10},{3,11},{4,12},{5,13},{6,14},{7,15},{8,0},{9,1},... | collective-permute-start | bytes 1204232 | tf_op jit(solution)/shard_map/ppermute | solution.py:225
  11.2 0.0 copy-start.1
  11.2 1.0 %copy-done.1 = bf16[512,512]{1,0:T(8,128)(2,1)S(1)} copy-done((bf16[512,512]{1,0:T(8,128)(2,1)S(1)}, bf16[512,512]{1,0:T(8,128)(2,1)}, u32[]{:S(2)}) %copy-start.1) | copy-done | bytes 524312
  12.2 0.7 %shard_map.95 = (f32[16,1024,128]{2,1,0:T(8,128)S(1)}, s32[8,128]{1,0:T(8,128)S(1)}, bf16[512,512]{1,0:T(8,128)(2,1)S(1)}) custom-call(bf16[512,512]{1,0:T(8,128)(2,1)S(1)} %copy-done.1, bf16[784,128]{1,0:T(8,128)(2,1)S(1)} %collective-permute-done.1.dep_ref), custom_call_target="tpu_custom_call" | custom-call | tf_op jit(solution)/shard_map/pallas_call | solution.py:419
  12.9 1.4 %collective-permute-done.value_ref = bf16[784,128]{1,0:T(8,128)(2,1)S(1)} collective-permute-done((bf16[784,128]{1,0:T(8,128)(2,1)S(1)}, bf16[784,128]{1,0:T(8,128)(2,1)S(1)}, u32[]{:S(2)}, u32[]{:S(2)}) %collective-permute-start) | collective-permute-done | bytes 200736 | tf_op jit(solution)/shard_map/ppermute | solution.py:225
  14.3 1.0 %collective-permute-start.2 = (bf16[784,128]{1,0:T(8,128)(2,1)S(1)}, bf16[784,128]{1,0:T(8,128)(2,1)S(1)}, u32[]{:S(2)}, u32[]{:S(2)}) collective-permute-start(bf16[784,128]{1,0:T(8,128)(2,1)S(1)} %shard_map.96), channel_id=1, source_target_pairs={{0,2},{1,5},{2,0},{3,7},{4,6},{5,1},{6,4},{7,3},{8,10},{9,13},{10,... | collective-permute-start | bytes 602120 | tf_op jit(solution)/shard_map/ppermute | solution.py:225
  15.3 1.0 %collective-permute-start.13 = (bf16[1568,128]{1,0:T(8,128)(2,1)S(1)}, bf16[1568,128]{1,0:T(8,128)(2,1)S(1)}, u32[]{:S(2)}, u32[]{:S(2)}) collective-permute-start(bf16[1568,128]{1,0:T(8,128)(2,1)S(1)} %pad_maximum_fusion.1.refs_0_), channel_id=1, source_target_pairs={{0,4},{1,3},{2,6},{3,1},{4,0},{5,7},{6,2},{7,5},{8,12},{9,11},{10,... | collective-permute-start | bytes 1204232 | tf_op jit(solution)/shard_map/ppermute | solution.py:225
  16.4 0.0 collective-permute-start.14
  16.4 1.0 %collective-permute-start.5 = (bf16[784,128]{1,0:T(8,128)(2,1)S(1)}, bf16[784,128]{1,0:T(8,128)(2,1)S(1)}, u32[]{:S(2)}, u32[]{:S(2)}) collective-permute-start(bf16[784,128]{1,0:T(8,128)(2,1)S(1)} %shard_map.96), channel_id=1, source_target_pairs={{0,4},{1,3},{2,6},{3,1},{4,0},{5,7},{6,2},{7,5},{8,12},{9,11},{10,... | collective-permute-start | bytes 602120 | tf_op jit(solution)/shard_map/ppermute | solution.py:225
  17.4 5.0 %collective-permute-done.9.refs_0_ = bf16[1568,128]{1,0:T(8,128)(2,1)S(1)} collective-permute-done((bf16[1568,128]{1,0:T(8,128)(2,1)S(1)}, bf16[1568,128]{1,0:T(8,128)(2,1)S(1)}, u32[]{:S(2)}, u32[]{:S(2)}) %collective-permute-start.9) | collective-permute-done | bytes 401440 | tf_op jit(solution)/shard_map/ppermute | solution.py:225
  22.3 0.6 %collective-permute-start.10 = (bf16[1568,128]{1,0:T(8,128)(2,1)S(1)}, bf16[1568,128]{1,0:T(8,128)(2,1)S(1)}, u32[]{:S(2)}, u32[]{:S(2)}) collective-permute-start(bf16[1568,128]{1,0:T(8,128)(2,1)S(1)} %collective-permute-done.9.refs_0_), channel_id=1, source_target_pairs={{0,4},{1,3},{2,6},{3,1},{4,0},{5,7},{6,2},{7,5},{8,12},{9,11},{10,... | collective-permute-start | bytes 1204232 | tf_op jit(solution)/shard_map/ppermute | solution.py:225
  23.0 0.0 collective-permute-done.2
  23.0 2.7 %collective-permute-start.3 = (bf16[1568,128]{1,0:T(8,128)(2,1)S(1)}, bf16[1568,128]{1,0:T(8,128)(2,1)S(1)}, u32[]{:S(2)}, u32[]{:S(2)}) collective-permute-start(bf16[1568,128]{1,0:T(8,128)(2,1)S(1)} %pad_maximum_fusion.refs_0_), channel_id=1, source_target_pairs={{0,8},{1,9},{2,10},{3,11},{4,12},{5,13},{6,14},{7,15},{8,0},{9,1},... | collective-permute-start | bytes 1204232 | tf_op jit(solution)/shard_map/ppermute | solution.py:225
  25.7 0.0 collective-permute-done.13.refs_1_
  25.7 0.0 collective-permute-start.15
  25.7 0.0 collective-permute-done.5
  25.7 0.7 %collective-permute-start.6 = (bf16[784,128]{1,0:T(8,128)(2,1)S(1)}, bf16[784,128]{1,0:T(8,128)(2,1)S(1)}, u32[]{:S(2)}, u32[]{:S(2)}) collective-permute-start(bf16[784,128]{1,0:T(8,128)(2,1)S(1)} %collective-permute-done.2), channel_id=1, source_target_pairs={{0,4},{1,3},{2,6},{3,1},{4,0},{5,7},{6,2},{7,5},{8,12},{9,11},{10,... | collective-permute-start | bytes 602120 | tf_op jit(solution)/shard_map/ppermute | solution.py:225
  26.4 5.9 %collective-permute-done.6 = bf16[784,128]{1,0:T(8,128)(2,1)S(1)} collective-permute-done((bf16[784,128]{1,0:T(8,128)(2,1)S(1)}, bf16[784,128]{1,0:T(8,128)(2,1)S(1)}, u32[]{:S(2)}, u32[]{:S(2)}) %collective-permute-start.6) | collective-permute-done | bytes 200736 | tf_op jit(solution)/shard_map/ppermute | solution.py:225
  32.3 0.0 collective-permute-start.11
  32.4 0.0 collective-permute-done.10.refs_1_
  32.4 0.6 %collective-permute-start.12 = (bf16[1568,128]{1,0:T(8,128)(2,1)S(1)}, bf16[1568,128]{1,0:T(8,128)(2,1)S(1)}, u32[]{:S(2)}, u32[]{:S(2)}) collective-permute-start(bf16[1568,128]{1,0:T(8,128)(2,1)S(1)} %collective-permute-done.10.refs_1_), channel_id=1, source_target_pairs={{0,1},{1,0},{2,3},{3,2},{4,5},{5,4},{6,7},{7,6},{8,9},{9,8},{10,11... | collective-permute-start | bytes 1204232 | tf_op jit(solution)/shard_map/ppermute | solution.py:225
  33.0 0.0 collective-permute-done.14.refs_2_
  33.0 0.1 collective-permute-start.7
  33.1 1.8 %collective-permute-done.3.refs_0_ = bf16[1568,128]{1,0:T(8,128)(2,1)S(1)} collective-permute-done((bf16[1568,128]{1,0:T(8,128)(2,1)S(1)}, bf16[1568,128]{1,0:T(8,128)(2,1)S(1)}, u32[]{:S(2)}, u32[]{:S(2)}) %collective-permute-start.3) | collective-permute-done | bytes 401440 | tf_op jit(solution)/shard_map/ppermute | solution.py:225
  34.9 0.0 collective-permute-start.8
  34.9 0.0 collective-permute-done.15.refs_3_
  34.9 0.1 collective-permute-start.4
  34.9 2.4 %shard_map.97 = (f32[16,1024,128]{2,1,0:T(8,128)S(1)}, s32[8,128]{1,0:T(8,128)S(1)}, bf16[4,256,128]{2,1,0:T(8,128)(2,1)S(1)}) custom-call(bf16[1568,128]{1,0:T(8,128)(2,1)S(1)} %pad_maximum_fusion.1.refs_0_, bf16[1568,128]{1,0:T(8,128)(2,1)S(1)} %collective-permute-done.13.refs_1_, ...), custom_call_target="tpu_custom_call", output_to_operand_aliasing={{0}: (4, {})} | custom-call | tf_op jit(solution)/shard_map/pallas_call | solution.py:440
  37.4 0.0 collective-permute-done.11.refs_2_
  37.4 0.7 %collective-permute-start.16 = (bf16[1568,128]{1,0:T(8,128)(2,1)S(1)}, bf16[1568,128]{1,0:T(8,128)(2,1)S(1)}, u32[]{:S(2)}, u32[]{:S(2)}) collective-permute-start(bf16[1568,128]{1,0:T(8,128)(2,1)S(1)} %collective-permute-done.3.refs_0_), channel_id=1, source_target_pairs={{0,1},{1,0},{2,3},{3,2},{4,5},{5,4},{6,7},{7,6},{8,9},{9,8},{10,11... | collective-permute-start | bytes 1204232 | tf_op jit(solution)/shard_map/ppermute | solution.py:225
  38.1 0.0 collective-permute-done.12.refs_3_
  38.1 3.4 %shard_map.98 = (f32[16,1024,128]{2,1,0:T(8,128)S(1)}, s32[8,128]{1,0:T(8,128)}) custom-call(bf16[1568,128]{1,0:T(8,128)(2,1)S(1)} %collective-permute-done.9.refs_0_, bf16[1568,128]{1,0:T(8,128)(2,1)S(1)} %collective-permute-done.10.refs_1_, bf16[1568,128]{1,0:T(8,128)(2,1)S(1)} %collective-permute-done.11.refs_2_, ...), custom_call_target="tpu_custom_call", output_to_operand_aliasing={{0}: (4, {})} | custom-call | tf_op jit(solution)/shard_map/pallas_call | solution.py:440
  41.5 0.0 collective-permute-done.7.refs_2_
  41.5 0.0 collective-permute-done.8.refs_3_
  41.5 0.0 copy-start
  41.5 2.5 %shard_map.99 = (f32[16,1024,128]{2,1,0:T(8,128)S(1)}, s32[8,128]{1,0:T(8,128)S(1)}) custom-call(bf16[1568,128]{1,0:T(8,128)(2,1)S(1)} %pad_maximum_fusion.refs_0_, bf16[1568,128]{1,0:T(8,128)(2,1)S(1)} %constant_dynamic-update-slice_fusion.refs_1_, bf16[1568,128]{1,0:T(8,128)(2,1)S(1)} %collective-permute-done.7.refs_2_, ...), custom_call_target="tpu_custom_call", output_to_operand_aliasing={{0}: (4, {})} | custom-call | tf_op jit(solution)/shard_map/pallas_call | solution.py:440
  44.1 0.0 collective-permute-done.4.value_ref
  44.1 0.1 collective-permute-start.17
  44.2 0.0 collective-permute-done.16.refs_2_
  44.2 1.7 %collective-permute-done.17.refs_3_ = bf16[1568,128]{1,0:T(8,128)(2,1)S(1)} collective-permute-done((bf16[1568,128]{1,0:T(8,128)(2,1)S(1)}, bf16[1568,128]{1,0:T(8,128)(2,1)S(1)}, u32[]{:S(2)}, u32[]{:S(2)}) %collective-permute-start.17) | collective-permute-done | bytes 401440 | tf_op jit(solution)/shard_map/ppermute | solution.py:225
  45.9 2.8 %shard_map.101 = (f32[16,1024,128]{2,1,0:T(8,128)S(1)}, s32[8,128]{1,0:T(8,128)}) custom-call(bf16[1568,128]{1,0:T(8,128)(2,1)S(1)} %collective-permute-done.3.refs_0_, bf16[1568,128]{1,0:T(8,128)(2,1)S(1)} %shard_map.100.refs_1_, bf16[1568,128]{1,0:T(8,128)(2,1)S(1)} %collective-permute-done.16.refs_2_, ...), custom_call_target="tpu_custom_call", output_to_operand_aliasing={{0}: (4, {})} | custom-call | tf_op jit(solution)/shard_map/pallas_call | solution.py:440
  48.7 0.0 copy-done
  48.7 7.1 %shard_map.102 = (bf16[64,512]{1,0:T(8,128)(2,1)}, f32[512,512]{1,0:T(8,128)}, f32[512,512]{1,0:T(8,128)}) custom-call(f32[16,1024,128]{2,1,0:T(8,128)S(1)} %get-tuple-element.19.sums, bf16[4,256,128]{2,1,0:T(8,128)(2,1)S(1)} %get-tuple-element.20.vals, s32[8,128]{1,0:T(8,128)S(1)} %get-tuple-element.21.info_v, bf16[512,512]{1,0:T(8,128)(2,1)S(1)} %get-tuple-element.22.w1t, ...), custom_call_target="tpu_custom_call" | custom-call | tf_op jit(solution)/shard_map/pallas_call | solution.py:461
  (6 shorter events, 0.1 us)
Async XLA Ops:
  2.3 6.7 %collective-permute-start.1 = (bf16[784,128]{1,0:T(8,128)(2,1)S(1)}, bf16[784,128]{1,0:T(8,128)(2,1)S(1)}, u32[]{:S(2)}, u32[]{:S(2)}) collective-permute-start(bf16[784,128]{1,0:T(8,128)(2,1)S(1)} %shard_map.94), channel_id=1, source_target_pairs={{0,2},{1,5},{2,0},{3,7},{4,6},{5,1},{6,4},{7,3},{8,10},{9,13},{10,... | collective-permute-start | bytes 602120 | tf_op jit(solution)/shard_map/ppermute | solution.py:225
  5.3 9.0 %collective-permute-start = (bf16[784,128]{1,0:T(8,128)(2,1)S(1)}, bf16[784,128]{1,0:T(8,128)(2,1)S(1)}, u32[]{:S(2)}, u32[]{:S(2)}) collective-permute-start(bf16[784,128]{1,0:T(8,128)(2,1)S(1)} %shard_map.94), channel_id=1, source_target_pairs={{0,24},{1,25},{2,26},{3,27},{4,28},{5,29},{6,30},{7,31},{8,16},{9,... | collective-permute-start | bytes 602120 | tf_op jit(solution)/shard_map/ppermute | solution.py:225
  9.0 13.3 %collective-permute-start.9 = (bf16[1568,128]{1,0:T(8,128)(2,1)S(1)}, bf16[1568,128]{1,0:T(8,128)(2,1)S(1)}, u32[]{:S(2)}, u32[]{:S(2)}) collective-permute-start(bf16[1568,128]{1,0:T(8,128)(2,1)S(1)} %pad_maximum_fusion.1.refs_0_), channel_id=1, source_target_pairs={{0,8},{1,9},{2,10},{3,11},{4,12},{5,13},{6,14},{7,15},{8,0},{9,1},... | collective-permute-start | bytes 1204232 | tf_op jit(solution)/shard_map/ppermute | solution.py:225
  11.2 1.0 %copy-start.1 = (bf16[512,512]{1,0:T(8,128)(2,1)S(1)}, bf16[512,512]{1,0:T(8,128)(2,1)}, u32[]{:S(2)}) copy-start(bf16[512,512]{1,0:T(8,128)(2,1)} %w1_ref.1) | copy-start | bytes 1572868
  14.3 8.7 %collective-permute-start.2 = (bf16[784,128]{1,0:T(8,128)(2,1)S(1)}, bf16[784,128]{1,0:T(8,128)(2,1)S(1)}, u32[]{:S(2)}, u32[]{:S(2)}) collective-permute-start(bf16[784,128]{1,0:T(8,128)(2,1)S(1)} %shard_map.96), channel_id=1, source_target_pairs={{0,2},{1,5},{2,0},{3,7},{4,6},{5,1},{6,4},{7,3},{8,10},{9,13},{10,... | collective-permute-start | bytes 602120 | tf_op jit(solution)/shard_map/ppermute | solution.py:225
  15.3 10.3 %collective-permute-start.13 = (bf16[1568,128]{1,0:T(8,128)(2,1)S(1)}, bf16[1568,128]{1,0:T(8,128)(2,1)S(1)}, u32[]{:S(2)}, u32[]{:S(2)}) collective-permute-start(bf16[1568,128]{1,0:T(8,128)(2,1)S(1)} %pad_maximum_fusion.1.refs_0_), channel_id=1, source_target_pairs={{0,4},{1,3},{2,6},{3,1},{4,0},{5,7},{6,2},{7,5},{8,12},{9,11},{10,... | collective-permute-start | bytes 1204232 | tf_op jit(solution)/shard_map/ppermute | solution.py:225
  16.4 16.6 %collective-permute-start.14 = (bf16[1568,128]{1,0:T(8,128)(2,1)S(1)}, bf16[1568,128]{1,0:T(8,128)(2,1)S(1)}, u32[]{:S(2)}, u32[]{:S(2)}) collective-permute-start(bf16[1568,128]{1,0:T(8,128)(2,1)S(1)} %pad_maximum_fusion.1.refs_0_), channel_id=1, source_target_pairs={{0,1},{1,0},{2,3},{3,2},{4,5},{5,4},{6,7},{7,6},{8,9},{9,8},{10,11... | collective-permute-start | bytes 1204232 | tf_op jit(solution)/shard_map/ppermute | solution.py:225
  16.4 9.3 %collective-permute-start.5 = (bf16[784,128]{1,0:T(8,128)(2,1)S(1)}, bf16[784,128]{1,0:T(8,128)(2,1)S(1)}, u32[]{:S(2)}, u32[]{:S(2)}) collective-permute-start(bf16[784,128]{1,0:T(8,128)(2,1)S(1)} %shard_map.96), channel_id=1, source_target_pairs={{0,4},{1,3},{2,6},{3,1},{4,0},{5,7},{6,2},{7,5},{8,12},{9,11},{10,... | collective-permute-start | bytes 602120 | tf_op jit(solution)/shard_map/ppermute | solution.py:225
  22.3 10.1 %collective-permute-start.10 = (bf16[1568,128]{1,0:T(8,128)(2,1)S(1)}, bf16[1568,128]{1,0:T(8,128)(2,1)S(1)}, u32[]{:S(2)}, u32[]{:S(2)}) collective-permute-start(bf16[1568,128]{1,0:T(8,128)(2,1)S(1)} %collective-permute-done.9.refs_0_), channel_id=1, source_target_pairs={{0,4},{1,3},{2,6},{3,1},{4,0},{5,7},{6,2},{7,5},{8,12},{9,11},{10,... | collective-permute-start | bytes 1204232 | tf_op jit(solution)/shard_map/ppermute | solution.py:225
  23.0 11.8 %collective-permute-start.3 = (bf16[1568,128]{1,0:T(8,128)(2,1)S(1)}, bf16[1568,128]{1,0:T(8,128)(2,1)S(1)}, u32[]{:S(2)}, u32[]{:S(2)}) collective-permute-start(bf16[1568,128]{1,0:T(8,128)(2,1)S(1)} %pad_maximum_fusion.refs_0_), channel_id=1, source_target_pairs={{0,8},{1,9},{2,10},{3,11},{4,12},{5,13},{6,14},{7,15},{8,0},{9,1},... | collective-permute-start | bytes 1204232 | tf_op jit(solution)/shard_map/ppermute | solution.py:225
  25.7 9.2 %collective-permute-start.15 = (bf16[1568,128]{1,0:T(8,128)(2,1)S(1)}, bf16[1568,128]{1,0:T(8,128)(2,1)S(1)}, u32[]{:S(2)}, u32[]{:S(2)}) collective-permute-start(bf16[1568,128]{1,0:T(8,128)(2,1)S(1)} %collective-permute-done.13.refs_1_), channel_id=1, source_target_pairs={{0,1},{1,0},{2,3},{3,2},{4,5},{5,4},{6,7},{7,6},{8,9},{9,8},{10,11... | collective-permute-start | bytes 1204232 | tf_op jit(solution)/shard_map/ppermute | solution.py:225
  25.7 6.7 %collective-permute-start.6 = (bf16[784,128]{1,0:T(8,128)(2,1)S(1)}, bf16[784,128]{1,0:T(8,128)(2,1)S(1)}, u32[]{:S(2)}, u32[]{:S(2)}) collective-permute-start(bf16[784,128]{1,0:T(8,128)(2,1)S(1)} %collective-permute-done.2), channel_id=1, source_target_pairs={{0,4},{1,3},{2,6},{3,1},{4,0},{5,7},{6,2},{7,5},{8,12},{9,11},{10,... | collective-permute-start | bytes 602120 | tf_op jit(solution)/shard_map/ppermute | solution.py:225
  32.3 5.0 %collective-permute-start.11 = (bf16[1568,128]{1,0:T(8,128)(2,1)S(1)}, bf16[1568,128]{1,0:T(8,128)(2,1)S(1)}, u32[]{:S(2)}, u32[]{:S(2)}) collective-permute-start(bf16[1568,128]{1,0:T(8,128)(2,1)S(1)} %collective-permute-done.9.refs_0_), channel_id=1, source_target_pairs={{0,1},{1,0},{2,3},{3,2},{4,5},{5,4},{6,7},{7,6},{8,9},{9,8},{10,11... | collective-permute-start | bytes 1204232 | tf_op jit(solution)/shard_map/ppermute | solution.py:225
  32.4 5.7 %collective-permute-start.12 = (bf16[1568,128]{1,0:T(8,128)(2,1)S(1)}, bf16[1568,128]{1,0:T(8,128)(2,1)S(1)}, u32[]{:S(2)}, u32[]{:S(2)}) collective-permute-start(bf16[1568,128]{1,0:T(8,128)(2,1)S(1)} %collective-permute-done.10.refs_1_), channel_id=1, source_target_pairs={{0,1},{1,0},{2,3},{3,2},{4,5},{5,4},{6,7},{7,6},{8,9},{9,8},{10,11... | collective-permute-start | bytes 1204232 | tf_op jit(solution)/shard_map/ppermute | solution.py:225
  33.0 8.5 %collective-permute-start.7 = (bf16[1568,128]{1,0:T(8,128)(2,1)S(1)}, bf16[1568,128]{1,0:T(8,128)(2,1)S(1)}, u32[]{:S(2)}, u32[]{:S(2)}) collective-permute-start(bf16[1568,128]{1,0:T(8,128)(2,1)S(1)} %pad_maximum_fusion.refs_0_), channel_id=1, source_target_pairs={{0,1},{1,0},{2,3},{3,2},{4,5},{5,4},{6,7},{7,6},{8,9},{9,8},{10,11... | collective-permute-start | bytes 1204232 | tf_op jit(solution)/shard_map/ppermute | solution.py:225
  34.9 6.7 %collective-permute-start.8 = (bf16[1568,128]{1,0:T(8,128)(2,1)S(1)}, bf16[1568,128]{1,0:T(8,128)(2,1)S(1)}, u32[]{:S(2)}, u32[]{:S(2)}) collective-permute-start(bf16[1568,128]{1,0:T(8,128)(2,1)S(1)} %constant_dynamic-update-slice_fusion.refs_1_), channel_id=1, source_target_pairs={{0,1},{1,0},{2,3},{3,2},{4,5},{5,4},{6,7},{7,6},{8,9},{9,8},{10,11... | collective-permute-start | bytes 1204232 | tf_op jit(solution)/shard_map/ppermute | solution.py:225
  34.9 9.2 %collective-permute-start.4 = (bf16[1568,128]{1,0:T(8,128)(2,1)S(1)}, bf16[1568,128]{1,0:T(8,128)(2,1)S(1)}, u32[]{:S(2)}, u32[]{:S(2)}) collective-permute-start(bf16[1568,128]{1,0:T(8,128)(2,1)S(1)} %collective-permute-done.3.refs_0_), channel_id=1, source_target_pairs={{0,4},{1,3},{2,6},{3,1},{4,0},{5,7},{6,2},{7,5},{8,12},{9,11},{10,... | collective-permute-start | bytes 1204232 | tf_op jit(solution)/shard_map/ppermute | solution.py:225
  37.4 6.8 %collective-permute-start.16 = (bf16[1568,128]{1,0:T(8,128)(2,1)S(1)}, bf16[1568,128]{1,0:T(8,128)(2,1)S(1)}, u32[]{:S(2)}, u32[]{:S(2)}) collective-permute-start(bf16[1568,128]{1,0:T(8,128)(2,1)S(1)} %collective-permute-done.3.refs_0_), channel_id=1, source_target_pairs={{0,1},{1,0},{2,3},{3,2},{4,5},{5,4},{6,7},{7,6},{8,9},{9,8},{10,11... | collective-permute-start | bytes 1204232 | tf_op jit(solution)/shard_map/ppermute | solution.py:225
  41.5 7.2 %copy-start = (bf16[512,512]{1,0:T(8,128)(2,1)S(1)}, bf16[512,512]{1,0:T(8,128)(2,1)}, u32[]{:S(2)}) copy-start(bf16[512,512]{1,0:T(8,128)(2,1)} %w2_ref.1) | copy-start | bytes 1572868
  44.1 1.8 %collective-permute-start.17 = (bf16[1568,128]{1,0:T(8,128)(2,1)S(1)}, bf16[1568,128]{1,0:T(8,128)(2,1)S(1)}, u32[]{:S(2)}, u32[]{:S(2)}) collective-permute-start(bf16[1568,128]{1,0:T(8,128)(2,1)S(1)} %shard_map.100.refs_1_), channel_id=1, source_target_pairs={{0,1},{1,0},{2,3},{3,2},{4,5},{5,4},{6,7},{7,6},{8,9},{9,8},{10,11... | collective-permute-start | bytes 1204232 | tf_op jit(solution)/shard_map/ppermute | solution.py:225

commit v6 on v5

--- a/solution.py
+++ b/solution.py
@@ -247,7 +247,7 @@
     planes = [(near, send(near, second_way))]
     near = send(near, flip(1))
     planes.append((near, send(near, second_way)))
-    sums, token, w1t = init(sz, w_first, one)
+    sums, token, w1t = init(sz, w_first, payload)
 
     low = 2
     while low < n_z:
@@ -372,10 +372,16 @@
         back = jnp.dot(w2_ref[...], b, preferred_element_type=jnp.float32)
         all_f[:, lanes] = (back * slope).astype(jnp.bfloat16)
 
-    gs[...] = lax.dot_general(all_a[...], all_b[...], nt, preferred_element_type=jnp.float32)
+    for at in range(0, width, width // 2):
+        gs[:, at : at + width // 2] = lax.dot_general(
+            all_a[...], all_b[at : at + width // 2, :], nt, preferred_element_type=jnp.float32
+        )
     gs_copy = pltpu.make_async_copy(gs, gs_ref, sems.at[1])
     gs_copy.start()
-    gf[...] = lax.dot_general(all_g[...], all_f[...], nt, preferred_element_type=jnp.float32)
+    for at in range(0, width, width // 2):
+        gf[:, at : at + width // 2] = lax.dot_general(
+            all_g[...], all_f[at : at + width // 2, :], nt, preferred_element_type=jnp.float32
+        )
     gf_copy = pltpu.make_async_copy(gf, gf_ref, sems.at[2])
     gf_copy.start()
     info_copy.wait()

time: 55.6 us -> 54.4 us (0.978)
  Pallas kernels: 19.9 us -> 17.8 us
  waiting for transfers between devices: 15.9 us -> 16.8 us
    pallas_call x4, Pallas kernels: 11.1 us -> 8.97 us  [add_plane(): pl.pallas_call(functools.partial(plane_kernel, sz, first), out_shape=tupl...]
    ppermute x18, waiting for transfers between devices: 15.9 us -> 16.8 us  [send(): return lax.ppermute(value, AXES, pairs)]
  transfers between devices with their start and end apart: 18 -> 18, of which waited for: 6 -> 7; matrix products, arithmetic and copies ran while one was open for 0% -> 0% of each run, Pallas kernels for 16% -> 12%
where the time goes in v6:
time: 54.4 us; the launch traced here: 54.6 us
  Pallas kernels  17.8 us (33%)
  starting transfers between devices  17.3 us (32%)
  waiting for transfers between devices  16.8 us (31%)
  between operations  1.57 us (3%)
  local copies, waits for them, and re-layouts  1.09 us (2%)
    ppermute x18, starting transfers between devices, send(): return lax.ppermute(value, AXES, pairs)  17.3 us
    ppermute x18, waiting for transfers between devices, send(): return lax.ppermute(value, AXES, pairs)  16.8 us
    pallas_call x4, Pallas kernels, add_plane(): pl.pallas_call(functools.partial(plane_kernel, sz, first), out_shape=tupl...  8.97 us
    pallas_call x1, Pallas kernels, dense(): pl.pallas_call(functools.partial(dense_kernel, sz), out_shape=(jax.ShapeD...  7.09 us
  transfers between devices with their start and end apart: 18, of which 7 were waited for; matrix products, arithmetic and copies ran while one was open for 0% of the time, Pallas kernels for 12%

profile of v6, /device:TPU:0, one launch (start us, length us, event | category | flops | bytes accessed | tf_op | source)
XLA Modules:
  0.0 54.6 jit_solution(2508410851314148536)
XLA Ops:
  1.3 1.0 %shard_map.94.dep_ref = bf16[784,128]{1,0:T(8,128)(2,1)S(1)} custom-call(s32[1,1,8]{2,1,0:T(1,128)} %index_ref.1, s32[1,1]{1,0:T(1,128)S(6)} %copy.23.count_ref, bf16[64,512]{1,0:T(8,128)(2,1)} %feat_ref.1, bf16[64,512]{1,0:T(8,128)(2,1)} %cot_ref.1, bf16[1,1,8,128,128]{4,3,2,1,0:T(8,128)(2,1)} %val_ref.1), custom_call_target="tpu_custom_call" | custom-call | tf_op jit(solution)/shard_map/pallas_call | solution.py:181
  2.3 3.0 %collective-permute-start.8 = (bf16[784,128]{1,0:T(8,128)(2,1)S(1)}, bf16[784,128]{1,0:T(8,128)(2,1)S(1)}, u32[]{:S(2)}, u32[]{:S(2)}) collective-permute-start(bf16[784,128]{1,0:T(8,128)(2,1)S(1)} %shard_map.94.dep_ref), channel_id=1, source_target_pairs={{0,2},{1,5},{2,0},{3,7},{4,6},{5,1},{6,4},{7,3},{8,10},{9,13},{10,... | collective-permute-start | bytes 602120 | tf_op jit(solution)/shard_map/ppermute | solution.py:225
  5.3 3.6 %collective-permute-start = (bf16[784,128]{1,0:T(8,128)(2,1)S(1)}, bf16[784,128]{1,0:T(8,128)(2,1)S(1)}, u32[]{:S(2)}, u32[]{:S(2)}) collective-permute-start(bf16[784,128]{1,0:T(8,128)(2,1)S(1)} %shard_map.94.dep_ref), channel_id=1, source_target_pairs={{0,24},{1,25},{2,26},{3,27},{4,28},{5,29},{6,30},{7,31},{8,16},{9,... | collective-permute-start | bytes 602120 | tf_op jit(solution)/shard_map/ppermute | solution.py:225
  8.9 0.1 collective-permute-done.8
  9.0 2.2 %collective-permute-start.9 = (bf16[1568,128]{1,0:T(8,128)(2,1)S(1)}, bf16[1568,128]{1,0:T(8,128)(2,1)S(1)}, u32[]{:S(2)}, u32[]{:S(2)}) collective-permute-start(bf16[1568,128]{1,0:T(8,128)(2,1)S(1)} %pad_maximum_fusion.1.refs_0_), channel_id=1, source_target_pairs={{0,8},{1,9},{2,10},{3,11},{4,12},{5,13},{6,14},{7,15},{8,0},{9,1},... | collective-permute-start | bytes 1204232 | tf_op jit(solution)/shard_map/ppermute | solution.py:225
  11.2 0.0 copy-start.1
  11.2 1.0 %copy-done.1 = bf16[512,512]{1,0:T(8,128)(2,1)S(1)} copy-done((bf16[512,512]{1,0:T(8,128)(2,1)S(1)}, bf16[512,512]{1,0:T(8,128)(2,1)}, u32[]{:S(2)}) %copy-start.1) | copy-done | bytes 524312
  12.2 0.7 %shard_map.95 = (f32[16,1024,128]{2,1,0:T(8,128)S(1)}, s32[8,128]{1,0:T(8,128)S(1)}, bf16[512,512]{1,0:T(8,128)(2,1)S(1)}) custom-call(bf16[512,512]{1,0:T(8,128)(2,1)S(1)} %copy-done.1, bf16[784,128]{1,0:T(8,128)(2,1)S(1)} %shard_map.94.dep_ref), custom_call_target="tpu_custom_call" | custom-call | tf_op jit(solution)/shard_map/pallas_call | solution.py:425
  12.9 1.4 %collective-permute-done.value_ref = bf16[784,128]{1,0:T(8,128)(2,1)S(1)} collective-permute-done((bf16[784,128]{1,0:T(8,128)(2,1)S(1)}, bf16[784,128]{1,0:T(8,128)(2,1)S(1)}, u32[]{:S(2)}, u32[]{:S(2)}) %collective-permute-start) | collective-permute-done | bytes 200736 | tf_op jit(solution)/shard_map/ppermute | solution.py:225
  14.3 1.0 %collective-permute-start.1 = (bf16[784,128]{1,0:T(8,128)(2,1)S(1)}, bf16[784,128]{1,0:T(8,128)(2,1)S(1)}, u32[]{:S(2)}, u32[]{:S(2)}) collective-permute-start(bf16[784,128]{1,0:T(8,128)(2,1)S(1)} %shard_map.96), channel_id=1, source_target_pairs={{0,2},{1,5},{2,0},{3,7},{4,6},{5,1},{6,4},{7,3},{8,10},{9,13},{10,... | collective-permute-start | bytes 602120 | tf_op jit(solution)/shard_map/ppermute | solution.py:225
  15.3 1.0 %collective-permute-start.13 = (bf16[1568,128]{1,0:T(8,128)(2,1)S(1)}, bf16[1568,128]{1,0:T(8,128)(2,1)S(1)}, u32[]{:S(2)}, u32[]{:S(2)}) collective-permute-start(bf16[1568,128]{1,0:T(8,128)(2,1)S(1)} %pad_maximum_fusion.1.refs_0_), channel_id=1, source_target_pairs={{0,4},{1,3},{2,6},{3,1},{4,0},{5,7},{6,2},{7,5},{8,12},{9,11},{10,... | collective-permute-start | bytes 1204232 | tf_op jit(solution)/shard_map/ppermute | solution.py:225
  16.4 0.0 collective-permute-start.14
  16.4 1.0 %collective-permute-start.4 = (bf16[784,128]{1,0:T(8,128)(2,1)S(1)}, bf16[784,128]{1,0:T(8,128)(2,1)S(1)}, u32[]{:S(2)}, u32[]{:S(2)}) collective-permute-start(bf16[784,128]{1,0:T(8,128)(2,1)S(1)} %shard_map.96), channel_id=1, source_target_pairs={{0,4},{1,3},{2,6},{3,1},{4,0},{5,7},{6,2},{7,5},{8,12},{9,11},{10,... | collective-permute-start | bytes 602120 | tf_op jit(solution)/shard_map/ppermute | solution.py:225
  17.4 5.0 %collective-permute-done.9.refs_0_ = bf16[1568,128]{1,0:T(8,128)(2,1)S(1)} collective-permute-done((bf16[1568,128]{1,0:T(8,128)(2,1)S(1)}, bf16[1568,128]{1,0:T(8,128)(2,1)S(1)}, u32[]{:S(2)}, u32[]{:S(2)}) %collective-permute-start.9) | collective-permute-done | bytes 401440 | tf_op jit(solution)/shard_map/ppermute | solution.py:225
  22.3 0.6 %collective-permute-start.10 = (bf16[1568,128]{1,0:T(8,128)(2,1)S(1)}, bf16[1568,128]{1,0:T(8,128)(2,1)S(1)}, u32[]{:S(2)}, u32[]{:S(2)}) collective-permute-start(bf16[1568,128]{1,0:T(8,128)(2,1)S(1)} %collective-permute-done.9.refs_0_), channel_id=1, source_target_pairs={{0,4},{1,3},{2,6},{3,1},{4,0},{5,7},{6,2},{7,5},{8,12},{9,11},{10,... | collective-permute-start | bytes 1204232 | tf_op jit(solution)/shard_map/ppermute | solution.py:225
  23.0 0.0 collective-permute-done.1
  23.0 2.7 %collective-permute-start.2 = (bf16[1568,128]{1,0:T(8,128)(2,1)S(1)}, bf16[1568,128]{1,0:T(8,128)(2,1)S(1)}, u32[]{:S(2)}, u32[]{:S(2)}) collective-permute-start(bf16[1568,128]{1,0:T(8,128)(2,1)S(1)} %pad_maximum_fusion.refs_0_), channel_id=1, source_target_pairs={{0,8},{1,9},{2,10},{3,11},{4,12},{5,13},{6,14},{7,15},{8,0},{9,1},... | collective-permute-start | bytes 1204232 | tf_op jit(solution)/shard_map/ppermute | solution.py:225
  25.7 0.0 collective-permute-done.13.refs_1_
  25.7 0.0 collective-permute-start.15
  25.7 0.0 collective-permute-done.4
  25.7 0.7 %collective-permute-start.5 = (bf16[784,128]{1,0:T(8,128)(2,1)S(1)}, bf16[784,128]{1,0:T(8,128)(2,1)S(1)}, u32[]{:S(2)}, u32[]{:S(2)}) collective-permute-start(bf16[784,128]{1,0:T(8,128)(2,1)S(1)} %collective-permute-done.1), channel_id=1, source_target_pairs={{0,4},{1,3},{2,6},{3,1},{4,0},{5,7},{6,2},{7,5},{8,12},{9,11},{10,... | collective-permute-start | bytes 602120 | tf_op jit(solution)/shard_map/ppermute | solution.py:225
  26.4 5.9 %collective-permute-done.5 = bf16[784,128]{1,0:T(8,128)(2,1)S(1)} collective-permute-done((bf16[784,128]{1,0:T(8,128)(2,1)S(1)}, bf16[784,128]{1,0:T(8,128)(2,1)S(1)}, u32[]{:S(2)}, u32[]{:S(2)}) %collective-permute-start.5) | collective-permute-done | bytes 200736 | tf_op jit(solution)/shard_map/ppermute | solution.py:225
  32.3 0.0 collective-permute-start.11
  32.4 0.0 collective-permute-done.10.refs_1_
  32.4 0.6 %collective-permute-start.12 = (bf16[1568,128]{1,0:T(8,128)(2,1)S(1)}, bf16[1568,128]{1,0:T(8,128)(2,1)S(1)}, u32[]{:S(2)}, u32[]{:S(2)}) collective-permute-start(bf16[1568,128]{1,0:T(8,128)(2,1)S(1)} %collective-permute-done.10.refs_1_), channel_id=1, source_target_pairs={{0,1},{1,0},{2,3},{3,2},{4,5},{5,4},{6,7},{7,6},{8,9},{9,8},{10,11... | collective-permute-start | bytes 1204232 | tf_op jit(solution)/shard_map/ppermute | solution.py:225
  33.0 0.0 collective-permute-done.14.refs_2_
  33.0 0.1 collective-permute-start.6
  33.1 1.8 %collective-permute-done.2.refs_0_ = bf16[1568,128]{1,0:T(8,128)(2,1)S(1)} collective-permute-done((bf16[1568,128]{1,0:T(8,128)(2,1)S(1)}, bf16[1568,128]{1,0:T(8,128)(2,1)S(1)}, u32[]{:S(2)}, u32[]{:S(2)}) %collective-permute-start.2) | collective-permute-done | bytes 401440 | tf_op jit(solution)/shard_map/ppermute | solution.py:225
  34.9 0.0 collective-permute-start.7
  34.9 0.0 collective-permute-done.15.refs_3_
  34.9 0.1 collective-permute-start.3
  34.9 2.5 %shard_map.97 = (f32[16,1024,128]{2,1,0:T(8,128)S(1)}, s32[8,128]{1,0:T(8,128)S(1)}, bf16[4,256,128]{2,1,0:T(8,128)(2,1)S(1)}) custom-call(bf16[1568,128]{1,0:T(8,128)(2,1)S(1)} %pad_maximum_fusion.1.refs_0_, bf16[1568,128]{1,0:T(8,128)(2,1)S(1)} %collective-permute-done.13.refs_1_, ...), custom_call_target="tpu_custom_call", output_to_operand_aliasing={{0}: (4, {})} | custom-call | tf_op jit(solution)/shard_map/pallas_call | solution.py:446
  37.5 0.0 collective-permute-done.11.refs_2_
  37.5 0.8 %collective-permute-start.16 = (bf16[1568,128]{1,0:T(8,128)(2,1)S(1)}, bf16[1568,128]{1,0:T(8,128)(2,1)S(1)}, u32[]{:S(2)}, u32[]{:S(2)}) collective-permute-start(bf16[1568,128]{1,0:T(8,128)(2,1)S(1)} %collective-permute-done.2.refs_0_), channel_id=1, source_target_pairs={{0,1},{1,0},{2,3},{3,2},{4,5},{5,4},{6,7},{7,6},{8,9},{9,8},{10,11... | collective-permute-start | bytes 1204232 | tf_op jit(solution)/shard_map/ppermute | solution.py:225
  38.2 0.0 collective-permute-done.12.refs_3_
  38.2 1.9 %shard_map.98 = (f32[16,1024,128]{2,1,0:T(8,128)S(1)}, s32[8,128]{1,0:T(8,128)}) custom-call(bf16[1568,128]{1,0:T(8,128)(2,1)S(1)} %collective-permute-done.9.refs_0_, bf16[1568,128]{1,0:T(8,128)(2,1)S(1)} %collective-permute-done.10.refs_1_, bf16[1568,128]{1,0:T(8,128)(2,1)S(1)} %collective-permute-done.11.refs_2_, ...), custom_call_target="tpu_custom_call", output_to_operand_aliasing={{0}: (4, {})} | custom-call | tf_op jit(solution)/shard_map/pallas_call | solution.py:446
  40.1 0.0 collective-permute-done.6.refs_2_
  40.1 0.0 collective-permute-done.7.refs_3_
  40.1 0.0 copy-start
  40.2 1.7 %shard_map.99 = (f32[16,1024,128]{2,1,0:T(8,128)S(1)}, s32[8,128]{1,0:T(8,128)S(1)}) custom-call(bf16[1568,128]{1,0:T(8,128)(2,1)S(1)} %pad_maximum_fusion.refs_0_, bf16[1568,128]{1,0:T(8,128)(2,1)S(1)} %constant_dynamic-update-slice_fusion.refs_1_, bf16[1568,128]{1,0:T(8,128)(2,1)S(1)} %collective-permute-done.6.refs_2_, ...), custom_call_target="tpu_custom_call", output_to_operand_aliasing={{0}: (4, {})} | custom-call | tf_op jit(solution)/shard_map/pallas_call | solution.py:446
  41.8 0.9 %collective-permute-done.3.value_ref = bf16[1568,128]{1,0:T(8,128)(2,1)S(1)} collective-permute-done((bf16[1568,128]{1,0:T(8,128)(2,1)S(1)}, bf16[1568,128]{1,0:T(8,128)(2,1)S(1)}, u32[]{:S(2)}, u32[]{:S(2)}) %collective-permute-start.3) | collective-permute-done | bytes 401440 | tf_op jit(solution)/shard_map/ppermute | solution.py:225
  42.7 0.0 collective-permute-start.17
  42.7 0.0 collective-permute-done.16.refs_2_
  42.7 1.7 %collective-permute-done.17.refs_3_ = bf16[1568,128]{1,0:T(8,128)(2,1)S(1)} collective-permute-done((bf16[1568,128]{1,0:T(8,128)(2,1)S(1)}, bf16[1568,128]{1,0:T(8,128)(2,1)S(1)}, u32[]{:S(2)}, u32[]{:S(2)}) %collective-permute-start.17) | collective-permute-done | bytes 401440 | tf_op jit(solution)/shard_map/ppermute | solution.py:225
  44.5 2.9 %shard_map.101 = (f32[16,1024,128]{2,1,0:T(8,128)S(1)}, s32[8,128]{1,0:T(8,128)}) custom-call(bf16[1568,128]{1,0:T(8,128)(2,1)S(1)} %collective-permute-done.2.refs_0_, bf16[1568,128]{1,0:T(8,128)(2,1)S(1)} %shard_map.100.refs_1_, bf16[1568,128]{1,0:T(8,128)(2,1)S(1)} %collective-permute-done.16.refs_2_, ...), custom_call_target="tpu_custom_call", output_to_operand_aliasing={{0}: (4, {})} | custom-call | tf_op jit(solution)/shard_map/pallas_call | solution.py:446
  47.4 0.0 copy-done
  47.4 7.1 %shard_map.102 = (bf16[64,512]{1,0:T(8,128)(2,1)}, f32[512,512]{1,0:T(8,128)}, f32[512,512]{1,0:T(8,128)}) custom-call(f32[16,1024,128]{2,1,0:T(8,128)S(1)} %get-tuple-element.19.sums, bf16[4,256,128]{2,1,0:T(8,128)(2,1)S(1)} %get-tuple-element.20.vals, s32[8,128]{1,0:T(8,128)S(1)} %get-tuple-element.21.info_v, bf16[512,512]{1,0:T(8,128)(2,1)S(1)} %get-tuple-element.22.w1t, ...), custom_call_target="tpu_custom_call" | custom-call | tf_op jit(solution)/shard_map/pallas_call | solution.py:467
  (6 shorter events, 0.1 us)
Async XLA Ops:
  2.3 6.7 %collective-permute-start.8 = (bf16[784,128]{1,0:T(8,128)(2,1)S(1)}, bf16[784,128]{1,0:T(8,128)(2,1)S(1)}, u32[]{:S(2)}, u32[]{:S(2)}) collective-permute-start(bf16[784,128]{1,0:T(8,128)(2,1)S(1)} %shard_map.94.dep_ref), channel_id=1, source_target_pairs={{0,2},{1,5},{2,0},{3,7},{4,6},{5,1},{6,4},{7,3},{8,10},{9,13},{10,... | collective-permute-start | bytes 602120 | tf_op jit(solution)/shard_map/ppermute | solution.py:225
  5.3 9.0 %collective-permute-start = (bf16[784,128]{1,0:T(8,128)(2,1)S(1)}, bf16[784,128]{1,0:T(8,128)(2,1)S(1)}, u32[]{:S(2)}, u32[]{:S(2)}) collective-permute-start(bf16[784,128]{1,0:T(8,128)(2,1)S(1)} %shard_map.94.dep_ref), channel_id=1, source_target_pairs={{0,24},{1,25},{2,26},{3,27},{4,28},{5,29},{6,30},{7,31},{8,16},{9,... | collective-permute-start | bytes 602120 | tf_op jit(solution)/shard_map/ppermute | solution.py:225
  9.0 13.3 %collective-permute-start.9 = (bf16[1568,128]{1,0:T(8,128)(2,1)S(1)}, bf16[1568,128]{1,0:T(8,128)(2,1)S(1)}, u32[]{:S(2)}, u32[]{:S(2)}) collective-permute-start(bf16[1568,128]{1,0:T(8,128)(2,1)S(1)} %pad_maximum_fusion.1.refs_0_), channel_id=1, source_target_pairs={{0,8},{1,9},{2,10},{3,11},{4,12},{5,13},{6,14},{7,15},{8,0},{9,1},... | collective-permute-start | bytes 1204232 | tf_op jit(solution)/shard_map/ppermute | solution.py:225
  11.2 1.0 %copy-start.1 = (bf16[512,512]{1,0:T(8,128)(2,1)S(1)}, bf16[512,512]{1,0:T(8,128)(2,1)}, u32[]{:S(2)}) copy-start(bf16[512,512]{1,0:T(8,128)(2,1)} %w1_ref.1) | copy-start | bytes 1572868
  14.3 8.7 %collective-permute-start.1 = (bf16[784,128]{1,0:T(8,128)(2,1)S(1)}, bf16[784,128]{1,0:T(8,128)(2,1)S(1)}, u32[]{:S(2)}, u32[]{:S(2)}) collective-permute-start(bf16[784,128]{1,0:T(8,128)(2,1)S(1)} %shard_map.96), channel_id=1, source_target_pairs={{0,2},{1,5},{2,0},{3,7},{4,6},{5,1},{6,4},{7,3},{8,10},{9,13},{10,... | collective-permute-start | bytes 602120 | tf_op jit(solution)/shard_map/ppermute | solution.py:225
  15.3 10.3 %collective-permute-start.13 = (bf16[1568,128]{1,0:T(8,128)(2,1)S(1)}, bf16[1568,128]{1,0:T(8,128)(2,1)S(1)}, u32[]{:S(2)}, u32[]{:S(2)}) collective-permute-start(bf16[1568,128]{1,0:T(8,128)(2,1)S(1)} %pad_maximum_fusion.1.refs_0_), channel_id=1, source_target_pairs={{0,4},{1,3},{2,6},{3,1},{4,0},{5,7},{6,2},{7,5},{8,12},{9,11},{10,... | collective-permute-start | bytes 1204232 | tf_op jit(solution)/shard_map/ppermute | solution.py:225
  16.4 16.6 %collective-permute-start.14 = (bf16[1568,128]{1,0:T(8,128)(2,1)S(1)}, bf16[1568,128]{1,0:T(8,128)(2,1)S(1)}, u32[]{:S(2)}, u32[]{:S(2)}) collective-permute-start(bf16[1568,128]{1,0:T(8,128)(2,1)S(1)} %pad_maximum_fusion.1.refs_0_), channel_id=1, source_target_pairs={{0,1},{1,0},{2,3},{3,2},{4,5},{5,4},{6,7},{7,6},{8,9},{9,8},{10,11... | collective-permute-start | bytes 1204232 | tf_op jit(solution)/shard_map/ppermute | solution.py:225
  16.4 9.3 %collective-permute-start.4 = (bf16[784,128]{1,0:T(8,128)(2,1)S(1)}, bf16[784,128]{1,0:T(8,128)(2,1)S(1)}, u32[]{:S(2)}, u32[]{:S(2)}) collective-permute-start(bf16[784,128]{1,0:T(8,128)(2,1)S(1)} %shard_map.96), channel_id=1, source_target_pairs={{0,4},{1,3},{2,6},{3,1},{4,0},{5,7},{6,2},{7,5},{8,12},{9,11},{10,... | collective-permute-start | bytes 602120 | tf_op jit(solution)/shard_map/ppermute | solution.py:225
  22.3 10.1 %collective-permute-start.10 = (bf16[1568,128]{1,0:T(8,128)(2,1)S(1)}, bf16[1568,128]{1,0:T(8,128)(2,1)S(1)}, u32[]{:S(2)}, u32[]{:S(2)}) collective-permute-start(bf16[1568,128]{1,0:T(8,128)(2,1)S(1)} %collective-permute-done.9.refs_0_), channel_id=1, source_target_pairs={{0,4},{1,3},{2,6},{3,1},{4,0},{5,7},{6,2},{7,5},{8,12},{9,11},{10,... | collective-permute-start | bytes 1204232 | tf_op jit(solution)/shard_map/ppermute | solution.py:225
  23.0 11.8 %collective-permute-start.2 = (bf16[1568,128]{1,0:T(8,128)(2,1)S(1)}, bf16[1568,128]{1,0:T(8,128)(2,1)S(1)}, u32[]{:S(2)}, u32[]{:S(2)}) collective-permute-start(bf16[1568,128]{1,0:T(8,128)(2,1)S(1)} %pad_maximum_fusion.refs_0_), channel_id=1, source_target_pairs={{0,8},{1,9},{2,10},{3,11},{4,12},{5,13},{6,14},{7,15},{8,0},{9,1},... | collective-permute-start | bytes 1204232 | tf_op jit(solution)/shard_map/ppermute | solution.py:225
  25.7 9.2 %collective-permute-start.15 = (bf16[1568,128]{1,0:T(8,128)(2,1)S(1)}, bf16[1568,128]{1,0:T(8,128)(2,1)S(1)}, u32[]{:S(2)}, u32[]{:S(2)}) collective-permute-start(bf16[1568,128]{1,0:T(8,128)(2,1)S(1)} %collective-permute-done.13.refs_1_), channel_id=1, source_target_pairs={{0,1},{1,0},{2,3},{3,2},{4,5},{5,4},{6,7},{7,6},{8,9},{9,8},{10,11... | collective-permute-start | bytes 1204232 | tf_op jit(solution)/shard_map/ppermute | solution.py:225
  25.7 6.7 %collective-permute-start.5 = (bf16[784,128]{1,0:T(8,128)(2,1)S(1)}, bf16[784,128]{1,0:T(8,128)(2,1)S(1)}, u32[]{:S(2)}, u32[]{:S(2)}) collective-permute-start(bf16[784,128]{1,0:T(8,128)(2,1)S(1)} %collective-permute-done.1), channel_id=1, source_target_pairs={{0,4},{1,3},{2,6},{3,1},{4,0},{5,7},{6,2},{7,5},{8,12},{9,11},{10,... | collective-permute-start | bytes 602120 | tf_op jit(solution)/shard_map/ppermute | solution.py:225
  32.3 5.1 %collective-permute-start.11 = (bf16[1568,128]{1,0:T(8,128)(2,1)S(1)}, bf16[1568,128]{1,0:T(8,128)(2,1)S(1)}, u32[]{:S(2)}, u32[]{:S(2)}) collective-permute-start(bf16[1568,128]{1,0:T(8,128)(2,1)S(1)} %collective-permute-done.9.refs_0_), channel_id=1, source_target_pairs={{0,1},{1,0},{2,3},{3,2},{4,5},{5,4},{6,7},{7,6},{8,9},{9,8},{10,11... | collective-permute-start | bytes 1204232 | tf_op jit(solution)/shard_map/ppermute | solution.py:225
  32.4 5.9 %collective-permute-start.12 = (bf16[1568,128]{1,0:T(8,128)(2,1)S(1)}, bf16[1568,128]{1,0:T(8,128)(2,1)S(1)}, u32[]{:S(2)}, u32[]{:S(2)}) collective-permute-start(bf16[1568,128]{1,0:T(8,128)(2,1)S(1)} %collective-permute-done.10.refs_1_), channel_id=1, source_target_pairs={{0,1},{1,0},{2,3},{3,2},{4,5},{5,4},{6,7},{7,6},{8,9},{9,8},{10,11... | collective-permute-start | bytes 1204232 | tf_op jit(solution)/shard_map/ppermute | solution.py:225
  33.0 7.2 %collective-permute-start.6 = (bf16[1568,128]{1,0:T(8,128)(2,1)S(1)}, bf16[1568,128]{1,0:T(8,128)(2,1)S(1)}, u32[]{:S(2)}, u32[]{:S(2)}) collective-permute-start(bf16[1568,128]{1,0:T(8,128)(2,1)S(1)} %pad_maximum_fusion.refs_0_), channel_id=1, source_target_pairs={{0,1},{1,0},{2,3},{3,2},{4,5},{5,4},{6,7},{7,6},{8,9},{9,8},{10,11... | collective-permute-start | bytes 1204232 | tf_op jit(solution)/shard_map/ppermute | solution.py:225
  34.9 5.3 %collective-permute-start.7 = (bf16[1568,128]{1,0:T(8,128)(2,1)S(1)}, bf16[1568,128]{1,0:T(8,128)(2,1)S(1)}, u32[]{:S(2)}, u32[]{:S(2)}) collective-permute-start(bf16[1568,128]{1,0:T(8,128)(2,1)S(1)} %constant_dynamic-update-slice_fusion.refs_1_), channel_id=1, source_target_pairs={{0,1},{1,0},{2,3},{3,2},{4,5},{5,4},{6,7},{7,6},{8,9},{9,8},{10,11... | collective-permute-start | bytes 1204232 | tf_op jit(solution)/shard_map/ppermute | solution.py:225
  34.9 7.9 %collective-permute-start.3 = (bf16[1568,128]{1,0:T(8,128)(2,1)S(1)}, bf16[1568,128]{1,0:T(8,128)(2,1)S(1)}, u32[]{:S(2)}, u32[]{:S(2)}) collective-permute-start(bf16[1568,128]{1,0:T(8,128)(2,1)S(1)} %collective-permute-done.2.refs_0_), channel_id=1, source_target_pairs={{0,4},{1,3},{2,6},{3,1},{4,0},{5,7},{6,2},{7,5},{8,12},{9,11},{10,... | collective-permute-start | bytes 1204232 | tf_op jit(solution)/shard_map/ppermute | solution.py:225
  37.5 5.2 %collective-permute-start.16 = (bf16[1568,128]{1,0:T(8,128)(2,1)S(1)}, bf16[1568,128]{1,0:T(8,128)(2,1)S(1)}, u32[]{:S(2)}, u32[]{:S(2)}) collective-permute-start(bf16[1568,128]{1,0:T(8,128)(2,1)S(1)} %collective-permute-done.2.refs_0_), channel_id=1, source_target_pairs={{0,1},{1,0},{2,3},{3,2},{4,5},{5,4},{6,7},{7,6},{8,9},{9,8},{10,11... | collective-permute-start | bytes 1204232 | tf_op jit(solution)/shard_map/ppermute | solution.py:225
  40.1 7.2 %copy-start = (bf16[512,512]{1,0:T(8,128)(2,1)S(1)}, bf16[512,512]{1,0:T(8,128)(2,1)}, u32[]{:S(2)}) copy-start(bf16[512,512]{1,0:T(8,128)(2,1)} %w2_ref.1) | copy-start | bytes 1572868
  42.7 1.7 %collective-permute-start.17 = (bf16[1568,128]{1,0:T(8,128)(2,1)S(1)}, bf16[1568,128]{1,0:T(8,128)(2,1)S(1)}, u32[]{:S(2)}, u32[]{:S(2)}) collective-permute-start(bf16[1568,128]{1,0:T(8,128)(2,1)S(1)} %shard_map.100.refs_1_), channel_id=1, source_target_pairs={{0,1},{1,0},{2,3},{3,2},{4,5},{5,4},{6,7},{7,6},{8,9},{9,8},{10,11... | collective-permute-start | bytes 1204232 | tf_op jit(solution)/shard_map/ppermute | solution.py:225
